TPU v7x, 32 devices: a whole 2x2x4 slice. The times are simulated.
32 devices in a mesh: dp: 4 (over y, x), fsdp: 8 (over z, core).
Axes of the slice: x: 2, y: 2, z: 4, core: 2. Of those that a mesh axis runs over, the one named last changes fastest.
Arguments:
- inputs: bfloat16 [32768, 1024], P(('dp', 'fsdp')), may hold values from -6 to 6
- skip_in: bfloat16 [32768, 1024], P(('dp', 'fsdp')), may hold values from -6 to 6
- time_emb: bfloat16 [32, 4, 1024], P(('dp', 'fsdp')), may hold values from -3 to 3
- seg_ids: int32 [32, 1024], P(('dp', 'fsdp')), may hold values from 0 to 3, as said below
- positions: int32 [32, 1024], P(('dp', 'fsdp')), may hold values from 0 to 639, as said below
- pad_mask: int32 [32, 1024], P(('dp', 'fsdp')), may hold values from 0 to 1, as said below
- w_skip: bfloat16 [2048, 1024], P('dp', 'fsdp'), may hold values from -0.125 to 0.125
- w_ada1: bfloat16 [1024, 1024], P('dp', 'fsdp'), may hold values from -0.1875 to 0.1875
- w_qkv: bfloat16 [1024, 3072], P('dp', 'fsdp'), may hold values from -0.1875 to 0.1875
- w_out: bfloat16 [1024, 1024], P('dp', 'fsdp'), may hold values from -0.75 to 0.75
- w_ada2: bfloat16 [1024, 1024], P('dp', 'fsdp'), may hold values from -0.1875 to 0.1875
- w_up: bfloat16 [1024, 4096], P('dp', 'fsdp'), may hold values from -0.1875 to 0.1875
- w_down: bfloat16 [4096, 1024], P('dp', 'fsdp'), may hold values from -0.09375 to 0.09375
- cotangent: bfloat16 [32768, 1024], P(('dp', 'fsdp')), may hold values from -6 to 6
Outputs:
- output: bfloat16 [32768, 1024], P(('dp', 'fsdp'))
- d_input: float32 [32768, 1024], P(('dp', 'fsdp'))
- d_skip: float32 [32768, 1024], P(('dp', 'fsdp'))
- d_time: float32 [32, 4, 1024], P(('dp', 'fsdp'))
- grad_w_skip: float32 [2048, 1024], P('dp', 'fsdp')
- grad_w_ada1: float32 [1024, 1024], P('dp', 'fsdp')
- grad_w_qkv: float32 [1024, 3072], P('dp', 'fsdp')
- grad_w_out: float32 [1024, 1024], P('dp', 'fsdp')
- grad_w_ada2: float32 [1024, 1024], P('dp', 'fsdp')
- grad_w_up: float32 [1024, 4096], P('dp', 'fsdp')
- grad_w_down: float32 [4096, 1024], P('dp', 'fsdp')
Inputs may be any that keep to these rules, and one draw needn't show every extreme that they name: `seg_ids`: each row of 1024 frames is cut into 4 utterances in order, numbered 0 to 3, none empty; one of them, at a place drawn from the seed, has 640 frames and is the longest. `positions`: A frame's index within its utterance, counted from 0. `pad_mask`: zeros only on the last 0 to 128 frames of a row.
All inputs are finite; a program needn't handle non-finite values.
Results may differ from a plain program's by a relative error of at most 0.022.
Values may be sent and summed in bfloat16 or wider, within the bound.
A program may use at most 256 MiB of HBM per device.

v0:
```python
import jax
import jax.numpy as jnp
from jax import lax
from jax.sharding import PartitionSpec as P

HD = 64


eps = 1e-06
masked = -1e30


def angles(positions):
    halfway = HD // 2
    frequency = 10000.0 ** (-2.0 * jnp.arange(halfway, dtype=jnp.float32) / HD)
    phases = positions.astype(jnp.float32)[..., None] * frequency
    phases = jnp.concatenate([phases, phases], axis=-1).reshape(-1, 1, HD)
    return (jnp.cos(phases), jnp.sin(phases))


def rotate(array, cosine, sine):
    halfway = array.shape[-1] // 2
    turned = jnp.concatenate([-array[..., halfway:], array[..., :halfway]], axis=-1)
    return array * cosine + turned * sine


def rotate_back(grad, cosine, sine):
    halfway = grad.shape[-1] // 2
    shifted = grad * sine
    return grad * cosine + jnp.concatenate(
        [shifted[..., halfway:], -shifted[..., :halfway]], axis=-1
    )


def normalize(stream, gain):
    inverse = lax.rsqrt(jnp.mean(stream * stream, axis=-1, keepdims=True) + eps)
    return (stream * inverse * (1.0 + gain), inverse)


def normalize_back(grad, stream, inverse, gain):
    unit_rows = stream * inverse
    scaled = grad * (1.0 + gain)
    d_stream = inverse * (scaled - unit_rows * jnp.mean(scaled * unit_rows, axis=-1, keepdims=True))
    return (d_stream, grad * unit_rows)


def allowed_keys(segment, padding):
    places = jnp.arange(segment.shape[0])
    return (segment[:, None] == segment[None, :]) & (
        (padding[None, :] > 0) | (places[:, None] == places[None, :])
    )


def head_cut(block, head_index):
    return lax.dynamic_slice_in_dim(block, head_index * HD, HD, 1)


def masked_scores(query_head, key_head, allowed):
    scores = jnp.einsum(
        "qd,kd->qk", query_head, key_head, preferred_element_type=jnp.float32
    ) * HD ** (-0.5)
    return jnp.where(allowed, scores, masked)


def merge_heads(per_head):
    return jnp.transpose(per_head, (1, 0, 2)).reshape(per_head.shape[1], -1)


def attend_row(bundle):
    query_rows, key_rows, value_rows, segment, padding = bundle
    allowed = allowed_keys(segment, padding)

    def one_head(head_index):
        scores = masked_scores(
            head_cut(query_rows, head_index), head_cut(key_rows, head_index), allowed
        )
        largest = jnp.max(scores, axis=-1, keepdims=True)
        exponent = jnp.exp(scores - largest)
        denominator = jnp.sum(exponent, axis=-1, keepdims=True)
        soft_low = (exponent / denominator).astype(jnp.bfloat16)
        context = jnp.dot(
            soft_low, head_cut(value_rows, head_index), preferred_element_type=jnp.float32
        )
        return (context, (largest + jnp.log(denominator))[:, 0])

    heads_count = query_rows.shape[1] // HD
    context, logsum = lax.map(one_head, jnp.arange(heads_count))
    return (merge_heads(context), logsum)


def attend_back(bundle):
    query_rows, key_rows, value_rows, grad_rows, logsum, segment, padding = bundle
    allowed = allowed_keys(segment, padding)
    factor = HD ** (-0.5)

    def one_head(head_index):
        query_head = head_cut(query_rows, head_index)
        key_head = head_cut(key_rows, head_index)
        value_head = head_cut(value_rows, head_index)
        grad_head = head_cut(grad_rows, head_index)
        scores = masked_scores(query_head, key_head, allowed)
        softened = jnp.exp(scores - logsum[head_index][:, None])
        d_soft = jnp.einsum("qd,kd->qk", grad_head, value_head, preferred_element_type=jnp.float32)
        d_scores = (
            softened * (d_soft - jnp.sum(softened * d_soft, axis=-1, keepdims=True))
        ).astype(jnp.bfloat16)
        d_query = jnp.dot(d_scores, key_head, preferred_element_type=jnp.float32) * factor
        d_key = (
            jnp.einsum("qk,qd->kd", d_scores, query_head, preferred_element_type=jnp.float32)
            * factor
        )
        d_value = jnp.einsum(
            "qk,qd->kd",
            softened.astype(jnp.bfloat16),
            grad_head,
            preferred_element_type=jnp.float32,
        )
        return (d_query, d_key, d_value)

    heads_count = query_rows.shape[1] // HD
    d_query, d_key, d_value = lax.map(one_head, jnp.arange(heads_count))
    return (merge_heads(d_query), merge_heads(d_key), merge_heads(d_value))


def shards(
    inputs,
    skip_in,
    time_emb,
    seg_ids,
    positions,
    pad_mask,
    w_skip,
    w_ada1,
    w_qkv,
    w_out,
    w_ada2,
    w_up,
    w_down,
    cotangent,
):
    part_skip, part_ada1, part_qkv, part_out, part_ada2, part_up, part_down = (
        lax.all_gather(w_skip, "fsdp", axis=1, tiled=True),
        lax.all_gather(w_ada1, "fsdp", axis=1, tiled=True),
        lax.all_gather(w_qkv, "fsdp", axis=1, tiled=True),
        lax.all_gather(w_out, "fsdp", axis=1, tiled=True),
        lax.all_gather(w_ada2, "fsdp", axis=1, tiled=True),
        lax.all_gather(w_up, "fsdp", axis=1, tiled=True),
        lax.all_gather(w_down, "fsdp", axis=1, tiled=True),
    )
    full_skip, full_ada1, full_qkv, full_out, full_ada2, full_up, full_down = (
        lax.all_gather(part_skip, "dp", axis=0, tiled=True),
        lax.all_gather(part_ada1, "dp", axis=0, tiled=True),
        lax.all_gather(part_qkv, "dp", axis=0, tiled=True),
        lax.all_gather(part_out, "dp", axis=0, tiled=True),
        lax.all_gather(part_ada2, "dp", axis=0, tiled=True),
        lax.all_gather(part_up, "dp", axis=0, tiled=True),
        lax.all_gather(part_down, "dp", axis=0, tiled=True),
    )
    rows_here, length = seg_ids.shape
    features = inputs.shape[1]
    slots_count = time_emb.shape[1]
    joined = jnp.concatenate([inputs, skip_in], axis=1)
    stream0 = jnp.dot(joined, full_skip, preferred_element_type=jnp.float32)
    selector = (seg_ids[:, None, :] == jnp.arange(slots_count)[None, :, None]).astype(jnp.float32)
    flat_time = time_emb.reshape(-1, features)
    gamma1 = jnp.dot(flat_time, full_ada1, preferred_element_type=jnp.float32).reshape(
        rows_here, slots_count, features
    )
    gamma2 = jnp.dot(flat_time, full_ada2, preferred_element_type=jnp.float32).reshape(
        rows_here, slots_count, features
    )
    tok_gamma1 = jnp.einsum(
        "rsl,rsd->rld", selector, gamma1, precision=lax.Precision.HIGHEST
    ).reshape(-1, features)
    tok_gamma2 = jnp.einsum(
        "rsl,rsd->rld", selector, gamma2, precision=lax.Precision.HIGHEST
    ).reshape(-1, features)
    normed1, inverse1 = normalize(stream0, tok_gamma1)
    normed1 = normed1.astype(jnp.bfloat16)
    projected = jnp.dot(normed1, full_qkv, preferred_element_type=jnp.float32)
    cosine, sine = angles(positions)
    head_shape = (-1, features // HD, HD)
    queries = (
        rotate(projected[:, :features].reshape(head_shape), cosine, sine)
        .astype(jnp.bfloat16)
        .reshape(-1, features)
    )
    key_rows = (
        rotate(projected[:, features : 2 * features].reshape(head_shape), cosine, sine)
        .astype(jnp.bfloat16)
        .reshape(-1, features)
    )
    value_rows = projected[:, 2 * features :].astype(jnp.bfloat16)

    def by_row(array):
        return array.reshape((rows_here, length) + array.shape[1:])

    context, logsum = lax.map(
        attend_row, (by_row(queries), by_row(key_rows), by_row(value_rows), seg_ids, pad_mask)
    )
    context_low = context.reshape(-1, features).astype(jnp.bfloat16)
    stream1 = stream0 + jnp.dot(context_low, full_out, preferred_element_type=jnp.float32)
    normed2, inverse2 = normalize(stream1, tok_gamma2)
    normed2 = normed2.astype(jnp.bfloat16)
    hidden_pre = jnp.dot(normed2, full_up, preferred_element_type=jnp.float32)
    activated = jax.nn.gelu(hidden_pre).astype(jnp.bfloat16)
    output = (stream1 + jnp.dot(activated, full_down, preferred_element_type=jnp.float32)).astype(
        jnp.bfloat16
    )
    again_skip, again_ada1, again_qkv, again_out, again_ada2, again_up, again_down = (
        lax.all_gather(w_skip, "fsdp", axis=1, tiled=True),
        lax.all_gather(w_ada1, "fsdp", axis=1, tiled=True),
        lax.all_gather(w_qkv, "fsdp", axis=1, tiled=True),
        lax.all_gather(w_out, "fsdp", axis=1, tiled=True),
        lax.all_gather(w_ada2, "fsdp", axis=1, tiled=True),
        lax.all_gather(w_up, "fsdp", axis=1, tiled=True),
        lax.all_gather(w_down, "fsdp", axis=1, tiled=True),
    )
    back_skip, back_ada1, back_qkv, back_out, back_ada2, back_up, back_down = (
        lax.all_gather(again_skip, "dp", axis=0, tiled=True),
        lax.all_gather(again_ada1, "dp", axis=0, tiled=True),
        lax.all_gather(again_qkv, "dp", axis=0, tiled=True),
        lax.all_gather(again_out, "dp", axis=0, tiled=True),
        lax.all_gather(again_ada2, "dp", axis=0, tiled=True),
        lax.all_gather(again_up, "dp", axis=0, tiled=True),
        lax.all_gather(again_down, "dp", axis=0, tiled=True),
    )
    grad_down = jnp.einsum("nf,nd->fd", activated, cotangent, preferred_element_type=jnp.float32)
    d_act = jnp.einsum("nd,fd->nf", cotangent, back_down, preferred_element_type=jnp.float32)
    gelu_pull = jax.vjp(jax.nn.gelu, hidden_pre)[1]
    d_pre = gelu_pull(d_act)[0].astype(jnp.bfloat16)
    grad_up = jnp.einsum("nd,nf->df", normed2, d_pre, preferred_element_type=jnp.float32)
    d_normed2 = jnp.einsum("nf,df->nd", d_pre, back_up, preferred_element_type=jnp.float32)
    stream_term2, d_tok2 = normalize_back(d_normed2, stream1, inverse2, tok_gamma2)
    d_stream1 = cotangent.astype(jnp.float32) + stream_term2
    d_att = d_stream1.astype(jnp.bfloat16)
    grad_out = jnp.einsum("nd,ne->de", context_low, d_att, preferred_element_type=jnp.float32)
    d_context = jnp.einsum("ne,de->nd", d_att, back_out, preferred_element_type=jnp.float32).astype(
        jnp.bfloat16
    )
    d_query, d_key, d_value = lax.map(
        attend_back,
        (
            by_row(queries),
            by_row(key_rows),
            by_row(value_rows),
            by_row(d_context),
            logsum,
            seg_ids,
            pad_mask,
        ),
    )
    d_query = rotate_back(d_query.reshape(head_shape), cosine, sine).reshape(-1, features)
    d_key = rotate_back(d_key.reshape(head_shape), cosine, sine).reshape(-1, features)
    d_projected = jnp.concatenate([d_query, d_key, d_value.reshape(-1, features)], axis=1).astype(
        jnp.bfloat16
    )
    grad_qkv = jnp.einsum("nd,ne->de", normed1, d_projected, preferred_element_type=jnp.float32)
    d_normed1 = jnp.einsum("ne,de->nd", d_projected, back_qkv, preferred_element_type=jnp.float32)
    stream_term1, d_tok1 = normalize_back(d_normed1, stream0, inverse1, tok_gamma1)
    d_stream0 = d_stream1 + stream_term1
    d_gamma1 = (
        jnp.einsum(
            "rsl,rld->rsd",
            selector,
            d_tok1.reshape(rows_here, length, features),
            precision=lax.Precision.HIGHEST,
        )
        .astype(jnp.bfloat16)
        .reshape(-1, features)
    )
    d_gamma2 = (
        jnp.einsum(
            "rsl,rld->rsd",
            selector,
            d_tok2.reshape(rows_here, length, features),
            precision=lax.Precision.HIGHEST,
        )
        .astype(jnp.bfloat16)
        .reshape(-1, features)
    )
    grad_ada1 = jnp.einsum("nd,ne->de", flat_time, d_gamma1, preferred_element_type=jnp.float32)
    grad_ada2 = jnp.einsum("nd,ne->de", flat_time, d_gamma2, preferred_element_type=jnp.float32)
    d_time = jnp.einsum("ne,de->nd", d_gamma1, back_ada1, preferred_element_type=jnp.float32)
    d_time = (
        d_time + jnp.einsum("ne,de->nd", d_gamma2, back_ada2, preferred_element_type=jnp.float32)
    ).reshape(time_emb.shape)
    d_low = d_stream0.astype(jnp.bfloat16)
    grad_skip = jnp.einsum("nc,nd->cd", joined, d_low, preferred_element_type=jnp.float32)
    d_joined = jnp.einsum("nd,cd->nc", d_low, back_skip, preferred_element_type=jnp.float32)
    d_input = d_joined[:, :features]
    d_skip = d_joined[:, features:]
    sum_skip, sum_ada1, sum_qkv, sum_out, sum_ada2, sum_up, sum_down = (
        lax.psum_scatter(
            grad_skip.astype(jnp.bfloat16), "fsdp", scatter_dimension=1, tiled=True
        ).astype(jnp.float32),
        lax.psum_scatter(
            grad_ada1.astype(jnp.bfloat16), "fsdp", scatter_dimension=1, tiled=True
        ).astype(jnp.float32),
        lax.psum_scatter(
            grad_qkv.astype(jnp.bfloat16), "fsdp", scatter_dimension=1, tiled=True
        ).astype(jnp.float32),
        lax.psum_scatter(
            grad_out.astype(jnp.bfloat16), "fsdp", scatter_dimension=1, tiled=True
        ).astype(jnp.float32),
        lax.psum_scatter(
            grad_ada2.astype(jnp.bfloat16), "fsdp", scatter_dimension=1, tiled=True
        ).astype(jnp.float32),
        lax.psum_scatter(
            grad_up.astype(jnp.bfloat16), "fsdp", scatter_dimension=1, tiled=True
        ).astype(jnp.float32),
        lax.psum_scatter(
            grad_down.astype(jnp.bfloat16), "fsdp", scatter_dimension=1, tiled=True
        ).astype(jnp.float32),
    )
    final_skip, final_ada1, final_qkv, final_out, final_ada2, final_up, final_down = (
        lax.psum_scatter(
            sum_skip.astype(jnp.bfloat16), "dp", scatter_dimension=0, tiled=True
        ).astype(jnp.float32),
        lax.psum_scatter(
            sum_ada1.astype(jnp.bfloat16), "dp", scatter_dimension=0, tiled=True
        ).astype(jnp.float32),
        lax.psum_scatter(
            sum_qkv.astype(jnp.bfloat16), "dp", scatter_dimension=0, tiled=True
        ).astype(jnp.float32),
        lax.psum_scatter(
            sum_out.astype(jnp.bfloat16), "dp", scatter_dimension=0, tiled=True
        ).astype(jnp.float32),
        lax.psum_scatter(
            sum_ada2.astype(jnp.bfloat16), "dp", scatter_dimension=0, tiled=True
        ).astype(jnp.float32),
        lax.psum_scatter(sum_up.astype(jnp.bfloat16), "dp", scatter_dimension=0, tiled=True).astype(
            jnp.float32
        ),
        lax.psum_scatter(
            sum_down.astype(jnp.bfloat16), "dp", scatter_dimension=0, tiled=True
        ).astype(jnp.float32),
    )
    return (
        output,
        d_input,
        d_skip,
        d_time,
        final_skip,
        final_ada1,
        final_qkv,
        final_out,
        final_ada2,
        final_up,
        final_down,
    )


def solution(mesh):
    return jax.shard_map(
        shards,
        mesh=mesh,
        in_specs=(
            P(("dp", "fsdp"), None),
            P(("dp", "fsdp"), None),
            P(("dp", "fsdp"), None, None),
            P(("dp", "fsdp"), None),
            P(("dp", "fsdp"), None),
            P(("dp", "fsdp"), None),
            P("dp", "fsdp"),
            P("dp", "fsdp"),
            P("dp", "fsdp"),
            P("dp", "fsdp"),
            P("dp", "fsdp"),
            P("dp", "fsdp"),
            P("dp", "fsdp"),
            P(("dp", "fsdp"), None),
        ),
        out_specs=(
            P(("dp", "fsdp"), None),
            P(("dp", "fsdp"), None),
            P(("dp", "fsdp"), None),
            P(("dp", "fsdp"), None, None),
            P("dp", "fsdp"),
            P("dp", "fsdp"),
            P("dp", "fsdp"),
            P("dp", "fsdp"),
            P("dp", "fsdp"),
            P("dp", "fsdp"),
            P("dp", "fsdp"),
        ),
        check_vma=False,
    )
```

profile of v0, /device:TPU:0, one launch (start us, length us, event | category | flops | bytes accessed | tf_op | source)
XLA Modules:
  0.0 1547.4 jit_solution(736781062012322141)
XLA Ops:
  9.5 17.1 %all_gather.58 = bf16[256,1024]{1,0:T(8,128)(2,1)} all-gather(bf16[256,128]{1,0:T(8,128)(2,1)} %param.25), channel_id=1, replica_groups=mesh['dp'=4,'fsdp'=8] {'fsdp'}, dimensions={1}, use_global_device_ids=true | all-gather | bytes 589824 | tf_op jit(solution)/shard_map/all_gather | solution.py:143
  26.6 16.0 %all_gather.64 = bf16[256,1024]{1,0:T(8,128)(2,1)} all-gather(bf16[256,128]{1,0:T(8,128)(2,1)} %param.28), channel_id=1, replica_groups=mesh['dp'=4,'fsdp'=8] {'fsdp'}, dimensions={1}, use_global_device_ids=true | all-gather | bytes 589824 | tf_op jit(solution)/shard_map/all_gather | solution.py:146
  44.0 20.6 %all-gather.18.cloned.1.call-done = bf16[256,3072]{1,0:T(8,128)(2,1)} async-done(((bf16[256,384]{1,0:T(8,128)(2,1)}), bf16[256,3072]{1,0:T(8,128)(2,1)}) %all-gather.18.cloned.1.call-update) | async-done | bytes 1572880 | tf_op jit(solution)/shard_map/all_gather | solution.py:144
  64.7 15.1 all_gather.62
  79.9 16.7 %all-gather.30.cloned.1.call-done = bf16[1024,1024]{1,0:T(8,128)(2,1)} async-done(((bf16[1024,128]{1,0:T(8,128)(2,1)}), bf16[1024,1024]{1,0:T(8,128)(2,1)}) %all-gather.30.cloned.1.call-update) | async-done | bytes 2097168 | tf_op jit(solution)/shard_map/all_gather | solution.py:148
  119.1 14.0 all-gather.16.cloned.1.call-done
  135.1 35.1 %all-gather.24.cloned.1.call-done = bf16[1024,1024]{1,0:T(8,128)(2,1)} async-done(((bf16[256,1024]{1,0:T(8,128)(2,1)}), bf16[1024,1024]{1,0:T(8,128)(2,1)}) %all-gather.24.cloned.1.call-update) | async-done | bytes 2097168 | tf_op jit(solution)/shard_map/all_gather | solution.py:155
  172.1 28.6 %all-gather.26.cloned.1.call-done = bf16[256,4096]{1,0:T(8,128)(2,1)} async-done(((bf16[256,512]{1,0:T(8,128)(2,1)}), bf16[256,4096]{1,0:T(8,128)(2,1)}) %all-gather.26.cloned.1.call-update) | async-done | bytes 2097168 | tf_op jit(solution)/shard_map/all_gather | solution.py:147
  201.0 53.8 %all-gather.14.cloned.1.call-done = bf16[2048,1024]{1,0:T(8,128)(2,1)} async-done(((bf16[512,1024]{1,0:T(8,128)(2,1)}), bf16[2048,1024]{1,0:T(8,128)(2,1)}) %all-gather.14.cloned.1.call-update) | async-done | bytes 4194320 | tf_op jit(solution)/shard_map/all_gather | solution.py:151
  268.8 58.1 %all-gather.20.cloned.1.call-done = bf16[1024,3072]{1,0:T(8,128)(2,1)} async-done(((bf16[256,3072]{1,0:T(8,128)(2,1)}), bf16[1024,3072]{1,0:T(8,128)(2,1)}) %all-gather.20.cloned.1.call-update) | async-done | bytes 6291472 | tf_op jit(solution)/shard_map/all_gather | solution.py:153
  376.0 10.2 add_convert_fusion.2
  386.2 162.4 %while.50 = (s32[]{:T(128)}, bf16[16,1024,64]{1,2,0:T(8,128)(2,1)}, f32[16,1024]{1,0:T(8,128)S(1)}, s32[16]{0:T(128)S(1)}, bf16[1024,1024]{1,0:T(8,128)(2,1)}, /...) while((s32[]{:T(128)}, bf16[16,1024,64]{1,2,0:T(8,128)(2,1)}, ...), condition=%wide.region_4.5_spmd.clone.clone, body=%wide.region_1.4_spmd.clone.sunk.clone | while | flops 281017344 | bytes 30460612 | solution.py:87
  562.6 14.5 fusion.93
  577.2 29.0 %fusion.48 = (bf16[1024,4096]{1,0:T(8,128)(2,1)}, f32[1024,4096]{1,0:T(8,128)}) fusion(f32[1024,4096]{1,0:T(8,128)} %fusion.93, bf16[1024,1024]{0,1:T(8,128)(2,1)} %get-tuple-element.334, bf16[1024,4096]{1,0:T(8,128)(2,1)} %all-gather.28.cloned.1.call-done), kind=kOutput, calls=%fused_computation.56 | convolution fusion | flops 8673820672 | bytes 52428800 | tf_op jit(solution)/shard_map/dot_general | solution.py:205
  606.1 16.2 %multiply_reduce_fusion.2 = (f32[1024]{0:T(1024)S(1)}, f32[1024,1024]{0,1:T(8,128)S(1)}) fusion(f32[1024,1024]{0,1:T(8,128)} %copy-done.3, f32[1024]{0:T(1024)S(1)} %add_rsqrt_fusion, f32[1024,1024]{0,1:T(8,128)} %get-tuple-element.335, bf16[1024,4096]{1,0:T(8,128)(2,1)} %get-tuple-element.336, bf16[1024,4096]{1,0:T(8,128)(2,1)} %all-gather.28.cloned.1.call-done), kind=kOutput, calls=%fused_computation.78 | convolution fusion | flops 8595176448 | bytes 29368320 | tf_op jit(solution)/shard_map/nf,df->nd/dot_general | solution.py:233
  641.0 316.0 %while.51 = (s32[]{:T(128)}, f32[16,1024,64]{1,2,0:T(8,128)}, f32[16,1024,64]{1,2,0:T(8,128)}, bf16[16,1024,64]{1,2,0:T(8,128)(2,1)}, s32[16]{0:T(128)S(1)}, /*i...) while((s32[]{:T(128)}, f32[16,1024,64]{1,2,0:T(8,128)}, ...), condition=%wide.region_9.10_spmd.clone.clone, body=%wide.region_7.9_spmd.clone.sunk.clone | while | flops 684850176 | bytes 50889468 | solution.py:121
  980.2 10.9 multiply_reduce_fusion.1
  995.6 10.2 add_convert_fusion
  1023.7 12.3 convolution_convert_fusion.2
  1046.6 14.3 convolution_convert_fusion.1
  1062.5 17.5 %convolution_convert_fusion = bf16[4096,1024]{1,0:T(8,128)(2,1)} fusion(bf16[1024,1024]{1,0:T(8,128)(2,1)S(1)} %copy-done.26, f32[1024,4096]{1,0:T(8,128)} %get-tuple-element.337), kind=kOutput, calls=%fused_computation.58 | convolution fusion | flops 8631877632 | bytes 27262976 | tf_op jit(solution)/shard_map/nf,nd->fd/dot_general | solution.py:228
  1080.0 11.4 copy.61
  1096.9 62.8 %reduce-scatter.45.cloned.1.call-done = bf16[384,1024]{1,0:T(8,128)(2,1)} async-done(((bf16[3072,1024]{1,0:T(8,128)(2,1)}), bf16[384,1024]{1,0:T(8,128)(2,1)}) %reduce-scatter.45.cloned.1.call-update) | async-done | bytes 786448
  1162.2 87.7 %reduce-scatter.37.cloned.1.call-done = bf16[1024,512]{1,0:T(8,128)(2,1)} async-done(((bf16[1024,4096]{1,0:T(8,128)(2,1)}), bf16[1024,512]{1,0:T(8,128)(2,1)}) %reduce-scatter.37.cloned.1.call-update) | async-done | bytes 1048592 | tf_op jit(solution)/shard_map/reduce_scatter | solution.py:309
  1250.2 89.8 %reduce-scatter.49.cloned.1.call-done = bf16[128,4096]{1,0:T(8,128)(2,1)} async-done(((bf16[1024,4096]{1,0:T(8,128)(2,1)}), bf16[128,4096]{1,0:T(8,128)(2,1)}) %reduce-scatter.49.cloned.1.call-update) | async-done | bytes 1048592
  1342.3 16.7 %add_convert_fusion.1 = bf16[1024,1024]{0,1:T(8,128)(2,1)} fusion(f32[1024,1024]{0,1:T(8,128)} %copy-done.3, bf16[4096,1024]{1,0:T(8,128)(2,1)} %all-gather.32.cloned.1.call-done, f32[1024,4096]{1,0:T(8,128)} %get-tuple-element.337), kind=kOutput, calls=%fused_computation.79 | convolution fusion | flops 8629780480 | bytes 31457280 | tf_op jit(solution)/shard_map/dot_general | solution.py:207
  1378.8 14.1 reduce-scatter.35.cloned.1.call-done
  1394.5 25.3 %reduce-scatter.27.cloned.1.call-done = bf16[256,128]{0,1:T(8,128)(2,1)} async-done(((bf16[1024,128]{0,1:T(8,128)(2,1)}), bf16[256,128]{0,1:T(8,128)(2,1)}) %reduce-scatter.27.cloned.1.call-update) | async-done | bytes 65552 | tf_op jit(solution)/shard_map/reduce_scatter | solution.py:320
  1421.3 26.9 %reduce-scatter.23.cloned.1.call-done = bf16[512,128]{1,0:T(8,128)(2,1)} async-done(((bf16[2048,128]{1,0:T(8,128)(2,1)}), bf16[512,128]{1,0:T(8,128)(2,1)}) %reduce-scatter.23.cloned.1.call-update) | async-done | bytes 131088 | tf_op jit(solution)/shard_map/reduce_scatter | solution.py:317
  1449.8 27.4 %reduce-scatter.29.cloned.1.call-done = bf16[256,384]{1,0:T(8,128)(2,1)} async-done(((bf16[1024,384]{1,0:T(8,128)(2,1)}), bf16[256,384]{1,0:T(8,128)(2,1)}) %reduce-scatter.29.cloned.1.call-update) | async-done | bytes 196624 | tf_op jit(solution)/shard_map/reduce_scatter | solution.py:323
  1478.9 28.8 %reduce-scatter.39.cloned.1.call-done = bf16[256,512]{1,0:T(8,128)(2,1)} async-done(((bf16[1024,512]{1,0:T(8,128)(2,1)}), bf16[256,512]{1,0:T(8,128)(2,1)}) %reduce-scatter.39.cloned.1.call-update) | async-done | bytes 262160 | tf_op jit(solution)/shard_map/reduce_scatter | solution.py:332
  1509.5 29.1 %reduce-scatter.41.cloned.1.call-done = bf16[1024,128]{1,0:T(8,128)(2,1)} async-done(((bf16[4096,128]{1,0:T(8,128)(2,1)}), bf16[1024,128]{1,0:T(8,128)(2,1)}) %reduce-scatter.41.cloned.1.call-update) | async-done | bytes 262160 | tf_op jit(solution)/shard_map/reduce_scatter | solution.py:335
  (488 shorter events, 648.7 us)
Async XLA Ops:
  7.2 125.9 %copy-start = (bf16[1,4,1024]{2,1,0:T(4,128)(2,1)S(1)}, bf16[1,4,1024]{2,1,0:T(4,128)(2,1)}, u32[]{:S(2)}) copy-start(bf16[1,4,1024]{2,1,0:T(4,128)(2,1)} %param.20) | copy-start | bytes 24580
  7.2 57.5 %copy-start.36 = (bf16[256,128]{1,0:T(8,128)(2,1)S(1)}, bf16[256,128]{1,0:T(8,128)(2,1)}, u32[]{:S(2)}) copy-start(bf16[256,128]{1,0:T(8,128)(2,1)} %param.27) | copy-start | bytes 196612
  7.2 36.1 %all-gather.12.cloned.1.call-start = ((), (), s32[]{:S(2)}) async-start(), calls=%async_computation.14 | async-start | bytes 1179648 | tf_op jit(solution)/shard_map/all_gather | solution.py:142
  7.9 56.7 %all-gather.18.cloned.1.call-start = ((), (), s32[]{:S(2)}) async-start(), calls=%async_computation.17 | async-start | bytes 1769472 | tf_op jit(solution)/shard_map/all_gather | solution.py:144
  8.7 87.9 %all-gather.30.cloned.1.call-start = ((), (), s32[]{:S(2)}) async-start(), calls=%async_computation.23 | async-start | bytes 2359296 | tf_op jit(solution)/shard_map/all_gather | solution.py:148
  9.4 87.3 %copy-start.38 = (s32[1,1024]{1,0:T(1,128)S(1)}, s32[1,1024]{1,0:T(1,128)}, u32[]{:S(2)}) copy-start(s32[1,1024]{1,0:T(1,128)} %param.22) | copy-start | bytes 12292
  9.4 123.7 %all-gather.16.cloned.1.call-start = ((), (), s32[]{:S(2)}) async-start(), calls=%async_computation.16 | async-start | bytes 2621440 | tf_op jit(solution)/shard_map/all_gather | solution.py:152
  26.6 143.6 %all-gather.24.cloned.1.call-start = ((), (), s32[]{:S(2)}) async-start(), calls=%async_computation.20 | async-start | bytes 2621440 | tf_op jit(solution)/shard_map/all_gather | solution.py:155
  42.6 158.1 %all-gather.26.cloned.1.call-start = ((), (), s32[]{:S(2)}) async-start(), calls=%async_computation.21 | async-start | bytes 2359296 | tf_op jit(solution)/shard_map/all_gather | solution.py:147
  43.2 211.6 %all-gather.14.cloned.1.call-start = ((), (), s32[]{:S(2)}) async-start(), calls=%async_computation.15 | async-start | bytes 5242880 | tf_op jit(solution)/shard_map/all_gather | solution.py:151
  44.0 282.9 %all-gather.20.cloned.1.call-start = ((), (), s32[]{:S(2)}) async-start(), calls=%async_computation.18 | async-start | bytes 7864320 | tf_op jit(solution)/shard_map/all_gather | solution.py:153
  64.7 483.9 %all-gather.22.cloned.1.call-start = ((), (), s32[]{:S(2)}) async-start(), calls=%async_computation.19 | async-start | bytes 2621440 | tf_op jit(solution)/shard_map/all_gather | solution.py:154
  79.8 482.8 %all-gather.32.cloned.1.call-start = ((), (), s32[]{:S(2)}) async-start(), calls=%async_computation.24 | async-start | bytes 10485760 | tf_op jit(solution)/shard_map/all_gather | solution.py:157
  96.6 480.5 %all-gather.28.cloned.1.call-start = ((), (), s32[]{:S(2)}) async-start(), calls=%async_computation.22 | async-start | bytes 10485760 | tf_op jit(solution)/shard_map/all_gather | solution.py:156
  97.8 262.5 %copy-start.17 = (f32[1024,64]{0,1:T(8,128)}, f32[1024,64]{0,1:T(8,128)S(1)}, u32[]{:S(2)}) copy-start(f32[1024,64]{0,1:T(8,128)S(1)} %get-tuple-element.327) | copy-start | bytes 786436
  200.8 63.8 %copy-start.33 = (s32[1,1024]{1,0:T(1,128)S(1)}, s32[1,1024]{1,0:T(1,128)}, u32[]{:S(2)}) copy-start(s32[1,1024]{1,0:T(1,128)} %param.21) | copy-start | bytes 12292
  200.8 890.8 %reduce-scatter.47.cloned.1.call-start = ((), (), s32[]{:S(2)}) async-start(), calls=%async_computation.37 | async-start | bytes 2359296
  268.8 67.1 %copy-start.28 = (bf16[1024,1024]{0,1:T(8,128)(2,1)}, bf16[1024,1024]{0,1:T(8,128)(2,1)S(1)}, u32[]{:S(2)}) copy-start(bf16[1024,1024]{0,1:T(8,128)(2,1)S(1)} %get-tuple-element.330) | copy-start | bytes 6291460
  606.1 16.3 %copy-start.10 = (bf16[1024,1024]{0,1:T(8,128)(2,1)S(1)}, bf16[1024,1024]{0,1:T(8,128)(2,1)}, u32[]{:S(2)}) copy-start(bf16[1024,1024]{0,1:T(8,128)(2,1)} %copy.50) | copy-start | bytes 6291460
  635.1 458.4 %reduce-scatter.33.cloned.1.call-start = ((), (), s32[]{:S(2)}) async-start(), calls=%async_computation.30 | async-start | bytes 2359296 | tf_op jit(solution)/shard_map/reduce_scatter | solution.py:306
  965.4 128.6 %reduce-scatter.25.cloned.1.call-start = ((), (), s32[]{:S(2)}) async-start(), calls=%async_computation.26 | async-start | bytes 2359296 | tf_op jit(solution)/shard_map/reduce_scatter | solution.py:297
  995.5 99.2 %reduce-scatter.43.cloned.1.call-start = ((), (), s32[]{:S(2)}) async-start(), calls=%async_computation.35 | async-start | bytes 4718592
  1022.1 137.6 %reduce-scatter.45.cloned.1.call-start = ((), (), s32[]{:S(2)}) async-start(), calls=%async_computation.36 | async-start | bytes 7077888
  1044.7 205.2 %reduce-scatter.37.cloned.1.call-start = ((), (), s32[]{:S(2)}) async-start(), calls=%async_computation.32 | async-start | bytes 9437184 | tf_op jit(solution)/shard_map/reduce_scatter | solution.py:309
  1060.9 279.2 %reduce-scatter.49.cloned.1.call-start = ((), (), s32[]{:S(2)}) async-start(), calls=%async_computation.38 | async-start | bytes 9437184
  1091.5 285.8 %reduce-scatter.31.cloned.1.call-start = ((), (), s32[]{:S(2)}) async-start(), calls=%async_computation.29 | async-start | bytes 327680 | tf_op jit(solution)/shard_map/reduce_scatter | solution.py:326
  1093.4 299.5 %reduce-scatter.35.cloned.1.call-start = ((), (), s32[]{:S(2)}) async-start(), calls=%async_computation.31 | async-start | bytes 327680 | tf_op jit(solution)/shard_map/reduce_scatter | solution.py:329
  1094.0 325.8 %reduce-scatter.27.cloned.1.call-start = ((), (), s32[]{:S(2)}) async-start(), calls=%async_computation.27 | async-start | bytes 327680 | tf_op jit(solution)/shard_map/reduce_scatter | solution.py:320
  1094.7 353.5 %reduce-scatter.23.cloned.1.call-start = ((), (), s32[]{:S(2)}) async-start(), calls=%async_computation.25 | async-start | bytes 655360 | tf_op jit(solution)/shard_map/reduce_scatter | solution.py:317
  1096.9 380.4 %reduce-scatter.29.cloned.1.call-start = ((), (), s32[]{:S(2)}) async-start(), calls=%async_computation.28 | async-start | bytes 983040 | tf_op jit(solution)/shard_map/reduce_scatter | solution.py:323
  1162.1 345.6 %reduce-scatter.39.cloned.1.call-start = ((), (), s32[]{:S(2)}) async-start(), calls=%async_computation.33 | async-start | bytes 1310720 | tf_op jit(solution)/shard_map/reduce_scatter | solution.py:332
  1249.9 288.7 %reduce-scatter.41.cloned.1.call-start = ((), (), s32[]{:S(2)}) async-start(), calls=%async_computation.34 | async-start | bytes 1310720 | tf_op jit(solution)/shard_map/reduce_scatter | solution.py:335
  (62 other events, 239.1 us)
Sparse Core Ops, SparseCore 0:
  9.6 29.2 all-gather.11
  40.5 24.0 all-gather.17
  66.2 30.3 all-gather.29
  98.3 34.7 all-gather.15
  134.8 35.2 all-gather.23
  171.6 29.0 all-gather.25
  202.6 52.1 all-gather.13
  256.6 70.1 all-gather.19
  328.7 35.3 all-gather.21
  365.7 87.5 all-gather.31
  455.2 87.6 all-gather.27
  635.2 35.9 reduce-scatter.46
  965.5 35.9 reduce-scatter.32
  1003.7 34.5 reduce-scatter.24
  1041.0 48.5 reduce-scatter.42
  1091.8 67.9 reduce-scatter.44
  1161.9 87.9 reduce-scatter.36
  1252.0 87.9 reduce-scatter.48
  1343.4 22.4 reduce-scatter.30
  1368.7 24.1 reduce-scatter.34
  1395.6 24.0 reduce-scatter.26
  1423.4 24.7 reduce-scatter.22
  1451.1 26.0 reduce-scatter.28
  1480.0 27.6 reduce-scatter.38
  1510.9 27.7 reduce-scatter.40
where the time goes:
time: 1560 us; the launch traced here: 1550 us
  waiting for transfers between devices  624 us (40%)
  matrix products  554 us (36%)
  local copies, waits for them, and re-layouts  169 us (11%)
  other arithmetic  83 us (5%)
  loops' own time  53.5 us (3%)
  blocking collectives  48.1 us (3%)
    unnamed x29, waiting for transfers between devices  157 us
    dot_general x32, matrix products, masked_scores(): jnp.einsum('qd,kd->qk', query_head, key_head, preferred_element_type=jnp....  106 us
    reduce_scatter x1, waiting for transfers between devices, shards(): lax.psum_scatter(grad_up.astype(jnp.bfloat16), 'fsdp', scatter_dimension=...  87.7 us
    unnamed x88, local copies, waits for them, and re-layouts  72.9 us
    dot_general x16, matrix products, one_head(): jnp.einsum('qd,kd->qk', grad_head, value_head, preferred_element_type=jnp...  61.5 us
    dot_general x16, matrix products, one_head(): jnp.dot(soft_low, head_cut(value_rows, head_index), preferred_element_typ...  61.5 us
    all_gather x1, waiting for transfers between devices, shards(): lax.all_gather(part_qkv, 'dp', axis=0, tiled=True)  58.1 us
    all_gather x1, waiting for transfers between devices, shards(): lax.all_gather(part_skip, 'dp', axis=0, tiled=True)  53.8 us
  transfers between devices with their start and end apart: 25, of which 16 were waited for; matrix products, arithmetic and copies ran while one was open for 45% of the time, Pallas kernels for 0%

commit v1 on v0

v1 whole, which is shorter than its diff:
```python
import functools

import jax
import jax.numpy as jnp
from jax import lax
from jax.experimental import pallas as pl
from jax.experimental.pallas import tpu as pltpu
from jax.sharding import PartitionSpec as P

HD = 64
NB = 8
EPS = 1e-06
MASKED = -1e30
BF = jnp.bfloat16
F32 = jnp.float32
NN = (((1,), (0,)), ((), ()))
NT = (((1,), (1,)), ((), ()))
TN = (((0,), (0,)), ((), ()))
ROOT = 0.7978845608028654
CUBE = 0.044715


def dot(left, right, form=NN):
    return lax.dot_general(left, right, form, preferred_element_type=F32)


def params(**extra):
    return pltpu.CompilerParams(vmem_limit_bytes=60 << 20, **extra)


def whole(shape):
    return pl.BlockSpec(shape, lambda *_: (0,) * len(shape))


def shaped(shape, kind):
    return jax.ShapeDtypeStruct(shape, kind)


def columns(ref, first, count, rows=slice(None)):
    return jnp.concatenate([ref[first + i, rows, :] for i in range(count)], axis=1)


def token_gain(seg, gamma):
    gain = gamma[0:1, :]
    for slot in range(1, 4):
        gain = jnp.where(seg == slot, gamma[slot : slot + 1, :], gain)
    return gain


def segment_sum(seg_row, values):
    slots = lax.broadcasted_iota(jnp.int32, (8, seg_row.shape[1]), 0)
    picked = (slots == seg_row).astype(BF)
    high = values.astype(BF)
    low = (values - high.astype(F32)).astype(BF)
    return dot(picked, high) + dot(picked, low)


def norm_back(grad, stream, gain):
    inverse = lax.rsqrt(jnp.mean(stream * stream, axis=-1, keepdims=True) + EPS)
    unit = stream * inverse
    scaled = grad * (1.0 + gain)
    d_stream = inverse * (scaled - unit * jnp.mean(scaled * unit, axis=-1, keepdims=True))
    return d_stream, grad * unit


def norm(stream, gain):
    inverse = lax.rsqrt(jnp.mean(stream * stream, axis=-1, keepdims=True) + EPS)
    return (stream * inverse * (1.0 + gain)).astype(BF)


def front_body(x_ref, s_ref, w_ref, time_ref, ada_ref, seg_ref, stream_ref, normed_ref, g1_ref, g2_ref):
    length, width = x_ref.shape
    per = ada_ref.shape[2] // 2
    for f in range(NB):
        both = dot(time_ref[...], ada_ref[f])
        g1_ref[:, f * per : (f + 1) * per] = both[:, :per]
        g2_ref[:, f * per : (f + 1) * per] = both[:, per:]
    for i in range(NB // 2):
        tile = columns(w_ref, 2 * i, 2)
        part = dot(x_ref[...], tile[:width]) + dot(s_ref[...], tile[width:])
        stream_ref[:, i * part.shape[1] : (i + 1) * part.shape[1]] = part

    @pl.loop(0, length // 128)
    def _(t):
        rows = pl.ds(pl.multiple_of(t * 128, 128), 128)
        gain = token_gain(seg_ref[rows, :], g1_ref)
        normed_ref[rows, :] = norm(stream_ref[rows, :], gain)


def front(inputs, skip_in, w_skip, time8, ada, seg_col):
    length, width = inputs.shape
    return pl.pallas_call(
        front_body,
        out_shape=(
            shaped((length, width), F32),
            shaped((length, width), BF),
            shaped((8, width), F32),
            shaped((8, width), F32),
        ),
        compiler_params=params(),
        name="front",
    )(inputs, skip_in, w_skip, time8, ada, seg_col)


def key_bias(seg_col, pad_col, seg_row, length):
    keys = lax.broadcasted_iota(jnp.int32, (length, length), 0)
    queries = lax.broadcasted_iota(jnp.int32, (length, length), 1)
    allowed = (seg_col == seg_row) & ((pad_col > 0) | (keys == queries))
    return jnp.where(allowed, 0.0, MASKED)


def fill_bias(bias_ref, seg_ref, pad_ref, row_ref):
    length = seg_ref.shape[0]
    for t in range(length // 128):
        rows = slice(t * 128, (t + 1) * 128)
        keys = lax.broadcasted_iota(jnp.int32, (128, length), 0) + t * 128
        queries = lax.broadcasted_iota(jnp.int32, (128, length), 1)
        allowed = (seg_ref[rows, :] == row_ref[0:1, :]) & (
            (pad_ref[rows, :] > 0) | (keys == queries)
        )
        bias_ref[rows, :] = jnp.where(allowed, 0.0, MASKED)


def turn(unit, cosine, before, after):
    return (
        unit * cosine
        + pltpu.roll(unit, 96, 1) * before
        + pltpu.roll(unit, 32, 1) * after
    )


def attend_body(
    n_ref, qa, qb, ka, kb, va, vb, cos_ref, lo_ref, hi_ref, seg_ref, pad_ref, row_ref,
    q_ref, k_ref, v_ref, c_ref, lse_ref, bias_ref,
):
    @pl.when(pl.program_id(0) == 0)
    def _():
        fill_bias(bias_ref, seg_ref, pad_ref, row_ref)

    normed = n_ref[...]
    for out, first, second, scale in ((q_ref, qa, qb, HD**-0.5), (k_ref, ka, kb, 1.0)):
        made = dot(normed, jnp.concatenate([first[0], second[0]], axis=1))
        for half in range(2):
            unit = made[:, half * 128 : (half + 1) * 128]
            turned = turn(unit, cos_ref[...], lo_ref[...], hi_ref[...])
            out[:, half * 128 : (half + 1) * 128] = (turned.astype(BF) * scale).astype(BF)
    v_ref[...] = dot(normed, jnp.concatenate([va[0], vb[0]], axis=1)).astype(BF)
    for head in range(4):
        lanes = slice(head * HD, (head + 1) * HD)
        scores = dot(k_ref[:, lanes], q_ref[:, lanes], NT) + bias_ref[...]
        largest = jnp.max(scores, axis=0, keepdims=True)
        exponent = jnp.exp(scores - largest)
        total = jnp.sum(exponent, axis=0, keepdims=True)
        mixed = dot(v_ref[:, lanes].T, exponent.astype(BF)) * (1.0 / total)
        c_ref[:, lanes] = mixed.T.astype(BF)
        lse_ref[head : head + 1, :] = largest + jnp.log(total)


def unit_spec(rows, base):
    def index(j):
        unit = base + 2 * j
        return (unit // 3, 0, unit % 3)

    return pl.BlockSpec((1, rows, 128), index)


def attend(normed, w_qkv, tables, seg_col, pad_col, seg_row):
    length, width = normed.shape
    groups = width // 256
    units = [unit_spec(width, part * (width // 128) + e) for part in range(3) for e in range(2)]
    column = pl.BlockSpec((length, 256), lambda j: (0, j))
    wide = shaped((length, width), BF)
    return pl.pallas_call(
        attend_body,
        grid=(groups,),
        in_specs=[whole((length, width))]
        + units
        + [whole((length, 128))] * 3
        + [whole((length, 1))] * 2
        + [whole((1, length))],
        out_specs=(column,) * 4 + (pl.BlockSpec((8, length), lambda j: (j, 0)),),
        out_shape=(wide,) * 4 + (shaped((8 * groups, length), F32),),
        scratch_shapes=[pltpu.VMEM((length, length), F32)],
        compiler_params=params(),
        name="attend",
    )(normed, *([w_qkv] * 6), *tables, seg_col, pad_col, seg_row)


def mlp_body(
    stream0_ref, ctx_ref, wout_ref, g2_ref, seg_ref, row_ref, up_ref, down_ref, cot_ref,
    out_ref, gdown_ref, gup_ref, gout_ref, ds1_ref, dctx_ref, dg2_ref,
    s1_ref, n2_ref, acc_ref, dn_ref,
):
    step = pl.program_id(0)
    length, width = ctx_ref.shape
    tiles = length // 128

    @pl.when(step == 0)
    def _():
        @pl.loop(0, NB // 2)
        def _(i):
            lanes = pl.ds(pl.multiple_of(i * 256, 256), 256)
            s1_ref[:, lanes] = stream0_ref[:, lanes] + dot(ctx_ref[...], columns(wout_ref, 2 * i, 2))

        @pl.loop(0, tiles)
        def _(t):
            rows = pl.ds(pl.multiple_of(t * 128, 128), 128)
            n2_ref[rows, :] = norm(s1_ref[rows, :], token_gain(seg_ref[rows, :], g2_ref))

        acc_ref[...] = jnp.zeros_like(acc_ref)
        dn_ref[...] = jnp.zeros_like(dn_ref)

    cot = cot_ref[...]
    up = up_ref[0]
    down = columns(down_ref, 0, NB)
    hidden = dot(n2_ref[...], up)
    square = hidden * hidden
    tanh = jnp.tanh(ROOT * hidden * (1.0 + CUBE * square))
    active = (0.5 * hidden * (1.0 + tanh)).astype(BF)
    slope = 0.5 * (1.0 + tanh) + 0.5 * hidden * (1.0 - tanh * tanh) * (
        ROOT * (1.0 + 3.0 * CUBE * square)
    )
    d_pre = (dot(cot, down, NT) * slope).astype(BF)
    acc_ref[...] += dot(active, down)
    dn_ref[...] += dot(d_pre, up, NT)
    grad = dot(active, cot, TN).astype(BF)
    for f in range(NB):
        gdown_ref[f] = grad[:, f * gdown_ref.shape[2] : (f + 1) * gdown_ref.shape[2]]
    gup_ref[0] = dot(n2_ref[...], d_pre, TN).astype(BF)

    @pl.when(step == pl.num_programs(0) - 1)
    def _():
        dg2_ref[...] = jnp.zeros_like(dg2_ref)

        @pl.loop(0, tiles)
        def _(t):
            rows = pl.ds(pl.multiple_of(t * 128, 128), 128)
            stream = s1_ref[rows, :]
            out_ref[rows, :] = (stream + acc_ref[rows, :]).astype(BF)
            gain = token_gain(seg_ref[rows, :], g2_ref)
            term, d_gain = norm_back(dn_ref[rows, :], stream, gain)
            d_stream = cot_ref[rows, :].astype(F32) + term
            ds1_ref[rows, :] = d_stream
            n2_ref[rows, :] = d_stream.astype(BF)
            dg2_ref[...] += segment_sum(row_ref[:, rows], d_gain)

        @pl.loop(0, NB // 2)
        def _(i):
            lanes = pl.ds(pl.multiple_of(i * 256, 256), 256)
            part = dot(ctx_ref[...], n2_ref[:, lanes], TN).astype(BF)
            gout_ref[2 * i] = part[:, :128]
            gout_ref[2 * i + 1] = part[:, 128:]

        acc_ref[...] = jnp.zeros_like(acc_ref)

        @pl.loop(0, NB // 2)
        def _(i):
            lanes = pl.ds(pl.multiple_of(i * 256, 256), 256)
            acc_ref[...] += dot(n2_ref[:, lanes], columns(wout_ref, 2 * i, 2), NT)

        dctx_ref[...] = acc_ref[...].astype(BF)


def mlp(stream0, ctx, w_out, gamma2, seg_col, seg_row, w_up, w_down, cotangent):
    length, width = ctx.shape
    hidden = w_down.shape[1]
    piece = hidden // NB
    per = width // NB
    full = whole((length, width))
    return pl.pallas_call(
        mlp_body,
        grid=(NB,),
        in_specs=[
            full,
            full,
            whole((NB, width, per)),
            whole((8, width)),
            whole((length, 1)),
            whole((1, length)),
            pl.BlockSpec((1, width, piece), lambda j: (j, 0, 0)),
            pl.BlockSpec((NB, piece, per), lambda j: (0, j, 0)),
            full,
        ],
        out_specs=(
            full,
            pl.BlockSpec((NB, piece, per), lambda j: (0, j, 0)),
            pl.BlockSpec((1, width, piece), lambda j: (j, 0, 0)),
            whole((NB, width, per)),
            full,
            full,
            whole((8, width)),
        ),
        out_shape=(
            shaped((length, width), BF),
            shaped((NB, hidden, per), BF),
            shaped((NB, width, piece), BF),
            shaped((NB, width, per), BF),
            shaped((length, width), F32),
            shaped((length, width), BF),
            shaped((8, width), F32),
        ),
        scratch_shapes=[
            pltpu.VMEM((length, width), F32),
            pltpu.VMEM((length, width), BF),
            pltpu.VMEM((length, width), F32),
            pltpu.VMEM((length, width), F32),
        ],
        compiler_params=params(),
        name="mlp",
    )(stream0, ctx, w_out, gamma2, seg_col, seg_row, w_up, w_down, cotangent)


def attend_back_body(
    n_ref, qa, qb, ka, kb, va, vb, cos_ref, lo_ref, hi_ref, seg_ref, pad_ref, row_ref,
    q_ref, k_ref, v_ref, g_ref, c_ref, lse_ref, s0_ref, g1_ref, ds1_ref,
    gw_ref, dlow_ref, dg1_ref, bias_ref, dn_ref, dq_ref, dk_ref, dv_ref,
):
    step = pl.program_id(0)
    length, width = n_ref.shape

    @pl.when(step == 0)
    def _():
        fill_bias(bias_ref, seg_ref, pad_ref, row_ref)
        dn_ref[...] = jnp.zeros_like(dn_ref)

    ones = jnp.ones((8, HD), BF)
    for head in range(4):
        lanes = slice(head * HD, (head + 1) * HD)
        query, key, value = q_ref[:, lanes], k_ref[:, lanes], v_ref[:, lanes]
        grad = g_ref[:, lanes]
        both = grad.astype(F32) * c_ref[:, lanes].astype(F32)
        high = both.astype(BF)
        low = (both - high.astype(F32)).astype(BF)
        delta = (dot(ones, high, NT) + dot(ones, low, NT))[0:1, :]
        probs = jnp.exp(dot(key, query, NT) + bias_ref[...] - lse_ref[head : head + 1, :])
        d_scores = (probs * (dot(value, grad, NT) - delta)).astype(BF)
        dv_ref[:, lanes] = dot(probs.astype(BF), grad)
        dk_ref[:, lanes] = dot(d_scores, query)
        dq_ref[:, lanes] = dot(key.T, d_scores).T * HD**-0.5
    for part, (src, first, second) in enumerate(
        ((dq_ref, qa, qb), (dk_ref, ka, kb), (dv_ref, va, vb))
    ):
        if part < 2:
            made = jnp.concatenate(
                [
                    turn(src[:, half * 128 : (half + 1) * 128], cos_ref[...], -lo_ref[...], -hi_ref[...])
                    for half in range(2)
                ],
                axis=1,
            ).astype(BF)
        else:
            made = src[...].astype(BF)
        grad = dot(n_ref[...], made, TN).astype(BF)
        gw_ref[part, 0] = grad[:, :128]
        gw_ref[part, 1] = grad[:, 128:]
        dn_ref[...] += dot(made, jnp.concatenate([first[0], second[0]], axis=1), NT)

    @pl.when(step == pl.num_programs(0) - 1)
    def _():
        dg1_ref[...] = jnp.zeros_like(dg1_ref)

        @pl.loop(0, length // 128)
        def _(t):
            rows = pl.ds(pl.multiple_of(t * 128, 128), 128)
            gain = token_gain(seg_ref[rows, :], g1_ref)
            term, d_gain = norm_back(dn_ref[rows, :], s0_ref[rows, :], gain)
            dlow_ref[rows, :] = (ds1_ref[rows, :] + term).astype(BF)
            dg1_ref[...] += segment_sum(row_ref[:, rows], d_gain)


def attend_back(
    normed, w_qkv, tables, seg_col, pad_col, seg_row, q, k, v, d_ctx, ctx, lse, stream0, gamma1, d_stream1
):
    length, width = normed.shape
    groups = width // 256
    units = [unit_spec(width, part * (width // 128) + e) for part in range(3) for e in range(2)]
    column = pl.BlockSpec((length, 256), lambda j: (0, j))
    full = whole((length, width))
    return pl.pallas_call(
        attend_back_body,
        grid=(groups,),
        in_specs=[full]
        + units
        + [whole((length, 128))] * 3
        + [whole((length, 1))] * 2
        + [whole((1, length))]
        + [column] * 5
        + [pl.BlockSpec((8, length), lambda j: (j, 0)), full, whole((8, width)), full],
        out_specs=(
            pl.BlockSpec((3, 2, width, 128), lambda j: (0, j, 0, 0)),
            full,
            whole((8, width)),
        ),
        out_shape=(
            shaped((3, width // 128, width, 128), BF),
            shaped((length, width), BF),
            shaped((8, width), F32),
        ),
        scratch_shapes=[pltpu.VMEM((length, length), F32), pltpu.VMEM((length, width), F32)]
        + [pltpu.VMEM((length, 256), F32)] * 3,
        compiler_params=params(),
        name="attend_back",
    )(
        normed, *([w_qkv] * 6), *tables, seg_col, pad_col, seg_row, q, k, v, d_ctx, ctx, lse,
        stream0, gamma1, d_stream1,
    )


def skip_back_body(x_ref, s_ref, d_ref, w_ref, gw_ref, dx_ref, ds_ref):
    low = d_ref[...]
    per = 256
    width = x_ref.shape[1]

    @pl.loop(0, width // per)
    def _(i):
        lanes = pl.ds(pl.multiple_of(i * per, per), per)
        part = d_ref[:, lanes]
        top = dot(x_ref[...], part, TN).astype(BF)
        end = dot(s_ref[...], part, TN).astype(BF)
        for e in range(2):
            gw_ref[2 * i + e, :width, :] = top[:, e * 128 : (e + 1) * 128]
            gw_ref[2 * i + e, width:, :] = end[:, e * 128 : (e + 1) * 128]

    tall = 256

    @pl.loop(0, width // tall)
    def _(i):
        rows = pl.ds(pl.multiple_of(i * tall, tall), tall)
        rest = pl.ds(pl.multiple_of(width + i * tall, tall), tall)
        dx_ref[:, rows] = dot(low, columns(w_ref, 0, NB, rows), NT)
        ds_ref[:, rows] = dot(low, columns(w_ref, 0, NB, rest), NT)


def skip_back(inputs, skip_in, d_low, w_skip):
    length, width = inputs.shape
    return pl.pallas_call(
        skip_back_body,
        out_shape=(
            shaped(w_skip.shape, BF),
            shaped((length, width), F32),
            shaped((length, width), F32),
        ),
        compiler_params=params(),
        name="skip_back",
    )(inputs, skip_in, d_low, w_skip)


def rotary(positions):
    half = HD // 2
    lane = jnp.arange(128)
    frequency = 10000.0 ** (-2.0 * (lane % half).astype(F32) / HD)
    phase = positions.reshape(-1, 1).astype(F32) * frequency[None, :]
    cosine, sine = jnp.cos(phase), jnp.sin(phase)
    early = (lane % HD < half)[None, :]
    return cosine, jnp.where(early, -sine, 0.0), jnp.where(early, 0.0, sine)


def gathered(shard):
    blocks = lax.all_gather(shard, "fsdp", axis=0, tiled=False)
    blocks = lax.all_gather(blocks, "dp", axis=1, tiled=True)
    count, rows, per = blocks.shape
    if count == NB:
        return blocks
    flat = jnp.transpose(blocks, (1, 0, 2)).reshape(rows, count * per)
    return jnp.transpose(flat.reshape(rows, NB, count * per // NB), (1, 0, 2))


def scattered(blocks):
    count, rows, per = blocks.shape
    flat = jnp.transpose(blocks, (1, 0, 2)).reshape(rows, count * per)
    part = lax.psum_scatter(flat, "fsdp", scatter_dimension=1, tiled=True)
    return lax.psum_scatter(part, "dp", scatter_dimension=0, tiled=True).astype(F32)


def shards(
    inputs, skip_in, time_emb, seg_ids, positions, pad_mask,
    w_skip, w_ada1, w_qkv, w_out, w_ada2, w_up, w_down, cotangent,
):
    slots = time_emb.shape[1]
    seg_col, seg_row = seg_ids.reshape(-1, 1), seg_ids.reshape(1, -1)
    pad_col = pad_mask.reshape(-1, 1)
    tables = rotary(positions)
    flat_time = time_emb.reshape(slots, -1)
    time8 = jnp.pad(flat_time, ((0, 8 - slots), (0, 0)))
    f_skip, f_qkv, f_out = gathered(w_skip), gathered(w_qkv), gathered(w_out)
    f_up, f_down = gathered(w_up), gathered(w_down)
    f_ada1, f_ada2 = gathered(w_ada1), gathered(w_ada2)
    ada = jnp.concatenate([f_ada1, f_ada2], axis=2)
    stream0, normed1, gamma1, gamma2 = front(inputs, skip_in, f_skip, time8, ada, seg_col)
    q, k, v, ctx, lse = attend(normed1, f_qkv, tables, seg_col, pad_col, seg_row)
    output, g_down, g_up, g_out, d_stream1, d_ctx, d_gamma2 = mlp(
        stream0, ctx, f_out, gamma2, seg_col, seg_row, f_up, f_down, cotangent
    )
    g_qkv, d_low, d_gamma1 = attend_back(
        normed1, f_qkv, tables, seg_col, pad_col, seg_row, q, k, v, d_ctx, ctx, lse,
        stream0, gamma1, d_stream1,
    )
    width = inputs.shape[1]
    g_qkv = jnp.transpose(
        g_qkv.reshape(NB, 3, width, 128), (0, 2, 1, 3)
    ).reshape(NB, width, 3 * width // NB)
    g_skip, d_input, d_skip = skip_back(inputs, skip_in, d_low, f_skip)
    d_gammas = [d[:slots].astype(BF) for d in (d_gamma1, d_gamma2)]
    d_time = 0.0
    g_ada = []
    for d_gamma, full in zip(d_gammas, (f_ada1, f_ada2)):
        flat = jnp.transpose(full, (1, 0, 2)).reshape(width, width)
        d_time = d_time + jnp.einsum("ne,de->nd", d_gamma, flat, preferred_element_type=F32)
        g = jnp.einsum("nd,ne->de", flat_time, d_gamma, preferred_element_type=F32).astype(BF)
        g_ada.append(jnp.transpose(g.reshape(width, NB, width // NB), (1, 0, 2)))
    return (
        output,
        d_input,
        d_skip,
        d_time.reshape(time_emb.shape),
        scattered(g_skip),
        scattered(g_ada[0]),
        scattered(g_qkv),
        scattered(g_out),
        scattered(g_ada[1]),
        scattered(g_up),
        scattered(g_down),
    )


def solution(mesh):
    rows = P(("dp", "fsdp"), None)
    cube = P(("dp", "fsdp"), None, None)
    tile = P("dp", "fsdp")
    return jax.shard_map(
        shards,
        mesh=mesh,
        in_specs=(rows, rows, cube) + (rows,) * 3 + (tile,) * 7 + (rows,),
        out_specs=(rows, rows, rows, cube) + (tile,) * 7,
        check_vma=False,
    )
```

time: 1560 us -> 1290 us (0.83)
  matrix products: 554 us -> 8.89 us
  waiting for transfers between devices: 624 us -> 906 us
  Pallas kernels: 0 us -> 228 us
  local copies, waits for them, and re-layouts: 169 us -> 63 us
  other arithmetic: 83 us -> 9.6 us
  loops' own time: 53.5 us -> 0 us
    dot_general x137 -> x4, matrix products: 554 us -> 8.89 us  [the longest x2 5.88 us: shards(): jnp.einsum('nd,ne->de', flat_time, d_gamma, preferred_element_type=F32)]
    pallas_call x0 -> x5, Pallas kernels: none -> 228 us  [the longest x1 84.2 us: mlp(): pl.pallas_call(mlp_body, grid=(NB,), in_specs=[full, full, whole((NB, wid...]
    all_gather x11, waiting for transfers between devices: 227 us -> 414 us  [the longest x7 353 us: gathered(): blocks = lax.all_gather(blocks, 'dp', axis=1, tiled=True)]
    reduce_scatter x10 -> x13, waiting for transfers between devices: 239 us -> 418 us  [the longest x6 240 us: scattered(): part = lax.psum_scatter(flat, 'fsdp', scatter_dimension=1, tiled=True)]
    unnamed x29 -> x26, waiting for transfers between devices: 157 us -> 74.8 us
    unnamed x88 -> x23, local copies, waits for them, and re-layouts: 72.9 us -> 12.6 us
    another operation x2 -> x0, loops' own time: 53.5 us -> none  [the longest x1 42.6 us: attend_back(): d_query, d_key, d_value = lax.map(one_head, jnp.arange(heads_count))]
    convert_element_type x25 -> x2, other arithmetic: 49.6 us -> 1.7 us  [the longest x1 1.7 us: scattered(): lax.psum_scatter(part, 'dp', scatter_dimension=0, tiled=True).astype(F32)]
  transfers between devices with their start and end apart: 25 -> 25, of which waited for: 16 -> 21; matrix products, arithmetic and copies ran while one was open for 45% -> 6% of each run, Pallas kernels for 0% -> 11%
where the time goes in v1:
time: 1290 us; the launch traced here: 1280 us
  waiting for transfers between devices  906 us (70%)
  Pallas kernels  228 us (18%)
  local copies, waits for them, and re-layouts  63 us (5%)
  blocking collectives  51.3 us (4%)
  between operations  14.5 us (1%)
    all_gather x7, waiting for transfers between devices, gathered(): blocks = lax.all_gather(blocks, 'dp', axis=1, tiled=True)  353 us
    reduce_scatter x6, waiting for transfers between devices, scattered(): part = lax.psum_scatter(flat, 'fsdp', scatter_dimension=1, tiled=True)  240 us
    reduce_scatter x7, waiting for transfers between devices, scattered(): lax.psum_scatter(part, 'dp', scatter_dimension=0, tiled=True).astype(F32)  177 us
    pallas_call x1, Pallas kernels, mlp(): pl.pallas_call(mlp_body, grid=(NB,), in_specs=[full, full, whole((NB, wid...  84.2 us
    unnamed x26, waiting for transfers between devices  74.8 us
    pallas_call x1, Pallas kernels, attend_back(): pl.pallas_call(attend_back_body, grid=(groups,), in_specs=[full] + units...  73.1 us
    all_gather x4, waiting for transfers between devices, gathered(): blocks = lax.all_gather(shard, 'fsdp', axis=0, tiled=False)  61.1 us
    all_gather x3, blocking collectives, gathered(): blocks = lax.all_gather(shard, 'fsdp', axis=0, tiled=False)  51.3 us
  transfers between devices with their start and end apart: 25, of which 21 were waited for; matrix products, arithmetic and copies ran while one was open for 6% of the time, Pallas kernels for 11%

profile of v1, /device:TPU:0, one launch (start us, length us, event | category | flops | bytes accessed | tf_op | source)
XLA Modules:
  0.0 1282.8 jit_solution(985577151798637376)
XLA Ops:
  10.0 18.9 %all-gather.1 = bf16[2048,128]{1,0:T(8,128)(2,1)} all-gather(bf16[256,128]{1,0:T(8,128)(2,1)} %param.21), channel_id=3, replica_groups=mesh['dp'=4,'fsdp'=8] {'fsdp'}, dimensions={0}, use_global_device_ids=true | all-gather | bytes 589824 | tf_op jit(solution)/shard_map/all_gather | solution.py:459
  28.9 16.2 %all-gather.2 = bf16[2048,128]{1,0:T(8,128)(2,1)} all-gather(bf16[256,128]{1,0:T(8,128)(2,1)} %param.24), channel_id=4, replica_groups=mesh['dp'=4,'fsdp'=8] {'fsdp'}, dimensions={0}, use_global_device_ids=true | all-gather | bytes 589824 | tf_op jit(solution)/shard_map/all_gather | solution.py:459
  45.9 16.4 %all-gather.35.cloned.1.call-done = bf16[2048,384]{1,0:T(8,128)(2,1)} async-done(((bf16[256,384]{1,0:T(8,128)(2,1)}), bf16[2048,384]{1,0:T(8,128)(2,1)}) %all-gather.35.cloned.1.call-update) | async-done | bytes 1572880 | tf_op jit(solution)/shard_map/all_gather | solution.py:459
  62.4 16.3 %all-gather.4 = bf16[2048,128]{1,0:T(8,128)(2,1)} all-gather(bf16[256,128]{1,0:T(8,128)(2,1)S(1)} %copy-done.5), channel_id=6, replica_groups=mesh['dp'=4,'fsdp'=8] {'fsdp'}, dimensions={0}, use_global_device_ids=true | all-gather | bytes 589824 | tf_op jit(solution)/shard_map/all_gather | solution.py:459
  78.8 14.5 %all-gather.37.cloned.1.call-done = bf16[2048,512]{1,0:T(8,128)(2,1)} async-done(((bf16[256,512]{1,0:T(8,128)(2,1)}), bf16[2048,512]{1,0:T(8,128)(2,1)}) %all-gather.37.cloned.1.call-update) | async-done | bytes 2097168 | tf_op jit(solution)/shard_map/all_gather | solution.py:459
  93.4 30.2 %all-gather.39.cloned.1.call-done = bf16[8192,128]{1,0:T(8,128)(2,1)} async-done(((bf16[1024,128]{1,0:T(8,128)(2,1)}), bf16[8192,128]{1,0:T(8,128)(2,1)}) %all-gather.39.cloned.1.call-update) | async-done | bytes 2097168 | tf_op jit(solution)/shard_map/all_gather | solution.py:459
  129.6 30.6 %all-gather.21.cloned.1.call-done = bf16[8,1024,128]{2,1,0:T(8,128)(2,1)} async-done(((bf16[8,256,128]{2,1,0:T(8,128)(2,1)}), bf16[8,1024,128]{2,1,0:T(8,128)(2,1)}) %all-gather.21.cloned.1.call-update) | async-done | bytes 2097168 | tf_op jit(solution)/shard_map/all_gather | solution.py:460
  160.1 37.0 %all-gather.23.cloned.1.call-done = bf16[8,1024,128]{2,1,0:T(8,128)(2,1)} async-done(((bf16[8,256,128]{2,1,0:T(8,128)(2,1)}), bf16[8,1024,128]{2,1,0:T(8,128)(2,1)}) %all-gather.23.cloned.1.call-update) | async-done | bytes 2097168 | tf_op jit(solution)/shard_map/all_gather | solution.py:460
  201.9 49.9 %all-gather.19.cloned.1.call-done.w_ref = bf16[8,2048,128]{2,1,0:T(8,128)(2,1)} async-done(((bf16[8,512,128]{2,1,0:T(8,128)(2,1)}), bf16[8,2048,128]{2,1,0:T(8,128)(2,1)}) %all-gather.19.cloned.1.call-update) | async-done | bytes 4194320 | tf_op jit(solution)/shard_map/all_gather | solution.py:460
  251.8 14.3 %front.1 = (f32[1024,1024]{1,0:T(8,128)}, bf16[1024,1024]{1,0:T(8,128)(2,1)}, f32[8,1024]{1,0:T(8,128)}, f32[8,1024]{1,0:T(8,128)}) custom-call(bf16[1024,1024]{1,0:T(8,128)(2,1)} %x_ref.3, bf16[1024,1024]{1,0:T(8,128)(2,1)} %s_ref.3, bf16[8,2048,128]{2,1,0:T(8,128)(2,1)} %all-gather.19.cloned.1.call-done.w_ref, bf16[8,1024]{1,0:T(8,128)(2,1)} %pad.4.time_ref, ...), custom_call_target="tpu_custom_call" | custom-call | tf_op jit(solution)/shard_map/front/pallas_call | solution.py:92
  266.0 57.8 %all-gather.25.cloned.1.call-done.qa.qb.ka.kb.va.vb = bf16[8,1024,384]{2,1,0:T(8,128)(2,1)} async-done(((bf16[8,256,384]{2,1,0:T(8,128)(2,1)}), bf16[8,1024,384]{2,1,0:T(8,128)(2,1)}) %all-gather.25.cloned.1.call-update) | async-done | bytes 6291472 | tf_op jit(solution)/shard_map/all_gather | solution.py:460
  323.8 38.4 %attend.1 = (bf16[1024,1024]{1,0:T(8,128)(2,1)}, bf16[1024,1024]{1,0:T(8,128)(2,1)}, bf16[1024,1024]{1,0:T(8,128)(2,1)}, bf16[1024,1024]{1,0:T(8,128)(2,1)}, f32[32,1024]{1,0:T(8,128)}) custom-call(bf16[1024,1024]{1,0:T(8,128)(2,1)} %get-tuple-element.34.n_ref, bf16[8,1024,384]{2,1,0:T(8,128)(2,1)} %all-gather.25.cloned.1.call-done.qa.qb.ka.kb.va.vb, ...), custom_call_target="tpu_custom_call" | custom-call | tf_op jit(solution)/shard_map/attend/pallas_call | solution.py:173
  362.2 88.1 %all-gather.29.cloned.1.call-done.up_ref = bf16[8,1024,512]{2,1,0:T(8,128)(2,1)} async-done(((bf16[8,256,512]{2,1,0:T(8,128)(2,1)}), bf16[8,1024,512]{2,1,0:T(8,128)(2,1)}) %all-gather.29.cloned.1.call-update) | async-done | bytes 8388624 | tf_op jit(solution)/shard_map/all_gather | solution.py:460
  450.3 89.5 %all-gather.31.cloned.1.call-done.down_ref = bf16[8,4096,128]{2,1,0:T(8,128)(2,1)} async-done(((bf16[8,1024,128]{2,1,0:T(8,128)(2,1)}), bf16[8,4096,128]{2,1,0:T(8,128)(2,1)}) %all-gather.31.cloned.1.call-update) | async-done | bytes 8388624 | tf_op jit(solution)/shard_map/all_gather | solution.py:460
  539.8 84.2 %mlp.1 = (bf16[1024,1024]{1,0:T(8,128)(2,1)}, bf16[8,4096,128]{2,1,0:T(8,128)(2,1)}, bf16[8,1024,512]{2,1,0:T(8,128)(2,1)}, bf16[8,1024,128]{2,1,0:T(8,128)(2,1)...) custom-call(f32[1024,1024]{1,0:T(8,128)} %get-tuple-element.33.stream0_ref.s0_ref, ...), custom_call_target="tpu_custom_call" | custom-call | tf_op jit(solution)/shard_map/mlp/pallas_call | solution.py:270
  627.0 73.1 %attend_back.1 = (bf16[3,8,1024,128]{3,2,1,0:T(8,128)(2,1)}, bf16[1024,1024]{1,0:T(8,128)(2,1)}, f32[8,1024]{1,0:T(8,128)}) custom-call(bf16[1024,1024]{1,0:T(8,128)(2,1)} %get-tuple-element.34.n_ref, bf16[8,1024,384]{2,1,0:T(8,128)(2,1)} %all-gather.25.cloned.1.call-done.qa.qb.ka.kb.va.vb, ...), custom_call_target="tpu_custom_call" | custom-call | tf_op jit(solution)/shard_map/attend_back/pallas_call | solution.py:379
  705.8 18.3 %skip_back.1 = (bf16[8,2048,128]{2,1,0:T(8,128)(2,1)}, f32[1024,1024]{1,0:T(8,128)}, f32[1024,1024]{1,0:T(8,128)}) custom-call(bf16[1024,1024]{1,0:T(8,128)(2,1)} %x_ref.3, bf16[1024,1024]{1,0:T(8,128)(2,1)} %s_ref.3, bf16[1024,1024]{1,0:T(8,128)(2,1)} %get-tuple-element.45.d_ref, bf16[8,2048,128]{2,1,0:T(8,128)(2,1)} %all-gather.19.cloned.1.call-done.w_ref), custom_call_target="tpu_custom_call" | custom-call | tf_op jit(solution)/shard_map/skip_back/pallas_call | solution.py:436
  730.7 8.7 copy.56
  739.4 11.5 copy.59
  751.0 11.6 copy.60
  764.1 11.5 reduce-scatter.27.cloned.1.call-done
  775.6 50.8 %reduce-scatter.17.cloned.1.call-done = bf16[2048,128]{0,1:T(8,128)(2,1)} async-done(((bf16[2048,1024]{0,1:T(8,128)(2,1)}), bf16[2048,128]{0,1:T(8,128)(2,1)}) %reduce-scatter.17.cloned.1.call-update) | async-done | bytes 524304 | tf_op jit(solution)/shard_map/reduce_scatter | solution.py:471
  826.5 70.1 %reduce-scatter.43.cloned.1.call-done = bf16[384,1024]{1,0:T(8,128)(2,1)} async-done(((bf16[3072,1024]{1,0:T(8,128)(2,1)}), bf16[384,1024]{1,0:T(8,128)(2,1)}) %reduce-scatter.43.cloned.1.call-update) | async-done | bytes 786448
  898.9 87.8 %reduce-scatter.35.cloned.1.call-done = bf16[1024,512]{0,1:T(8,128)(2,1)} async-done(((bf16[1024,4096]{0,1:T(8,128)(2,1)}), bf16[1024,512]{0,1:T(8,128)(2,1)}) %reduce-scatter.35.cloned.1.call-update) | async-done | bytes 1048592 | tf_op jit(solution)/shard_map/reduce_scatter | solution.py:471
  986.8 90.1 %reduce-scatter.39.cloned.1.call-done = bf16[4096,128]{0,1:T(8,128)(2,1)} async-done(((bf16[4096,1024]{0,1:T(8,128)(2,1)}), bf16[4096,128]{0,1:T(8,128)(2,1)}) %reduce-scatter.39.cloned.1.call-update) | async-done | bytes 1048592 | tf_op jit(solution)/shard_map/reduce_scatter | solution.py:471
  1086.7 15.4 %reduce-scatter.33.cloned.1.call-done = bf16[256,128]{0,1:T(8,128)(2,1)} async-done(((bf16[1024,128]{0,1:T(8,128)(2,1)}), bf16[256,128]{0,1:T(8,128)(2,1)}) %reduce-scatter.33.cloned.1.call-update) | async-done | bytes 65552 | tf_op jit(solution)/shard_map/reduce_scatter | solution.py:472
  1103.7 25.3 %reduce-scatter.23.cloned.1.call-done = bf16[256,128]{0,1:T(8,128)(2,1)} async-done(((bf16[1024,128]{0,1:T(8,128)(2,1)}), bf16[256,128]{0,1:T(8,128)(2,1)}) %reduce-scatter.23.cloned.1.call-update) | async-done | bytes 65552 | tf_op jit(solution)/shard_map/reduce_scatter | solution.py:472
  1130.6 25.3 %reduce-scatter.29.cloned.1.call-done = bf16[256,128]{0,1:T(8,128)(2,1)} async-done(((bf16[1024,128]{0,1:T(8,128)(2,1)}), bf16[256,128]{0,1:T(8,128)(2,1)}) %reduce-scatter.29.cloned.1.call-update) | async-done | bytes 65552 | tf_op jit(solution)/shard_map/reduce_scatter | solution.py:472
  1157.5 26.3 %reduce-scatter.19.cloned.1.call-done = bf16[512,128]{0,1:T(8,128)(2,1)} async-done(((bf16[2048,128]{0,1:T(8,128)(2,1)}), bf16[512,128]{0,1:T(8,128)(2,1)}) %reduce-scatter.19.cloned.1.call-update) | async-done | bytes 131088 | tf_op jit(solution)/shard_map/reduce_scatter | solution.py:472
  1185.5 27.3 %reduce-scatter.25.cloned.1.call-done = bf16[256,384]{1,0:T(8,128)(2,1)} async-done(((bf16[1024,384]{1,0:T(8,128)(2,1)}), bf16[256,384]{1,0:T(8,128)(2,1)}) %reduce-scatter.25.cloned.1.call-update) | async-done | bytes 196624 | tf_op jit(solution)/shard_map/reduce_scatter | solution.py:472
  1214.5 28.8 %reduce-scatter.37.cloned.1.call-done = bf16[256,512]{0,1:T(8,128)(2,1)} async-done(((bf16[1024,512]{0,1:T(8,128)(2,1)}), bf16[256,512]{0,1:T(8,128)(2,1)}) %reduce-scatter.37.cloned.1.call-update) | async-done | bytes 262160 | tf_op jit(solution)/shard_map/reduce_scatter | solution.py:472
  1245.2 29.0 %reduce-scatter.41.cloned.1.call-done = bf16[1024,128]{0,1:T(8,128)(2,1)} async-done(((bf16[4096,128]{0,1:T(8,128)(2,1)}), bf16[1024,128]{0,1:T(8,128)(2,1)}) %reduce-scatter.41.cloned.1.call-update) | async-done | bytes 262160 | tf_op jit(solution)/shard_map/reduce_scatter | solution.py:472
  (94 shorter events, 55.4 us)
Async XLA Ops:
  7.2 38.0 %all-gather.33.cloned.1.call-start = ((), (), s32[]{:S(2)}) async-start(), calls=%async_computation.34 | async-start | bytes 1179648 | tf_op jit(solution)/shard_map/all_gather | solution.py:459
  7.9 54.4 %all-gather.35.cloned.1.call-start = ((), (), s32[]{:S(2)}) async-start(), calls=%async_computation.35 | async-start | bytes 1769472 | tf_op jit(solution)/shard_map/all_gather | solution.py:459
  8.7 84.7 %all-gather.37.cloned.1.call-start = ((), (), s32[]{:S(2)}) async-start(), calls=%async_computation.36 | async-start | bytes 2359296 | tf_op jit(solution)/shard_map/all_gather | solution.py:459
  9.4 114.2 %all-gather.39.cloned.1.call-start = ((), (), s32[]{:S(2)}) async-start(), calls=%async_computation.37 | async-start | bytes 2359296 | tf_op jit(solution)/shard_map/all_gather | solution.py:459
  10.0 150.2 %all-gather.21.cloned.1.call-start = ((), (), s32[]{:S(2)}) async-start(), calls=%async_computation.15 | async-start | bytes 2621440 | tf_op jit(solution)/shard_map/all_gather | solution.py:460
  28.9 33.6 %copy-start.5 = (bf16[256,128]{1,0:T(8,128)(2,1)S(1)}, bf16[256,128]{1,0:T(8,128)(2,1)}, u32[]{:S(2)}) copy-start(bf16[256,128]{1,0:T(8,128)(2,1)} %param.23) | copy-start | bytes 196612
  28.9 168.3 %all-gather.23.cloned.1.call-start = ((), (), s32[]{:S(2)}) async-start(), calls=%async_computation.16 | async-start | bytes 2621440 | tf_op jit(solution)/shard_map/all_gather | solution.py:460
  45.2 206.6 %all-gather.19.cloned.1.call-start = ((), (), s32[]{:S(2)}) async-start(), calls=%async_computation.14 | async-start | bytes 5242880 | tf_op jit(solution)/shard_map/all_gather | solution.py:460
  45.9 277.9 %all-gather.25.cloned.1.call-start = ((), (), s32[]{:S(2)}) async-start(), calls=%async_computation.17 | async-start | bytes 7864320 | tf_op jit(solution)/shard_map/all_gather | solution.py:460
  62.4 299.8 %all-gather.27.cloned.1.call-start = ((), (), s32[]{:S(2)}) async-start(), calls=%async_computation.18 | async-start | bytes 2621440 | tf_op jit(solution)/shard_map/all_gather | solution.py:460
  78.7 371.6 %all-gather.29.cloned.1.call-start = ((), (), s32[]{:S(2)}) async-start(), calls=%async_computation.19 | async-start | bytes 10485760 | tf_op jit(solution)/shard_map/all_gather | solution.py:460
  93.3 30.3 %copy-start.7 = (s32[1,1024]{1,0:T(1,128)S(1)}, s32[1,1024]{1,0:T(1,128)}, u32[]{:S(2)}) copy-start(s32[1,1024]{1,0:T(1,128)} %param.18) | copy-start | bytes 12292
  93.3 30.4 %copy-start.4 = (s32[1,1024]{1,0:T(1,128)S(1)}, s32[1,1024]{1,0:T(1,128)}, u32[]{:S(2)}) copy-start(s32[1,1024]{1,0:T(1,128)} %row_ref.5) | copy-start | bytes 12292
  93.3 31.4 %copy-start.6 = (s32[1,1024]{1,0:T(1,128)S(1)}, s32[1,1024]{1,0:T(1,128)}, u32[]{:S(2)}) copy-start(s32[1,1024]{1,0:T(1,128)} %param.19) | copy-start | bytes 12292
  93.4 32.4 %copy-start.3 = (bf16[1,4,1024]{2,1,0:T(4,128)(2,1)S(1)}, bf16[1,4,1024]{2,1,0:T(4,128)(2,1)}, u32[]{:S(2)}) copy-start(bf16[1,4,1024]{2,1,0:T(4,128)(2,1)} %param.16) | copy-start | bytes 24580
  93.4 446.5 %all-gather.31.cloned.1.call-start = ((), (), s32[]{:S(2)}) async-start(), calls=%async_computation.20 | async-start | bytes 10485760 | tf_op jit(solution)/shard_map/all_gather | solution.py:460
  123.6 639.1 %reduce-scatter.31.cloned.1.call-start = ((), (), s32[]{:S(2)}) async-start(), calls=%async_computation.28 | async-start | bytes 2359296 | tf_op jit(solution)/shard_map/reduce_scatter | solution.py:471
  627.0 136.6 %reduce-scatter.21.cloned.1.call-start = ((), (), s32[]{:S(2)}) async-start(), calls=%async_computation.23 | async-start | bytes 2359296 | tf_op jit(solution)/shard_map/reduce_scatter | solution.py:471
  700.1 3.1 copy-start
  703.1 72.5 %reduce-scatter.27.cloned.1.call-start = ((), (), s32[]{:S(2)}) async-start(), calls=%async_computation.26 | async-start | bytes 2359296 | tf_op jit(solution)/shard_map/reduce_scatter | solution.py:471
  705.8 120.7 %reduce-scatter.17.cloned.1.call-start = ((), (), s32[]{:S(2)}) async-start(), calls=%async_computation.21 | async-start | bytes 4718592 | tf_op jit(solution)/shard_map/reduce_scatter | solution.py:471
  730.6 165.9 %reduce-scatter.43.cloned.1.call-start = ((), (), s32[]{:S(2)}) async-start(), calls=%async_computation.38 | async-start | bytes 7077888
  739.4 247.3 %reduce-scatter.35.cloned.1.call-start = ((), (), s32[]{:S(2)}) async-start(), calls=%async_computation.30 | async-start | bytes 9437184 | tf_op jit(solution)/shard_map/reduce_scatter | solution.py:471
  751.0 325.9 %reduce-scatter.39.cloned.1.call-start = ((), (), s32[]{:S(2)}) async-start(), calls=%async_computation.32 | async-start | bytes 9437184 | tf_op jit(solution)/shard_map/reduce_scatter | solution.py:471
  762.7 339.4 %reduce-scatter.33.cloned.1.call-start = ((), (), s32[]{:S(2)}) async-start(), calls=%async_computation.29 | async-start | bytes 327680 | tf_op jit(solution)/shard_map/reduce_scatter | solution.py:472
  763.4 365.6 %reduce-scatter.23.cloned.1.call-start = ((), (), s32[]{:S(2)}) async-start(), calls=%async_computation.24 | async-start | bytes 327680 | tf_op jit(solution)/shard_map/reduce_scatter | solution.py:472
  764.0 391.9 %reduce-scatter.29.cloned.1.call-start = ((), (), s32[]{:S(2)}) async-start(), calls=%async_computation.27 | async-start | bytes 327680 | tf_op jit(solution)/shard_map/reduce_scatter | solution.py:472
  775.6 408.2 %reduce-scatter.19.cloned.1.call-start = ((), (), s32[]{:S(2)}) async-start(), calls=%async_computation.22 | async-start | bytes 655360 | tf_op jit(solution)/shard_map/reduce_scatter | solution.py:472
  826.5 386.4 %reduce-scatter.25.cloned.1.call-start = ((), (), s32[]{:S(2)}) async-start(), calls=%async_computation.25 | async-start | bytes 983040 | tf_op jit(solution)/shard_map/reduce_scatter | solution.py:472
  898.9 344.4 %reduce-scatter.37.cloned.1.call-start = ((), (), s32[]{:S(2)}) async-start(), calls=%async_computation.31 | async-start | bytes 1310720 | tf_op jit(solution)/shard_map/reduce_scatter | solution.py:472
  986.8 287.4 %reduce-scatter.41.cloned.1.call-start = ((), (), s32[]{:S(2)}) async-start(), calls=%async_computation.33 | async-start | bytes 1310720 | tf_op jit(solution)/shard_map/reduce_scatter | solution.py:472
  1079.8 3.9 copy-start.2
  (1 other events, 2.0 us)
Sparse Core Ops, SparseCore 0:
  9.6 26.5 all-gather.32
  37.8 24.4 all-gather.34
  64.0 29.3 all-gather.36
  94.8 28.7 all-gather.38
  125.3 34.7 all-gather.20
  161.8 35.2 all-gather.22
  199.0 52.6 all-gather.18
  253.6 70.1 all-gather.24
  325.6 35.3 all-gather.26
  362.7 87.5 all-gather.28
  452.2 87.5 all-gather.30
  627.1 35.7 reduce-scatter.30
  703.2 35.6 reduce-scatter.20
  741.1 34.4 reduce-scatter.26
  777.7 48.6 reduce-scatter.16
  828.6 67.9 reduce-scatter.42
  898.7 87.9 reduce-scatter.34
  988.9 87.9 reduce-scatter.38
  1079.6 22.4 reduce-scatter.32
  1104.9 24.0 reduce-scatter.22
  1131.8 24.0 reduce-scatter.28
  1159.0 24.7 reduce-scatter.18
  1186.7 26.0 reduce-scatter.24
  1215.6 27.6 reduce-scatter.36
  1246.4 27.7 reduce-scatter.40

commit v2 on v1

--- a/solution.py
+++ b/solution.py
@@ -455,6 +455,264 @@
     return cosine, jnp.where(early, -sine, 0.0), jnp.where(early, 0.0, sine)
 
 
+class Place:
+    def __init__(self):
+        dp, fs = lax.axis_index("dp"), lax.axis_index("fsdp")
+        self.y, self.x, self.z, self.c = dp // 2, dp % 2, fs // 2, fs % 2
+        self.dp, self.fs = dp, fs
+
+    def across_x(self):
+        return (self.y * 2 + 1 - self.x, self.fs)
+
+    def across_y(self):
+        return ((1 - self.y) * 2 + self.x, self.fs)
+
+    def sibling(self):
+        return (self.dp, self.z * 2 + 1 - self.c)
+
+    def along_z(self, hop):
+        return (self.dp, ((self.z + hop) % 4) * 2 + self.c)
+
+    def greet(self):
+        barrier = pltpu.get_barrier_semaphore()
+        peers = [self.across_x(), self.across_y(), self.sibling()]
+        peers += [self.along_z(hop) for hop in (1, 2, 3)]
+        for peer in peers:
+            pl.semaphore_signal(barrier, inc=1, device_id=peer, device_id_type=pl.DeviceIdType.MESH)
+        pl.semaphore_wait(barrier, len(peers))
+
+
+def remote(src, dst, send, recv, peer):
+    return pltpu.make_async_remote_copy(
+        src_ref=src, dst_ref=dst, send_sem=send, recv_sem=recv,
+        device_id=peer, device_id_type=pl.DeviceIdType.MESH,
+    )
+
+
+class Lazy:
+    def __init__(self, plan, send, recv):
+        self.plan, self.send, self.recv = plan, send, recv
+
+    def __len__(self):
+        return len(self.plan)
+
+    def __getitem__(self, i):
+        if isinstance(i, slice):
+            return [self[k] for k in range(*i.indices(len(self)))]
+        if i >= len(self.plan):
+            raise IndexError
+        src, dst, peer = self.plan[i]
+        return remote(src, dst, self.send.at[i], self.recv.at[i], peer)
+
+
+class Gather:
+    slots = 8
+    stages = 5
+
+    def __init__(self, place, shard, full, first, count, flip, send, recv, local):
+        self.me, self.shard, self.full = place, shard, full
+        self.rows = pl.ds(first, count)
+        self.flip, self.send, self.recv, self.local = flip, send, recv, local
+
+    def copies(self):
+        me, full, rows = self.me, self.full, self.rows
+        own = self.shard.at[rows, :]
+        spot = full.at[me.z, me.c, me.y, me.x, rows, :]
+        line = full.at[:, me.c, me.y, me.x, rows, :]
+        if self.flip:
+            pair = full.at[:, me.c, :, me.x, rows, :]
+            near, far = me.across_y(), me.across_x()
+            got = full.at[:, me.c, 1 - me.y, me.x, rows, :]
+            late = full.at[:, me.c, :, 1 - me.x, rows, :]
+        else:
+            pair = full.at[:, me.c, me.y, :, rows, :]
+            near, far = me.across_x(), me.across_y()
+            got = full.at[:, me.c, me.y, 1 - me.x, rows, :]
+            late = full.at[:, me.c, 1 - me.y, :, rows, :]
+        sib = me.sibling()
+        plan = [(own, spot, me.along_z(hop)) for hop in (1, 2, 3)]
+        plan += [(line, line, near), (pair, pair, far), (line, line, sib), (got, got, sib), (late, late, sib)]
+        return Lazy(plan, self.send, self.recv), (own, spot, self.local)
+
+    def stage(self, number):
+        made, keep = self.copies()
+        if number == 0:
+            pltpu.make_async_copy(*keep).start()
+            for copy in made[:3]:
+                copy.start()
+        elif number == 1:
+            pltpu.make_async_copy(*keep).wait()
+            for copy in made[:3]:
+                copy.wait_recv()
+            made[3].start()
+            made[5].start()
+        elif number == 2:
+            made[3].wait_recv()
+            made[4].start()
+            made[6].start()
+        elif number == 3:
+            made[4].wait_recv()
+            made[7].start()
+        else:
+            for copy in made[5:]:
+                copy.wait_recv()
+            for copy in made:
+                copy.wait_send()
+
+
+class Reduce:
+    slots = 6
+    stages = 5
+
+    def __init__(self, place, grad, out, first, count, flip, send, recv, local, own, half, quarter, parts):
+        self.me, self.grad, self.out = place, grad, out
+        self.rows = pl.ds(first, count)
+        self.flip, self.send, self.recv, self.local = flip, send, recv, local
+        self.own, self.other = own
+        self.half, self.quarter, self.parts = half, quarter, parts
+
+    @staticmethod
+    def scratch(count, per):
+        return [
+            pltpu.VMEM((2, 4, 2, 2, count, per), BF),
+            pltpu.VMEM((4, 2, count, per), BF),
+            pltpu.VMEM((4, count, per), BF),
+            pltpu.VMEM((3, count, per), BF),
+        ]
+
+    def copies(self):
+        me, rows = self.me, self.rows
+        theirs = self.grad.at[:, 1 - me.c, :, :, rows, :]
+        mine = self.grad.at[:, me.c, :, :, rows, :]
+        if self.flip:
+            give, near = self.own.at[:, :, 1 - me.x], me.across_x()
+            give2, far = self.half.at[:, 1 - me.y], me.across_y()
+        else:
+            give, near = self.own.at[:, 1 - me.y], me.across_y()
+            give2, far = self.half.at[:, 1 - me.x], me.across_x()
+        plan = [(theirs, self.other, me.sibling()), (give, self.half, near), (give2, self.quarter, far)]
+        plan += [
+            (self.quarter.at[(me.z + hop) % 4], self.parts.at[hop - 1], me.along_z(hop)) for hop in (1, 2, 3)
+        ]
+        return Lazy(plan, self.send, self.recv), (mine, self.own, self.local)
+
+    def stage(self, number):
+        me = self.me
+        made, load = self.copies()
+        if number == 0:
+            made[0].start()
+            pltpu.make_async_copy(*load).start()
+        elif number == 1:
+            pltpu.make_async_copy(*load).wait()
+            made[0].wait_recv()
+            self.own[...] = self.own[...] + self.other[...]
+            made[1].start()
+        elif number == 2:
+            made[1].wait_recv()
+            if self.flip:
+                self.half[...] = self.half[...] + self.own[:, :, me.x]
+            else:
+                self.half[...] = self.half[...] + self.own[:, me.y]
+            made[2].start()
+        elif number == 3:
+            made[2].wait_recv()
+            kept = me.y if self.flip else me.x
+            self.quarter[...] = self.quarter[...] + self.half[:, kept]
+            for copy in made[3:]:
+                copy.start()
+        else:
+            for copy in made[3:]:
+                copy.wait_recv()
+            total = self.quarter[me.z].astype(F32)
+            for i in range(3):
+                total = total + self.parts[i].astype(F32)
+            self.out[self.rows, :] = total
+            for copy in made:
+                copy.wait_send()
+
+
+def run_ticks(pieces, tick):
+    for i in range(len(pieces)):
+        stage = tick - i // 2
+        if 0 <= stage < pieces[i].stages:
+            pieces[i].stage(stage)
+
+
+def ticks_of(count):
+    return (count + 1) // 2 + 4
+
+
+ANY = pl.BlockSpec(memory_space=pl.ANY)
+PIECE = 1 << 19
+
+
+def cut(shapes):
+    made = []
+    for which, (tall, per) in enumerate(shapes):
+        count = 4 if tall * per * 32 >= 4 * PIECE else 2
+        for i in range(count):
+            made.append((which, i * tall // count, tall // count, i % 2 == 1))
+    return made
+
+
+def gather_body(plan, count, *refs):
+    shard, full, (send, recv, local) = refs[:count], refs[count : 2 * count], refs[2 * count :]
+    me = Place()
+    me.greet()
+    pieces = [
+        Gather(me, shard[w], full[w], first, rows, flip, send.at[i], recv.at[i], local.at[i])
+        for i, (w, first, rows, flip) in enumerate(plan)
+    ]
+    for tick in range(ticks_of(len(pieces))):
+        run_ticks(pieces, tick)
+
+
+def gather_all(*weights):
+    plan = cut([w.shape for w in weights])
+    sems = [pltpu.SemaphoreType.DMA((len(plan), 8))] * 2 + [pltpu.SemaphoreType.DMA((len(plan),))]
+    full = pl.pallas_call(
+        functools.partial(gather_body, plan, len(weights)),
+        in_specs=[ANY] * len(weights),
+        out_specs=(ANY,) * len(weights),
+        out_shape=tuple(shaped((4, 2, 2, 2) + w.shape, BF) for w in weights),
+        scratch_shapes=sems,
+        compiler_params=params(collective_id=0, has_side_effects=True),
+        name="gather_all",
+    )(*weights)
+    return [f.reshape(NB, 4 * w.shape[0], w.shape[1]) for f, w in zip(full, weights)]
+
+
+def reduce_body(plan, count, *refs):
+    grad, out, (send, recv, local) = refs[:count], refs[count : 2 * count], refs[2 * count : 2 * count + 3]
+    room = refs[2 * count + 3 :]
+    me = Place()
+    me.greet()
+    pieces = [
+        Reduce(
+            me, grad[w], out[w], first, rows, flip, send.at[i], recv.at[i], local.at[i],
+            (room[4 * i].at[0], room[4 * i].at[1]), *room[4 * i + 1 : 4 * i + 4],
+        )
+        for i, (w, first, rows, flip) in enumerate(plan)
+    ]
+    for tick in range(ticks_of(len(pieces))):
+        run_ticks(pieces, tick)
+
+
+def reduce_all(*grads):
+    tops = [(g.shape[1] // 4, g.shape[2]) for g in grads]
+    plan = cut(tops)
+    sems = [pltpu.SemaphoreType.DMA((len(plan), 6))] * 2 + [pltpu.SemaphoreType.DMA((len(plan),))]
+    room = [buffer for w, _, rows, _ in plan for buffer in Reduce.scratch(rows, tops[w][1])]
+    return pl.pallas_call(
+        functools.partial(reduce_body, plan, len(grads)),
+        in_specs=[ANY] * len(grads),
+        out_shape=tuple(shaped(top, F32) for top in tops),
+        scratch_shapes=sems + room,
+        compiler_params=params(collective_id=1, has_side_effects=True),
+        name="reduce_all",
+    )(*[g.reshape((4, 2, 2, 2) + top) for g, top in zip(grads, tops)])
+
+
 def gathered(shard):
     blocks = lax.all_gather(shard, "fsdp", axis=0, tiled=False)
     blocks = lax.all_gather(blocks, "dp", axis=1, tiled=True)
@@ -473,7 +731,7 @@
 
 
 def shards(
-    inputs, skip_in, time_emb, seg_ids, positions, pad_mask,
+    fast, inputs, skip_in, time_emb, seg_ids, positions, pad_mask,
     w_skip, w_ada1, w_qkv, w_out, w_ada2, w_up, w_down, cotangent,
 ):
     slots = time_emb.shape[1]
@@ -482,10 +740,13 @@
     tables = rotary(positions)
     flat_time = time_emb.reshape(slots, -1)
     time8 = jnp.pad(flat_time, ((0, 8 - slots), (0, 0)))
-    f_skip, f_qkv, f_out = gathered(w_skip), gathered(w_qkv), gathered(w_out)
-    f_up, f_down = gathered(w_up), gathered(w_down)
-    f_ada1, f_ada2 = gathered(w_ada1), gathered(w_ada2)
-    ada = jnp.concatenate([f_ada1, f_ada2], axis=2)
+    if fast:
+        w_ada = jnp.concatenate([w_ada1, w_ada2], axis=1)
+        f_skip, ada, f_qkv, f_out, f_up, f_down = gather_all(w_skip, w_ada, w_qkv, w_out, w_up, w_down)
+    else:
+        f_skip, f_qkv, f_out = gathered(w_skip), gathered(w_qkv), gathered(w_out)
+        f_up, f_down = gathered(w_up), gathered(w_down)
+        ada = jnp.concatenate([gathered(w_ada1), gathered(w_ada2)], axis=2)
     stream0, normed1, gamma1, gamma2 = front(inputs, skip_in, f_skip, time8, ada, seg_col)
     q, k, v, ctx, lse = attend(normed1, f_qkv, tables, seg_col, pad_col, seg_row)
     output, g_down, g_up, g_out, d_stream1, d_ctx, d_gamma2 = mlp(
@@ -501,25 +762,36 @@
     ).reshape(NB, width, 3 * width // NB)
     g_skip, d_input, d_skip = skip_back(inputs, skip_in, d_low, f_skip)
     d_gammas = [d[:slots].astype(BF) for d in (d_gamma1, d_gamma2)]
+    per = width // NB
     d_time = 0.0
+    for d_gamma, part in zip(d_gammas, (ada[:, :, :per], ada[:, :, per:])):
+        flat = jnp.transpose(part, (1, 0, 2)).reshape(width, width)
+        d_time = d_time + jnp.einsum("ne,de->nd", d_gamma, flat, preferred_element_type=F32)
+    axes = ("dp", "fsdp")
+    all_time = lax.all_gather(flat_time, axes, axis=0, tiled=True)
+    tall, thin = w_ada1.shape
+    all_time = lax.dynamic_slice_in_dim(all_time, lax.axis_index("dp") * tall, tall, 1)
+    all_gamma = lax.all_gather(jnp.concatenate(d_gammas, axis=1), axes, axis=0, tiled=True)
     g_ada = []
-    for d_gamma, full in zip(d_gammas, (f_ada1, f_ada2)):
-        flat = jnp.transpose(full, (1, 0, 2)).reshape(width, width)
-        d_time = d_time + jnp.einsum("ne,de->nd", d_gamma, flat, preferred_element_type=F32)
-        g = jnp.einsum("nd,ne->de", flat_time, d_gamma, preferred_element_type=F32).astype(BF)
-        g_ada.append(jnp.transpose(g.reshape(width, NB, width // NB), (1, 0, 2)))
+    for i in range(2):
+        mine = lax.dynamic_slice_in_dim(all_gamma, i * width + lax.axis_index("fsdp") * thin, thin, 1)
+        g_ada.append(jnp.einsum("nd,ne->de", all_time, mine, preferred_element_type=F32))
+    if fast:
+        s_down, s_up, s_out, s_qkv, s_skip = reduce_all(g_down, g_up, g_out, g_qkv, g_skip)
+    else:
+        s_down, s_up, s_out, s_qkv, s_skip = [scattered(g) for g in (g_down, g_up, g_out, g_qkv, g_skip)]
     return (
         output,
         d_input,
         d_skip,
         d_time.reshape(time_emb.shape),
-        scattered(g_skip),
-        scattered(g_ada[0]),
-        scattered(g_qkv),
-        scattered(g_out),
-        scattered(g_ada[1]),
-        scattered(g_up),
-        scattered(g_down),
+        s_skip,
+        g_ada[0],
+        s_qkv,
+        s_out,
+        g_ada[1],
+        s_up,
+        s_down,
     )
 
 
@@ -527,8 +799,9 @@
     rows = P(("dp", "fsdp"), None)
     cube = P(("dp", "fsdp"), None, None)
     tile = P("dp", "fsdp")
+    fast = mesh.shape["dp"] == 4 and mesh.shape["fsdp"] == NB
     return jax.shard_map(
-        shards,
+        functools.partial(shards, fast),
         mesh=mesh,
         in_specs=(rows, rows, cube) + (rows,) * 3 + (tile,) * 7 + (rows,),
         out_specs=(rows, rows, rows, cube) + (tile,) * 7,

time: 1290 us -> 683 us (0.53)
  waiting for transfers between devices: 906 us -> 0 us
  Pallas kernels: 228 us -> 534 us
  blocking collectives: 51.3 us -> 79.5 us
  between operations: 14.5 us -> 1.02 us
    reduce_scatter x13 -> x0, waiting for transfers between devices: 418 us -> none  [the longest x6 240 us: scattered(): part = lax.psum_scatter(flat, 'fsdp', scatter_dimension=1, tiled=True)]
    all_gather x11 -> x0, waiting for transfers between devices: 414 us -> none  [the longest x7 353 us: gathered(): blocks = lax.all_gather(blocks, 'dp', axis=1, tiled=True)]
    pallas_call x0 -> x2, Pallas kernels: none -> 306 us  [the longest x1 164 us: gather_all(): pl.pallas_call(functools.partial(gather_body, plan, len(weights)), in_spe...]
    unnamed x26 -> x0, waiting for transfers between devices: 74.8 us -> none
    transpose x6 -> x3, local copies, waits for them, and re-layouts: 39.1 us -> 10.3 us  [shards(): flat = jnp.transpose(part, (1, 0, 2)).reshape(width, width)]
    all_gather x3 -> x2, blocking collectives: 51.3 us -> 79.5 us  [the longest x1 40.6 us: shards(): lax.all_gather(jnp.concatenate(d_gammas, axis=1), axes, axis=0, tiled=True)]
    another operation x0 -> x2, local copies, waits for them, and re-layouts: none -> 27.4 us  [reduce_all(): g.reshape((4, 2, 2, 2) + top)]
  transfers between devices with their start and end apart: 25 -> 0, of which waited for: 21 -> 0; matrix products, arithmetic and copies ran while one was open for 6% -> 0% of each run, Pallas kernels for 11% -> 0%
where the time goes in v2:
time: 683 us; the launch traced here: 677 us
  Pallas kernels  534 us (78%)
  blocking collectives  79.5 us (12%)
  local copies, waits for them, and re-layouts  55.3 us (8%)
    pallas_call x1, Pallas kernels, gather_all(): pl.pallas_call(functools.partial(gather_body, plan, len(weights)), in_spe...  164 us
    pallas_call x1, Pallas kernels, reduce_all(): pl.pallas_call(functools.partial(reduce_body, plan, len(grads)), in_specs...  142 us
    pallas_call x1, Pallas kernels, mlp(): pl.pallas_call(mlp_body, grid=(NB,), in_specs=[full, full, whole((NB, wid...  83.7 us
    pallas_call x1, Pallas kernels, attend_back(): pl.pallas_call(attend_back_body, grid=(groups,), in_specs=[full] + units...  73 us
    all_gather x1, blocking collectives, shards(): lax.all_gather(jnp.concatenate(d_gammas, axis=1), axes, axis=0, tiled=True)  40.6 us
    all_gather x1, blocking collectives, shards(): all_time = lax.all_gather(flat_time, axes, axis=0, tiled=True)  38.9 us
    pallas_call x1, Pallas kernels, attend(): pl.pallas_call(attend_body, grid=(groups,), in_specs=[whole((length, widt...  38.1 us
    another operation x2, local copies, waits for them, and re-layouts, reduce_all(): g.reshape((4, 2, 2, 2) + top)  27.4 us

profile of v2, /device:TPU:0, one launch (start us, length us, event | category | flops | bytes accessed | tf_op | source)
XLA Modules:
  0.0 677.4 jit_solution(7006364931746861208)
XLA Ops:
  0.6 1.5 pad_maximum_fusion.refs_1_
  2.2 164.2 %gather_all.1 = (bf16[4,2,2,2,512,128]{5,4,3,2,1,0:T(8,128)(2,1)}, bf16[4,2,2,2,256,256]{5,4,3,2,1,0:T(8,128)(2,1)}, bf16[4,2,2,2,256,384]{5,4,3,2,1,0:T(8,128)(...) custom-call(bf16[512,128]{1,0:T(8,128)(2,1)} %refs_0_.1, ...), custom_call_target="tpu_custom_call" | custom-call | tf_op jit(solution)/shard_map/gather_all/pallas_call | solution.py:673
  166.4 1.7 copy.47.seg_ref
  168.1 1.3 pad.4.time_ref
  169.4 14.8 %front.1 = (f32[1024,1024]{1,0:T(8,128)}, bf16[1024,1024]{1,0:T(8,128)(2,1)}, f32[8,1024]{1,0:T(8,128)}, f32[8,1024]{1,0:T(8,128)}) custom-call(bf16[1024,1024]{1,0:T(8,128)(2,1)} %x_ref.3, bf16[1024,1024]{1,0:T(8,128)(2,1)} %s_ref.3, bf16[8,2048,128]{2,1,0:T(8,128)(2,1)} %bitcast.51, bf16[8,1024]{1,0:T(8,128)(2,1)} %pad.4.time_ref, ...), custom_call_target="tpu_custom_call" | custom-call | tf_op jit(solution)/shard_map/front/pallas_call | solution.py:92
  184.3 3.2 fusion.1
  187.5 1.1 copy.49.pad_ref
  188.6 38.1 %attend.1 = (bf16[1024,1024]{1,0:T(8,128)(2,1)}, bf16[1024,1024]{1,0:T(8,128)(2,1)}, bf16[1024,1024]{1,0:T(8,128)(2,1)}, bf16[1024,1024]{1,0:T(8,128)(2,1)}, f32[32,1024]{1,0:T(8,128)}) custom-call(bf16[1024,1024]{1,0:T(8,128)(2,1)} %get-tuple-element.47.n_ref, bf16[8,1024,384]{2,1,0:T(8,128)(2,1)} %bitcast.36, bf16[8,1024,384]{2,1,0:T(8,128)(2,1)} %bitcast.37, ...), custom_call_target="tpu_custom_call" | custom-call | tf_op jit(solution)/shard_map/attend/pallas_call | solution.py:173
  226.6 83.7 %mlp.1 = (bf16[1024,1024]{1,0:T(8,128)(2,1)}, bf16[8,4096,128]{2,1,0:T(8,128)(2,1)}, bf16[8,1024,512]{2,1,0:T(8,128)(2,1)}, bf16[8,1024,128]{2,1,0:T(8,128)(2,1)...) custom-call(f32[1024,1024]{1,0:T(8,128)} %get-tuple-element.46.stream0_ref.s0_ref, ...), custom_call_target="tpu_custom_call" | custom-call | tf_op jit(solution)/shard_map/mlp/pallas_call | solution.py:270
  310.4 73.0 %attend_back.1 = (bf16[3,8,1024,128]{3,2,1,0:T(8,128)(2,1)}, bf16[1024,1024]{1,0:T(8,128)(2,1)}, f32[8,1024]{1,0:T(8,128)}) custom-call(bf16[1024,1024]{1,0:T(8,128)(2,1)} %get-tuple-element.47.n_ref, bf16[8,1024,384]{2,1,0:T(8,128)(2,1)} %bitcast.42, bf16[8,1024,384]{2,1,0:T(8,128)(2,1)} %bitcast.43, bf16[8,1024,384]{2,1,0:T(8,128)(2,1)} %bitcast.44, ...), custom_call_target="tpu_custom_call" | custom-call | tf_op jit(solution)/shard_map/attend_back/pallas_call | solution.py:379
  383.5 0.8 slice.27
  384.3 40.6 %all-gather.1 = bf16[32,4,2048]{2,1,0:T(4,128)(2,1)S(1)} all-gather(bf16[1,4,2048]{2,1,0:T(4,128)(2,1)S(1)} %maximum_bitcast_fusion), channel_id=1, replica_groups=mesh['dp'=4,'fsdp'=8] {'dp','fsdp'}, dimensions={0}, use_global_device_ids=true | all-gather | bytes 540672 | tf_op jit(solution)/shard_map/all_gather | solution.py:774
  424.8 0.1 reshape.124
  425.0 38.9 %all-gather = bf16[1,128,1024]{2,0,1:T(2,128)(2,1)S(1)} all-gather(bf16[1,4,1024]{2,0,1:T(2,128)(2,1)S(1)} %copy.57), channel_id=2, replica_groups=mesh['dp'=4,'fsdp'=8] {'dp','fsdp'}, dimensions={1}, use_global_device_ids=true | all-gather | bytes 270336 | tf_op jit(solution)/shard_map/all_gather | solution.py:771
  463.9 0.1 constant_dynamic-slice_fusion
  464.0 0.9 fusion.4
  464.9 0.9 fusion.6
  465.8 8.6 %copy.55 = bf16[8,3,1024,128]{2,3,1,0:T(8,128)(2,1)} copy(bf16[8,3,1024,128]{3,2,1,0:T(8,128)(2,1)} %bitcast.59) | data formatting | bytes 12582912 | tf_op jit(solution)/shard_map/reshape | solution.py:761
  474.4 11.1 %reshape_reshape.3 = bf16[4,2,2,2,256,384]{4,3,2,5,1,0:T(2,128)(2,1)} reshape(bf16[8,1024,3,128]{1,3,2,0:T(8,128)(2,1)} %bitcast.48) | data formatting | bytes 12582912 | tf_op jit(solution)/shard_map/reshape;reshape | solution.py:713
  485.5 16.3 %copy.56.refs_3_ = bf16[4,2,2,2,256,384]{5,4,3,2,1,0:T(8,128)(2,1)} copy(bf16[4,2,2,2,256,384]{4,3,2,5,1,0:T(2,128)(2,1)} %reshape_reshape.3) | data formatting | bytes 12582912 | tf_op jit(solution)/shard_map/reshape;reshape | solution.py:713
  501.8 18.1 %skip_back.1 = (bf16[8,2048,128]{2,1,0:T(8,128)(2,1)}, f32[1024,1024]{1,0:T(8,128)}, f32[1024,1024]{1,0:T(8,128)}) custom-call(bf16[1024,1024]{1,0:T(8,128)(2,1)} %x_ref.3, bf16[1024,1024]{1,0:T(8,128)(2,1)} %s_ref.3, bf16[1024,1024]{1,0:T(8,128)(2,1)} %get-tuple-element.62.d_ref, bf16[8,2048,128]{2,1,0:T(8,128)(2,1)} %bitcast.52), custom_call_target="tpu_custom_call" | custom-call | tf_op jit(solution)/shard_map/skip_back/pallas_call | solution.py:436
  519.9 141.8 %reduce_all.1 = (f32[1024,128]{1,0:T(8,128)}, f32[256,512]{1,0:T(8,128)}, f32[256,128]{1,0:T(8,128)}, f32[256,384]{1,0:T(8,128)}, f32[512,128]{1,0:T(8,128)}) custom-call(bf16[4,2,2,2,1024,128]{5,4,3,2,1,0:T(8,128)(2,1)} %bitcast.53, bf16[4,2,2,2,256,512]{5,4,3,2,1,0:T(8,128)(2,1)} %bitcast.54, bf16[4,2,2,2,256,128]{5,4,3,2,1,0:T(8,128)(2,1)} %bitcast.61, ...), custom_call_target="tpu_custom_call" | custom-call | tf_op jit(solution)/shard_map/reduce_all/pallas_call | solution.py:706
  661.8 4.6 slice_bitcast_fusion
  666.3 2.9 copy.53
  669.2 0.4 fusion.14
  669.6 2.9 copy.54
  672.5 1.0 fusion
  673.5 0.7 copy.68
  674.2 0.7 copy.69
  675.0 0.7 copy.70
  675.6 0.8 copy.71
  676.4 0.8 copy.72
  (26 shorter events, 0.1 us)
Async XLA Ops:
  169.4 14.8 %copy-start.9 = (s32[1,1024]{1,0:T(1,128)S(1)}, s32[1,1024]{1,0:T(1,128)}, u32[]{:S(2)}) copy-start(s32[1,1024]{1,0:T(1,128)} %param.18) | copy-start | bytes 12292
  169.4 18.1 %copy-start.8 = (s32[1,1024]{1,0:T(1,128)S(1)}, s32[1,1024]{1,0:T(1,128)}, u32[]{:S(2)}) copy-start(s32[1,1024]{1,0:T(1,128)} %param.19) | copy-start | bytes 12292
  310.4 73.8 %copy-start.5 = (f32[8,1024]{1,0:T(8,128)S(1)}, f32[8,1024]{1,0:T(8,128)}, u32[]{:S(2)}) copy-start(f32[8,1024]{1,0:T(8,128)} %get-tuple-element.66) | copy-start | bytes 98308
  310.4 114.6 %copy-start.7 = (bf16[1,4,1024]{2,1,0:T(4,128)(2,1)S(1)}, bf16[1,4,1024]{2,1,0:T(4,128)(2,1)}, u32[]{:S(2)}) copy-start(bf16[1,4,1024]{2,1,0:T(4,128)(2,1)} %param.16) | copy-start | bytes 24580
  666.3 2.9 copy-start.6
  672.5 1.0 copy-start.3
  672.5 1.7 copy-start.2
  672.5 2.5 copy-start.4
  672.5 3.1 copy-start.1
  672.5 3.9 copy-start

commit v3 on v2

--- a/solution.py
+++ b/solution.py
@@ -29,7 +29,11 @@
 
 
 def whole(shape):
-    return pl.BlockSpec(shape, lambda *_: (0,) * len(shape))
+    return pl.BlockSpec(shape, lambda *_: (0,) * len(shape), pipeline_mode=pl.Buffered(1))
+
+
+ANY = pl.BlockSpec(memory_space=pl.ANY)
+UNIT = 128
 
 
 def shaped(shape, kind):
@@ -68,7 +72,35 @@
     return (stream * inverse * (1.0 + gain)).astype(BF)
 
 
-def front_body(x_ref, s_ref, w_ref, time_ref, ada_ref, seg_ref, stream_ref, normed_ref, g1_ref, g2_ref):
+def fill_bias(bias_ref, seg_ref, pad_ref, row_ref):
+    length = seg_ref.shape[0]
+    for t in range(length // 128):
+        rows = slice(t * 128, (t + 1) * 128)
+        keys = lax.broadcasted_iota(jnp.int32, (128, length), 0) + t * 128
+        queries = lax.broadcasted_iota(jnp.int32, (128, length), 1)
+        allowed = (seg_ref[rows, :] == row_ref[0:1, :]) & (
+            (pad_ref[rows, :] > 0) | (keys == queries)
+        )
+        bias_ref[rows, :] = jnp.where(allowed, 0.0, MASKED)
+
+
+def turn(unit, cosine, before, after):
+    return (
+        unit * cosine
+        + pltpu.roll(unit, 96, 1) * before
+        + pltpu.roll(unit, 32, 1) * after
+    )
+
+
+def unit_spec(rows, base):
+    def index(j):
+        unit = base + 2 * j
+        return (unit // 3, 0, unit % 3)
+
+    return pl.BlockSpec((1, rows, 128), index)
+
+
+def plain_front_body(x_ref, s_ref, w_ref, time_ref, ada_ref, seg_ref, stream_ref, normed_ref, g1_ref, g2_ref):
     length, width = x_ref.shape
     per = ada_ref.shape[2] // 2
     for f in range(NB):
@@ -87,10 +119,10 @@
         normed_ref[rows, :] = norm(stream_ref[rows, :], gain)
 
 
-def front(inputs, skip_in, w_skip, time8, ada, seg_col):
+def plain_front(inputs, skip_in, w_skip, time8, ada, seg_col):
     length, width = inputs.shape
     return pl.pallas_call(
-        front_body,
+        plain_front_body,
         out_shape=(
             shaped((length, width), F32),
             shaped((length, width), BF),
@@ -102,34 +134,7 @@
     )(inputs, skip_in, w_skip, time8, ada, seg_col)
 
 
-def key_bias(seg_col, pad_col, seg_row, length):
-    keys = lax.broadcasted_iota(jnp.int32, (length, length), 0)
-    queries = lax.broadcasted_iota(jnp.int32, (length, length), 1)
-    allowed = (seg_col == seg_row) & ((pad_col > 0) | (keys == queries))
-    return jnp.where(allowed, 0.0, MASKED)
-
-
-def fill_bias(bias_ref, seg_ref, pad_ref, row_ref):
-    length = seg_ref.shape[0]
-    for t in range(length // 128):
-        rows = slice(t * 128, (t + 1) * 128)
-        keys = lax.broadcasted_iota(jnp.int32, (128, length), 0) + t * 128
-        queries = lax.broadcasted_iota(jnp.int32, (128, length), 1)
-        allowed = (seg_ref[rows, :] == row_ref[0:1, :]) & (
-            (pad_ref[rows, :] > 0) | (keys == queries)
-        )
-        bias_ref[rows, :] = jnp.where(allowed, 0.0, MASKED)
-
-
-def turn(unit, cosine, before, after):
-    return (
-        unit * cosine
-        + pltpu.roll(unit, 96, 1) * before
-        + pltpu.roll(unit, 32, 1) * after
-    )
-
-
-def attend_body(
+def plain_attend_body(
     n_ref, qa, qb, ka, kb, va, vb, cos_ref, lo_ref, hi_ref, seg_ref, pad_ref, row_ref,
     q_ref, k_ref, v_ref, c_ref, lse_ref, bias_ref,
 ):
@@ -156,22 +161,14 @@
         lse_ref[head : head + 1, :] = largest + jnp.log(total)
 
 
-def unit_spec(rows, base):
-    def index(j):
-        unit = base + 2 * j
-        return (unit // 3, 0, unit % 3)
-
-    return pl.BlockSpec((1, rows, 128), index)
-
-
-def attend(normed, w_qkv, tables, seg_col, pad_col, seg_row):
+def plain_attend(normed, w_qkv, tables, seg_col, pad_col, seg_row):
     length, width = normed.shape
     groups = width // 256
     units = [unit_spec(width, part * (width // 128) + e) for part in range(3) for e in range(2)]
     column = pl.BlockSpec((length, 256), lambda j: (0, j))
     wide = shaped((length, width), BF)
     return pl.pallas_call(
-        attend_body,
+        plain_attend_body,
         grid=(groups,),
         in_specs=[whole((length, width))]
         + units
@@ -186,7 +183,7 @@
     )(normed, *([w_qkv] * 6), *tables, seg_col, pad_col, seg_row)
 
 
-def mlp_body(
+def plain_mlp_body(
     stream0_ref, ctx_ref, wout_ref, g2_ref, seg_ref, row_ref, up_ref, down_ref, cot_ref,
     out_ref, gdown_ref, gup_ref, gout_ref, ds1_ref, dctx_ref, dg2_ref,
     s1_ref, n2_ref, acc_ref, dn_ref,
@@ -261,14 +258,14 @@
         dctx_ref[...] = acc_ref[...].astype(BF)
 
 
-def mlp(stream0, ctx, w_out, gamma2, seg_col, seg_row, w_up, w_down, cotangent):
+def plain_mlp(stream0, ctx, w_out, gamma2, seg_col, seg_row, w_up, w_down, cotangent):
     length, width = ctx.shape
     hidden = w_down.shape[1]
     piece = hidden // NB
     per = width // NB
     full = whole((length, width))
     return pl.pallas_call(
-        mlp_body,
+        plain_mlp_body,
         grid=(NB,),
         in_specs=[
             full,
@@ -310,7 +307,7 @@
     )(stream0, ctx, w_out, gamma2, seg_col, seg_row, w_up, w_down, cotangent)
 
 
-def attend_back_body(
+def plain_attend_back_body(
     n_ref, qa, qb, ka, kb, va, vb, cos_ref, lo_ref, hi_ref, seg_ref, pad_ref, row_ref,
     q_ref, k_ref, v_ref, g_ref, c_ref, lse_ref, s0_ref, g1_ref, ds1_ref,
     gw_ref, dlow_ref, dg1_ref, bias_ref, dn_ref, dq_ref, dk_ref, dv_ref,
@@ -368,7 +365,7 @@
             dg1_ref[...] += segment_sum(row_ref[:, rows], d_gain)
 
 
-def attend_back(
+def plain_attend_back(
     normed, w_qkv, tables, seg_col, pad_col, seg_row, q, k, v, d_ctx, ctx, lse, stream0, gamma1, d_stream1
 ):
     length, width = normed.shape
@@ -377,7 +374,7 @@
     column = pl.BlockSpec((length, 256), lambda j: (0, j))
     full = whole((length, width))
     return pl.pallas_call(
-        attend_back_body,
+        plain_attend_back_body,
         grid=(groups,),
         in_specs=[full]
         + units
@@ -406,7 +403,7 @@
     )
 
 
-def skip_back_body(x_ref, s_ref, d_ref, w_ref, gw_ref, dx_ref, ds_ref):
+def plain_skip_back_body(x_ref, s_ref, d_ref, w_ref, gw_ref, dx_ref, ds_ref):
     low = d_ref[...]
     per = 256
     width = x_ref.shape[1]
@@ -431,10 +428,10 @@
         ds_ref[:, rows] = dot(low, columns(w_ref, 0, NB, rest), NT)
 
 
-def skip_back(inputs, skip_in, d_low, w_skip):
+def plain_skip_back(inputs, skip_in, d_low, w_skip):
     length, width = inputs.shape
     return pl.pallas_call(
-        skip_back_body,
+        plain_skip_back_body,
         out_shape=(
             shaped(w_skip.shape, BF),
             shaped((length, width), F32),
@@ -445,16 +442,6 @@
     )(inputs, skip_in, d_low, w_skip)
 
 
-def rotary(positions):
-    half = HD // 2
-    lane = jnp.arange(128)
-    frequency = 10000.0 ** (-2.0 * (lane % half).astype(F32) / HD)
-    phase = positions.reshape(-1, 1).astype(F32) * frequency[None, :]
-    cosine, sine = jnp.cos(phase), jnp.sin(phase)
-    early = (lane % HD < half)[None, :]
-    return cosine, jnp.where(early, -sine, 0.0), jnp.where(early, 0.0, sine)
-
-
 class Place:
     def __init__(self):
         dp, fs = lax.axis_index("dp"), lax.axis_index("fsdp")
@@ -505,18 +492,21 @@
         return remote(src, dst, self.send.at[i], self.recv.at[i], peer)
 
 
+def flow(*copy):
+    return pltpu.make_async_copy(*copy)
+
+
 class Gather:
-    slots = 8
-    stages = 5
-
-    def __init__(self, place, shard, full, first, count, flip, send, recv, local):
-        self.me, self.shard, self.full = place, shard, full
-        self.rows = pl.ds(first, count)
-        self.flip, self.send, self.recv, self.local = flip, send, recv, local
+    sems = 8
+
+    def __init__(self, place, source, full, rows, flip):
+        self.me, self.source, self.full, self.rows, self.flip = place, source, full, rows, flip
+
+    def bind(self, send, recv, local):
+        self.send, self.recv, self.local = send, recv, local
 
     def copies(self):
         me, full, rows = self.me, self.full, self.rows
-        own = self.shard.at[rows, :]
         spot = full.at[me.z, me.c, me.y, me.x, rows, :]
         line = full.at[:, me.c, me.y, me.x, rows, :]
         if self.flip:
@@ -530,18 +520,18 @@
             got = full.at[:, me.c, me.y, 1 - me.x, rows, :]
             late = full.at[:, me.c, 1 - me.y, :, rows, :]
         sib = me.sibling()
-        plan = [(own, spot, me.along_z(hop)) for hop in (1, 2, 3)]
+        plan = [(self.source, spot, me.along_z(hop)) for hop in (1, 2, 3)]
         plan += [(line, line, near), (pair, pair, far), (line, line, sib), (got, got, sib), (late, late, sib)]
-        return Lazy(plan, self.send, self.recv), (own, spot, self.local)
+        return Lazy(plan, self.send, self.recv), (self.source, spot, self.local)
 
     def stage(self, number):
         made, keep = self.copies()
         if number == 0:
-            pltpu.make_async_copy(*keep).start()
+            flow(*keep).start()
             for copy in made[:3]:
                 copy.start()
         elif number == 1:
-            pltpu.make_async_copy(*keep).wait()
+            flow(*keep).wait()
             for copy in made[:3]:
                 copy.wait_recv()
             made[3].start()
@@ -556,54 +546,54 @@
         else:
             for copy in made[5:]:
                 copy.wait_recv()
-            for copy in made:
+            for copy in made[:]:
                 copy.wait_send()
 
 
 class Reduce:
-    slots = 6
-    stages = 5
-
-    def __init__(self, place, grad, out, first, count, flip, send, recv, local, own, half, quarter, parts):
-        self.me, self.grad, self.out = place, grad, out
-        self.rows = pl.ds(first, count)
-        self.flip, self.send, self.recv, self.local = flip, send, recv, local
-        self.own, self.other = own
-        self.half, self.quarter, self.parts = half, quarter, parts
+    sems = 6
+
+    def __init__(self, place, theirs, mine, own, room, out, flip, load):
+        self.me, self.theirs, self.mine, self.own = place, theirs, mine, own
+        self.other, self.half, self.quarter, self.parts = room
+        self.out, self.flip, self.load = out, flip, load
 
     @staticmethod
-    def scratch(count, per):
+    def room(count, per):
         return [
-            pltpu.VMEM((2, 4, 2, 2, count, per), BF),
+            pltpu.VMEM((4, 2, 2, count, per), BF),
             pltpu.VMEM((4, 2, count, per), BF),
             pltpu.VMEM((4, count, per), BF),
             pltpu.VMEM((3, count, per), BF),
         ]
 
+    def bind(self, send, recv, local):
+        self.send, self.recv, self.local = send, recv, local
+
     def copies(self):
-        me, rows = self.me, self.rows
-        theirs = self.grad.at[:, 1 - me.c, :, :, rows, :]
-        mine = self.grad.at[:, me.c, :, :, rows, :]
+        me = self.me
         if self.flip:
             give, near = self.own.at[:, :, 1 - me.x], me.across_x()
             give2, far = self.half.at[:, 1 - me.y], me.across_y()
         else:
             give, near = self.own.at[:, 1 - me.y], me.across_y()
             give2, far = self.half.at[:, 1 - me.x], me.across_x()
-        plan = [(theirs, self.other, me.sibling()), (give, self.half, near), (give2, self.quarter, far)]
+        plan = [(self.theirs, self.other, me.sibling()), (give, self.half, near), (give2, self.quarter, far)]
         plan += [
             (self.quarter.at[(me.z + hop) % 4], self.parts.at[hop - 1], me.along_z(hop)) for hop in (1, 2, 3)
         ]
-        return Lazy(plan, self.send, self.recv), (mine, self.own, self.local)
+        return Lazy(plan, self.send, self.recv), (self.mine, self.own, self.local)
 
     def stage(self, number):
         me = self.me
         made, load = self.copies()
         if number == 0:
             made[0].start()
-            pltpu.make_async_copy(*load).start()
+            if self.load:
+                flow(*load).start()
         elif number == 1:
-            pltpu.make_async_copy(*load).wait()
+            if self.load:
+                flow(*load).wait()
             made[0].wait_recv()
             self.own[...] = self.own[...] + self.other[...]
             made[1].start()
@@ -615,6 +605,8 @@
                 self.half[...] = self.half[...] + self.own[:, me.y]
             made[2].start()
         elif number == 3:
+            made[0].wait_send()
+            made[1].wait_send()
             made[2].wait_recv()
             kept = me.y if self.flip else me.x
             self.quarter[...] = self.quarter[...] + self.half[:, kept]
@@ -626,91 +618,670 @@
             total = self.quarter[me.z].astype(F32)
             for i in range(3):
                 total = total + self.parts[i].astype(F32)
-            self.out[self.rows, :] = total
-            for copy in made:
+            self.out[...] = total
+            for copy in made[2:]:
                 copy.wait_send()
 
 
-def run_ticks(pieces, tick):
-    for i in range(len(pieces)):
-        stage = tick - i // 2
-        if 0 <= stage < pieces[i].stages:
-            pieces[i].stage(stage)
-
-
-def ticks_of(count):
-    return (count + 1) // 2 + 4
-
-
-ANY = pl.BlockSpec(memory_space=pl.ANY)
-PIECE = 1 << 19
-
-
-def cut(shapes):
-    made = []
-    for which, (tall, per) in enumerate(shapes):
-        count = 4 if tall * per * 32 >= 4 * PIECE else 2
-        for i in range(count):
-            made.append((which, i * tall // count, tall // count, i % 2 == 1))
-    return made
-
-
-def gather_body(plan, count, *refs):
-    shard, full, (send, recv, local) = refs[:count], refs[count : 2 * count], refs[2 * count :]
+class Traffic:
+    def __init__(self):
+        self.todo, self.pieces = {}, []
+
+    def add(self, first, *pieces, gap=1):
+        self.pieces += pieces
+        for piece in pieces:
+            for stage in range(5):
+                self.todo.setdefault(first + stage * gap, []).append((stage, piece))
+
+    def bind(self, send, recv, local):
+        for i, piece in enumerate(self.pieces):
+            piece.bind(send.at[i], recv.at[i], local.at[i])
+
+    def at(self, hook):
+        for stage, piece in sorted(self.todo.pop(hook, []), key=lambda item: -item[0]):
+            piece.stage(stage)
+
+    def fire(self, step, steps, per, hook):
+        for s in range(steps):
+            if s * per + hook in self.todo:
+                pl.when(step == s)(functools.partial(self.at, s * per + hook))
+
+    def drain(self):
+        for hook in sorted(self.todo):
+            self.at(hook)
+
+
+def semaphores(count, kind):
+    return [pltpu.SemaphoreType.DMA((count, kind))] * 2 + [pltpu.SemaphoreType.DMA((count,))]
+
+
+def full_of(rows, per):
+    return shaped((4, 2, 2, 2, rows, per), BF)
+
+
+def halves(rows):
+    return [(pl.ds(e * (rows // 2), rows // 2), e == 1) for e in range(2)]
+
+
+def up_pair(me, shard, full, q):
+    lanes = pl.ds(q * UNIT, UNIT)
+    return [Gather(me, shard.at[rows, lanes], full, rows, flip) for rows, flip in halves(shard.shape[0])]
+
+
+def down_pair(me, shard, full, q):
+    tall = shard.shape[0] // 2
+    step = tall // 4
+    return [
+        Gather(me, shard.at[pl.ds(e * tall + q * step, step), :], full, pl.ds(e * step, step), e == 1)
+        for e in range(2)
+    ]
+
+
+def row_pairs(me, shard, full, count):
+    tall = shard.shape[0] // count
+    made = [
+        Gather(me, shard.at[pl.ds(i * tall, tall), :], full, pl.ds(i * tall, tall), i % 2 == 1)
+        for i in range(count)
+    ]
+    return [made[i : i + 2] for i in range(0, count, 2)]
+
+
+def front_body(
+    x_ref, s_ref, time_ref, seg_ref, skip_ref, ada_ref, qkv_ref,
+    stream_ref, normed_ref, g1_ref, g2_ref, fskip_ref, fada_ref, fqkv_ref,
+    w_ref, a_ref, w_sem, send, recv, local,
+):
+    length, width = x_ref.shape
+    per = ada_ref.shape[1] // 2
     me = Place()
     me.greet()
-    pieces = [
-        Gather(me, shard[w], full[w], first, rows, flip, send.at[i], recv.at[i], local.at[i])
-        for i, (w, first, rows, flip) in enumerate(plan)
+    traffic = Traffic()
+    plan = row_pairs(me, skip_ref, fskip_ref, 4) + row_pairs(me, ada_ref, fada_ref, 2)
+    need = len(plan) + 4
+    plan += row_pairs(me, qkv_ref, fqkv_ref, 4)
+    for i, pair in enumerate(plan):
+        traffic.add(i, *pair)
+    traffic.bind(send, recv, local)
+    for hook in range(need):
+        traffic.at(hook)
+    loads = [flow(fskip_ref, w_ref, w_sem.at[0]), flow(fada_ref, a_ref, w_sem.at[1])]
+    for load in loads:
+        load.start()
+    for load in loads:
+        load.wait()
+    for i in range(4):
+        tile = jnp.concatenate([w_ref[i, c].reshape(2 * width, UNIT) for c in range(2)], axis=1)
+        part = dot(x_ref[...], tile[:width]) + dot(s_ref[...], tile[width:])
+        stream_ref[:, i * 2 * UNIT : (i + 1) * 2 * UNIT] = part
+        if i % 2 == 1:
+            traffic.at(need + i // 2)
+    for f in range(NB):
+        both = dot(time_ref[...], a_ref[f // 2, f % 2].reshape(width, 2 * per))
+        g1_ref[:, f * per : (f + 1) * per] = both[:, :per]
+        g2_ref[:, f * per : (f + 1) * per] = both[:, per:]
+
+    @pl.loop(0, length // UNIT)
+    def _(t):
+        rows = pl.ds(pl.multiple_of(t * UNIT, UNIT), UNIT)
+        gain = token_gain(seg_ref[rows, :], g1_ref)
+        normed_ref[rows, :] = norm(stream_ref[rows, :], gain)
+
+    traffic.drain()
+
+
+def front(inputs, skip_in, time8, seg_col, w_skip, w_ada, w_qkv):
+    length, width = inputs.shape
+    fulls = [full_of(*w.shape) for w in (w_skip, w_ada, w_qkv)]
+    vmem = pl.BlockSpec(memory_space=pltpu.VMEM)
+    return pl.pallas_call(
+        front_body,
+        in_specs=[vmem] * 4 + [ANY] * 3,
+        out_specs=(vmem,) * 4 + (ANY,) * 3,
+        out_shape=(
+            shaped((length, width), F32),
+            shaped((length, width), BF),
+            shaped((8, width), F32),
+            shaped((8, width), F32),
+            *fulls,
+        ),
+        scratch_shapes=[pltpu.VMEM(f.shape, BF) for f in fulls[:2]]
+        + [pltpu.SemaphoreType.DMA((2,))]
+        + semaphores(10, Gather.sems),
+        compiler_params=params(collective_id=0, has_side_effects=True),
+        name="front",
+    )(inputs, skip_in, time8, seg_col, w_skip, w_ada, w_qkv)
+
+
+def attend_body(
+    n_ref, qa, qb, ka, kb, va, vb, cos_ref, lo_ref, hi_ref, seg_ref, pad_ref, row_ref, out_ref, up_ref, down_ref,
+    q_ref, k_ref, v_ref, c_ref, lse_ref, fout_ref, fup0_ref, fdn0_ref, fup1_ref,
+    bias_ref, send, recv, local,
+):
+    step = pl.program_id(0)
+    last = pl.num_programs(0) - 1
+    me = Place()
+    traffic = Traffic()
+    pairs = row_pairs(me, out_ref, fout_ref, 2) + [
+        up_pair(me, up_ref, fup0_ref, 0),
+        down_pair(me, down_ref, fdn0_ref, 0),
+        up_pair(me, up_ref, fup1_ref, 1),
     ]
-    for tick in range(ticks_of(len(pieces))):
-        run_ticks(pieces, tick)
-
-
-def gather_all(*weights):
-    plan = cut([w.shape for w in weights])
-    sems = [pltpu.SemaphoreType.DMA((len(plan), 8))] * 2 + [pltpu.SemaphoreType.DMA((len(plan),))]
-    full = pl.pallas_call(
-        functools.partial(gather_body, plan, len(weights)),
-        in_specs=[ANY] * len(weights),
-        out_specs=(ANY,) * len(weights),
-        out_shape=tuple(shaped((4, 2, 2, 2) + w.shape, BF) for w in weights),
-        scratch_shapes=sems,
-        compiler_params=params(collective_id=0, has_side_effects=True),
-        name="gather_all",
-    )(*weights)
-    return [f.reshape(NB, 4 * w.shape[0], w.shape[1]) for f, w in zip(full, weights)]
-
-
-def reduce_body(plan, count, *refs):
-    grad, out, (send, recv, local) = refs[:count], refs[count : 2 * count], refs[2 * count : 2 * count + 3]
-    room = refs[2 * count + 3 :]
+    for i, pair in enumerate(pairs):
+        traffic.add(2 * i, *pair, gap=2)
+    traffic.bind(send, recv, local)
+    fire = functools.partial(traffic.fire, step, 4, 4)
+
+    @pl.when(step == 0)
+    def _():
+        me.greet()
+        traffic.at(0)
+        fill_bias(bias_ref, seg_ref, pad_ref, row_ref)
+
+    normed = n_ref[...]
+    for out, first, second, scale in ((q_ref, qa, qb, HD**-0.5), (k_ref, ka, kb, 1.0)):
+        made = dot(normed, jnp.concatenate([first[0], second[0]], axis=1))
+        for half in range(2):
+            unit = made[:, half * 128 : (half + 1) * 128]
+            turned = turn(unit, cos_ref[...], lo_ref[...], hi_ref[...])
+            out[:, half * 128 : (half + 1) * 128] = (turned.astype(BF) * scale).astype(BF)
+    v_ref[...] = dot(normed, jnp.concatenate([va[0], vb[0]], axis=1)).astype(BF)
+    for head in range(4):
+        fire(head)
+        lanes = slice(head * HD, (head + 1) * HD)
+        scores = dot(k_ref[:, lanes], q_ref[:, lanes], NT) + bias_ref[...]
+        largest = jnp.max(scores, axis=0, keepdims=True)
+        exponent = jnp.exp(scores - largest)
+        total = jnp.sum(exponent, axis=0, keepdims=True)
+        mixed = dot(v_ref[:, lanes].T, exponent.astype(BF)) * (1.0 / total)
+        c_ref[:, lanes] = mixed.T.astype(BF)
+        lse_ref[head : head + 1, :] = largest + jnp.log(total)
+    pl.when(step == last)(traffic.drain)
+
+
+def attend(normed, w_qkv, tables, seg_col, pad_col, seg_row, w_out, w_up, w_down):
+    length, width = normed.shape
+    groups = width // 256
+    units = [unit_spec(width, part * (width // 128) + e) for part in range(3) for e in range(2)]
+    column = pl.BlockSpec((length, 256), lambda j: (0, j))
+    wide = shaped((length, width), BF)
+    quarter = full_of(w_up.shape[0], UNIT)
+    return pl.pallas_call(
+        attend_body,
+        grid=(groups,),
+        in_specs=[whole((length, width))]
+        + units
+        + [whole((length, 128))] * 3
+        + [whole((length, 1))] * 2
+        + [whole((1, length))]
+        + [ANY] * 3,
+        out_specs=(column,) * 4 + (pl.BlockSpec((8, length), lambda j: (j, 0)),) + (ANY,) * 4,
+        out_shape=(wide,) * 4
+        + (shaped((8 * groups, length), F32), full_of(*w_out.shape), quarter, quarter, quarter),
+        scratch_shapes=[pltpu.VMEM((length, length), F32)] + semaphores(8, Gather.sems),
+        compiler_params=params(collective_id=1, has_side_effects=True),
+        name="attend",
+    )(normed, *([w_qkv] * 6), *tables, seg_col, pad_col, seg_row, w_out, w_up, w_down)
+
+
+def mlp_body(
+    stream0_ref, ctx_ref, wout_ref, g2_ref, seg_ref, row_ref, cot_ref,
+    up_ref, down_ref, fup0, fdn0, fup1,
+    out_ref, gout_ref, ds1_ref, dctx_ref, dg2_ref, sup0, sdn0, sup1, sdn1, gup2, gdn2, gup3, gdn3,
+    fdn1, fup2, fdn2, fup3, fdn3,
+    s1_ref, n2_ref, acc_ref, dn_ref, up_tile, dn_tile, act_ref, pre_ref, stage_up, stage_dn,
+    sem, gsend, grecv, glocal, rsend, rrecv, rlocal, *room,
+):
+    step = pl.program_id(0)
+    steps = 8
+    length, width = ctx_ref.shape
+    tiles = length // UNIT
+    me = Place()
+    gather, reduce = Traffic(), Traffic()
+    gather.add(0, *down_pair(me, down_ref, fdn1, 1))
+    gather.add(2, *up_pair(me, up_ref, fup2, 2))
+    gather.add(4, *down_pair(me, down_ref, fdn2, 2))
+    gather.add(6, *up_pair(me, up_ref, fup3, 3))
+    gather.add(8, *down_pair(me, down_ref, fdn3, 3))
+    gather.bind(gsend, grecv, glocal)
+    count = 0
+    for q, (sup, sdn) in enumerate(((sup0, sdn0), (sup1, sdn1))):
+        made = []
+        for rows, flip in halves(2 * UNIT):
+            theirs = stage_up.at[q, 1 - me.c, :, :, :, rows, :]
+            mine = stage_up.at[q, me.c, :, :, :, rows, :]
+            made.append(Reduce(me, theirs, mine, mine, room[4 * count : 4 * count + 4], sup.at[rows, :], flip, False))
+            count += 1
+        for e in range(2):
+            theirs = stage_dn.at[q, e, :, 1 - me.c]
+            mine = stage_dn.at[q, e, :, me.c]
+            rows = pl.ds(e * UNIT, UNIT)
+            made.append(Reduce(me, theirs, mine, mine, room[4 * count : 4 * count + 4], sdn.at[rows, :], e == 1, False))
+            count += 1
+        reduce.add(4 + 4 * q, *made[2:])
+        reduce.add(5 + 4 * q, *made[:2])
+    reduce.bind(rsend, rrecv, rlocal)
+    ups, downs = (fup0, fup1, fup2, fup3), (fdn0, fdn1, fdn2, fdn3)
+    saves = {4: (gup2, gdn2), 6: (gup3, gdn3)}
+
+    def tile_loads(s):
+        q, e = s // 2, s % 2
+        return (
+            flow(ups[q].at[:, e], up_tile.at[s % 2], sem.at[0, s % 2]),
+            flow(downs[q].at[:, :, :, :, pl.ds(e * UNIT, UNIT), :], dn_tile.at[s % 2], sem.at[1, s % 2]),
+        )
+
+    def grad_saves(s):
+        q, e = s // 2, s % 2
+        gup, gdn = saves[2 * q]
+        return (
+            flow(stage_up.at[q % 2, e], gup.at[e], sem.at[2, s - 4]),
+            flow(stage_dn.at[q % 2, e], gdn.at[e], sem.at[3, s - 4]),
+        )
+
+    def hook(which):
+        gather.fire(step, steps, 2, which)
+        reduce.fire(step, steps, 2, which)
+
+    @pl.when(step == 0)
+    def _():
+        me.greet()
+        gather.at(0)
+        for load in tile_loads(0):
+            load.start()
+        first = flow(stream0_ref, s1_ref, sem.at[2, 0])
+        first.start()
+        first.wait()
+        for i in range(4):
+            lanes = slice(i * 2 * UNIT, (i + 1) * 2 * UNIT)
+            tile = jnp.concatenate([wout_ref[i, c].reshape(width, UNIT) for c in range(2)], axis=1)
+            s1_ref[:, lanes] += dot(ctx_ref[...], tile)
+
+        @pl.loop(0, tiles)
+        def _(t):
+            rows = pl.ds(pl.multiple_of(t * UNIT, UNIT), UNIT)
+            n2_ref[rows, :] = norm(s1_ref[rows, :], token_gain(seg_ref[rows, :], g2_ref))
+
+        acc_ref[...] = jnp.zeros_like(acc_ref)
+        dn_ref[...] = jnp.zeros_like(dn_ref)
+
+    hook(0)
+    for s in range(steps):
+
+        @pl.when(step == s)
+        def _(s=s):
+            if s in (2, 4, 6):
+                for load in tile_loads(s):
+                    load.start()
+            for load in tile_loads(s):
+                load.wait()
+            if s % 2 == 0:
+                for load in tile_loads(s + 1):
+                    load.start()
+
+    slot = step % 2
+    up = jnp.concatenate([up_tile[slot, z].reshape(width, UNIT) for z in range(4)], axis=1)
+    down = jnp.concatenate([dn_tile[slot, f // 2, f % 2].reshape(4 * UNIT, UNIT) for f in range(NB)], axis=1)
+    hidden = dot(n2_ref[...], up)
+    square = hidden * hidden
+    tanh = jnp.tanh(ROOT * hidden * (1.0 + CUBE * square))
+    active = (0.5 * hidden * (1.0 + tanh)).astype(BF)
+    act_ref[...] = active
+    slope = 0.5 * (1.0 + tanh) + 0.5 * hidden * (1.0 - tanh * tanh) * (
+        ROOT * (1.0 + 3.0 * CUBE * square)
+    )
+    d_pre = (dot(cot_ref[...], down, NT) * slope).astype(BF)
+    pre_ref[...] = d_pre
+    acc_ref[...] += dot(active, down)
+    dn_ref[...] += dot(d_pre, up, NT)
+    hook(1)
+    par = (step // 2) % 2
+    grad = dot(act_ref[...], cot_ref[...], TN).astype(BF)
+    for f in range(NB):
+        stage_dn[par, slot, f // 2, f % 2] = grad[:, f * UNIT : (f + 1) * UNIT].reshape(2, 2, UNIT, UNIT)
+    grad = dot(n2_ref[...], pre_ref[...], TN).astype(BF)
+    for z in range(4):
+        stage_up[par, slot, z] = grad[:, z * UNIT : (z + 1) * UNIT].reshape(2, 2, 2 * UNIT, UNIT)
+    for s in range(4, steps):
+
+        @pl.when(step == s)
+        def _(s=s):
+            for save in grad_saves(s):
+                save.start()
+
+    @pl.when(step == steps - 1)
+    def _():
+        dg2_ref[...] = jnp.zeros_like(dg2_ref)
+
+        @pl.loop(0, tiles)
+        def _(t):
+            rows = pl.ds(pl.multiple_of(t * UNIT, UNIT), UNIT)
+            stream = s1_ref[rows, :]
+            out_ref[rows, :] = (stream + acc_ref[rows, :]).astype(BF)
+            gain = token_gain(seg_ref[rows, :], g2_ref)
+            term, d_gain = norm_back(dn_ref[rows, :], stream, gain)
+            d_stream = cot_ref[rows, :].astype(F32) + term
+            s1_ref[rows, :] = d_stream
+            n2_ref[rows, :] = d_stream.astype(BF)
+            dg2_ref[...] += segment_sum(row_ref[:, rows], d_gain)
+
+        keep = flow(s1_ref, ds1_ref, sem.at[0, 0])
+        keep.start()
+        for i in range(4):
+            lanes = slice(i * 2 * UNIT, (i + 1) * 2 * UNIT)
+            part = dot(ctx_ref[...], n2_ref[:, lanes], TN).astype(BF)
+            for c in range(2):
+                gout_ref[i, c] = part[:, c * UNIT : (c + 1) * UNIT].reshape(2, 2, 2 * UNIT, UNIT)
+        for i in range(4):
+            lanes = slice(i * 2 * UNIT, (i + 1) * 2 * UNIT)
+            tile = jnp.concatenate([wout_ref[i, c].reshape(width, UNIT) for c in range(2)], axis=1)
+            part = dot(n2_ref[:, lanes], tile, NT)
+            acc_ref[...] = part if i == 0 else acc_ref[...] + part
+        dctx_ref[...] = acc_ref[...].astype(BF)
+        gather.drain()
+        reduce.drain()
+        for s in range(4, steps):
+            for save in grad_saves(s):
+                save.wait()
+        keep.wait()
+
+
+def mlp(stream0, ctx, w_out, gamma2, seg_col, seg_row, cotangent, s_up, s_down, fup0, fdn0, fup1):
+    length, width = ctx.shape
+    full = whole((length, width))
+    part = pl.BlockSpec((2 * UNIT, UNIT), lambda j: (0, 0))
+    quarter = full_of(2 * UNIT, UNIT)
+    grads = (shaped((2, 4, 2, 2, 2 * UNIT, UNIT), BF), shaped((2, 4, 2, 2, 2, UNIT, UNIT), BF))
+    pieces = 8
+    return pl.pallas_call(
+        mlp_body,
+        grid=(8,),
+        in_specs=[
+            ANY,
+            full,
+            whole(w_out.shape),
+            whole((8, width)),
+            whole((length, 1)),
+            whole((1, length)),
+            full,
+        ]
+        + [ANY] * 5,
+        out_specs=(full, whole(w_out.shape), ANY, full, whole((8, width))) + (part,) * 4 + (ANY,) * 9,
+        out_shape=(
+            shaped((length, width), BF),
+            shaped(w_out.shape, BF),
+            shaped((length, width), F32),
+            shaped((length, width), BF),
+            shaped((8, width), F32),
+        )
+        + (shaped((2 * UNIT, UNIT), F32),) * 4
+        + grads * 2
+        + (quarter,) * 5,
+        scratch_shapes=[
+            pltpu.VMEM((length, width), F32),
+            pltpu.VMEM((length, width), BF),
+            pltpu.VMEM((length, width), F32),
+            pltpu.VMEM((length, width), F32),
+            pltpu.VMEM((2, 4, 2, 2, 2 * UNIT, UNIT), BF),
+            pltpu.VMEM((2, 4, 2, 2, 2, UNIT, UNIT), BF),
+            pltpu.VMEM((length, 4 * UNIT), BF),
+            pltpu.VMEM((length, 4 * UNIT), BF),
+            pltpu.VMEM((2, 2, 4, 2, 2, 2 * UNIT, UNIT), BF),
+            pltpu.VMEM((2, 2, 4, 2, 2, 2, UNIT, UNIT), BF),
+            pltpu.SemaphoreType.DMA((4, 4)),
+        ]
+        + semaphores(10, Gather.sems)
+        + semaphores(pieces, Reduce.sems)
+        + Reduce.room(UNIT, UNIT) * pieces,
+        compiler_params=params(collective_id=2, has_side_effects=True),
+        name="mlp",
+    )(stream0, ctx, w_out, gamma2, seg_col, seg_row, cotangent, s_up, s_down, fup0, fdn0, fup1)
+
+
+def attend_back_body(
+    n_ref, qa, qb, ka, kb, va, vb, cos_ref, lo_ref, hi_ref, seg_ref, pad_ref, row_ref,
+    q_ref, k_ref, v_ref, g_ref, c_ref, lse_ref, g1_ref, s0_ref, ds1_ref, gup2, gdn2, gup3, gdn3, gout,
+    gw_ref, dlow_ref, dg1_ref, sup2, sdn2, sup3, sdn3, sout,
+    bias_ref, dn_ref, dq_ref, dk_ref, dv_ref, s0_buf, sem, send, recv, local, *room,
+):
+    step = pl.program_id(0)
+    last = pl.num_programs(0) - 1
+    length, width = n_ref.shape
+    me = Place()
+    traffic = Traffic()
+    count = 0
+    for q, (gup, gdn, sup, sdn) in enumerate(((gup2, gdn2, sup2, sdn2), (gup3, gdn3, sup3, sdn3))):
+        ups, downs = [], []
+        for e, (rows, flip) in enumerate(halves(2 * UNIT)):
+            own, *rest = room[5 * count : 5 * count + 5]
+            ups.append(
+                Reduce(
+                    me, gup.at[1 - me.c, :, :, :, rows, :], gup.at[me.c, :, :, :, rows, :], own, rest,
+                    sup.at[rows, :], flip, True,
+                )
+            )
+            count += 1
+            own, *rest = room[5 * count : 5 * count + 5]
+            downs.append(
+                Reduce(
+                    me, gdn.at[e, :, 1 - me.c], gdn.at[e, :, me.c], own, rest,
+                    sdn.at[pl.ds(e * UNIT, UNIT), :], flip, True,
+                )
+            )
+            count += 1
+        traffic.add(6 * q, *ups, gap=2)
+        traffic.add(6 * q + 3, *downs, gap=2)
+    outs = []
+    for rows, flip in halves(2 * UNIT):
+        own, *rest = room[5 * count : 5 * count + 5]
+        theirs, mine = gout.at[:, 1 - me.c, :, :, rows, :], gout.at[:, me.c, :, :, rows, :]
+        outs.append(Reduce(me, theirs, mine, own, rest, sout.at[rows, :], flip, True))
+        count += 1
+    traffic.add(11, *outs, gap=2)
+    traffic.bind(send, recv, local)
+    fire = functools.partial(traffic.fire, step, 4, 5)
+
+    @pl.when(step == 0)
+    def _():
+        me.greet()
+        traffic.at(0)
+        flow(s0_ref, s0_buf, sem.at[0]).start()
+        fill_bias(bias_ref, seg_ref, pad_ref, row_ref)
+        dn_ref[...] = jnp.zeros_like(dn_ref)
+
+    ones = jnp.ones((8, HD), BF)
+    for head in range(4):
+        fire(head)
+        lanes = slice(head * HD, (head + 1) * HD)
+        query, key, value = q_ref[:, lanes], k_ref[:, lanes], v_ref[:, lanes]
+        grad = g_ref[:, lanes]
+        both = grad.astype(F32) * c_ref[:, lanes].astype(F32)
+        high = both.astype(BF)
+        low = (both - high.astype(F32)).astype(BF)
+        delta = (dot(ones, high, NT) + dot(ones, low, NT))[0:1, :]
+        probs = jnp.exp(dot(key, query, NT) + bias_ref[...] - lse_ref[head : head + 1, :])
+        d_scores = (probs * (dot(value, grad, NT) - delta)).astype(BF)
+        dv_ref[:, lanes] = dot(probs.astype(BF), grad)
+        dk_ref[:, lanes] = dot(d_scores, query)
+        dq_ref[:, lanes] = dot(key.T, d_scores).T * HD**-0.5
+
+    @pl.when(step == last)
+    def _():
+        flow(ds1_ref, bias_ref, sem.at[1]).start()
+
+    fire(4)
+    for part, (src, first, second) in enumerate(
+        ((dq_ref, qa, qb), (dk_ref, ka, kb), (dv_ref, va, vb))
+    ):
+        if part < 2:
+            made = jnp.concatenate(
+                [
+                    turn(src[:, half * 128 : (half + 1) * 128], cos_ref[...], -lo_ref[...], -hi_ref[...])
+                    for half in range(2)
+                ],
+                axis=1,
+            ).astype(BF)
+        else:
+            made = src[...].astype(BF)
+        grad = dot(n_ref[...], made, TN).astype(BF)
+        gw_ref[part, 0] = grad[:, :128]
+        gw_ref[part, 1] = grad[:, 128:]
+        dn_ref[...] += dot(made, jnp.concatenate([first[0], second[0]], axis=1), NT)
+
+    @pl.when(step == last)
+    def _():
+        dg1_ref[...] = jnp.zeros_like(dg1_ref)
+        flow(s0_ref, s0_buf, sem.at[0]).wait()
+        flow(ds1_ref, bias_ref, sem.at[1]).wait()
+
+        @pl.loop(0, length // UNIT)
+        def _(t):
+            rows = pl.ds(pl.multiple_of(t * UNIT, UNIT), UNIT)
+            gain = token_gain(seg_ref[rows, :], g1_ref)
+            term, d_gain = norm_back(dn_ref[rows, :], s0_buf[rows, :], gain)
+            dlow_ref[rows, :] = (bias_ref[rows, :] + term).astype(BF)
+            dg1_ref[...] += segment_sum(row_ref[:, rows], d_gain)
+
+        traffic.drain()
+
+
+def attend_back(
+    normed, w_qkv, tables, seg_col, pad_col, seg_row, q, k, v, d_ctx, ctx, lse, gamma1, stream0, d_stream1, grads
+):
+    length, width = normed.shape
+    groups = width // 256
+    units = [unit_spec(width, part * (width // 128) + e) for part in range(3) for e in range(2)]
+    column = pl.BlockSpec((length, 256), lambda j: (0, j))
+    full = whole((length, width))
+    part = whole((2 * UNIT, UNIT))
+    pieces = 10
+    return pl.pallas_call(
+        attend_back_body,
+        grid=(groups,),
+        in_specs=[full]
+        + units
+        + [whole((length, 128))] * 3
+        + [whole((length, 1))] * 2
+        + [whole((1, length))]
+        + [column] * 5
+        + [pl.BlockSpec((8, length), lambda j: (j, 0)), whole((8, width))]
+        + [ANY] * 7,
+        out_specs=(
+            pl.BlockSpec((3, 2, width, 128), lambda j: (0, j, 0, 0)),
+            full,
+            whole((8, width)),
+        )
+        + (part,) * 5,
+        out_shape=(
+            shaped((3, width // 128, width, 128), BF),
+            shaped((length, width), BF),
+            shaped((8, width), F32),
+        )
+        + (shaped((2 * UNIT, UNIT), F32),) * 5,
+        scratch_shapes=[pltpu.VMEM((length, length), F32), pltpu.VMEM((length, width), F32)]
+        + [pltpu.VMEM((length, 256), F32)] * 3
+        + [pltpu.VMEM((length, width), F32), pltpu.SemaphoreType.DMA((2,))]
+        + semaphores(pieces, Reduce.sems)
+        + ([pltpu.VMEM((4, 2, 2, UNIT, UNIT), BF)] + Reduce.room(UNIT, UNIT)) * pieces,
+        compiler_params=params(collective_id=3, has_side_effects=True),
+        name="attend_back",
+    )(
+        normed, *([w_qkv] * 6), *tables, seg_col, pad_col, seg_row, q, k, v, d_ctx, ctx, lse,
+        gamma1, stream0, d_stream1, *grads,
+    )
+
+
+def skip_back_body(
+    x_ref, s_ref, d_ref, w_ref, ada_ref, dg_ref, gw_ref,
+    dx_ref, ds_ref, time_ref, sskip, sqkv, stage, send, recv, local, *room,
+):
+    low = d_ref[...]
+    width = x_ref.shape[1]
+    per = ada_ref.shape[5] // 2
     me = Place()
     me.greet()
-    pieces = [
-        Reduce(
-            me, grad[w], out[w], first, rows, flip, send.at[i], recv.at[i], local.at[i],
-            (room[4 * i].at[0], room[4 * i].at[1]), *room[4 * i + 1 : 4 * i + 4],
-        )
-        for i, (w, first, rows, flip) in enumerate(plan)
-    ]
-    for tick in range(ticks_of(len(pieces))):
-        run_ticks(pieces, tick)
-
-
-def reduce_all(*grads):
-    tops = [(g.shape[1] // 4, g.shape[2]) for g in grads]
-    plan = cut(tops)
-    sems = [pltpu.SemaphoreType.DMA((len(plan), 6))] * 2 + [pltpu.SemaphoreType.DMA((len(plan),))]
-    room = [buffer for w, _, rows, _ in plan for buffer in Reduce.scratch(rows, tops[w][1])]
+    traffic = Traffic()
+    count = 0
+    pairs = []
+    for sub in range(3):
+        made = []
+        for rows, flip in halves(2 * UNIT):
+            own, *rest = room[5 * count : 5 * count + 5]
+            theirs, mine = gw_ref.at[:, 1 - me.c, sub, :, :, rows, :], gw_ref.at[:, me.c, sub, :, :, rows, :]
+            out = sqkv.at[rows, pl.ds(sub * UNIT, UNIT)]
+            made.append(Reduce(me, theirs, mine, own, rest, out, flip, True))
+            count += 1
+        pairs.append(made)
+    tall = 512
+    for i in range(2):
+        made = []
+        for e in range(2):
+            rows = pl.ds((2 * i + e) * UNIT, UNIT)
+            own, *rest = room[5 * count : 5 * count + 5]
+            theirs, mine = stage.at[:, 1 - me.c, :, :, rows, :], stage.at[:, me.c, :, :, rows, :]
+            made.append(Reduce(me, theirs, mine, own, rest, sskip.at[rows, :], e == 1, True))
+            count += 1
+        pairs.append(made)
+    for i, made in enumerate(pairs):
+        traffic.add(i if i < 3 else i + 1, *made)
+    traffic.bind(send, recv, local)
+    traffic.at(0)
+    for i in range(4):
+        lanes = slice(i * 2 * UNIT, (i + 1) * 2 * UNIT)
+        part = d_ref[:, lanes]
+        top = dot(x_ref[...], part, TN).astype(BF)
+        end = dot(s_ref[...], part, TN).astype(BF)
+        for c in range(2):
+            cols = slice(c * UNIT, (c + 1) * UNIT)
+            stage[i, c, 0] = top[:, cols].reshape(2, tall, UNIT)
+            stage[i, c, 1] = end[:, cols].reshape(2, tall, UNIT)
+        if i < 3:
+            traffic.at(i + 1)
+    traffic.at(4)
+    for i in range(4):
+        rows = slice((i % 2) * tall, (i % 2 + 1) * tall)
+        tile = jnp.concatenate([w_ref[f // 2, f % 2, i // 2, i % 2] for f in range(NB)], axis=1)
+        out = (dx_ref, ds_ref)[i // 2]
+        out[:, rows] = dot(low, tile, NT)
+        traffic.at(5 + i)
+    total = jnp.zeros((8, width), F32)
+    for f in range(NB):
+        block = ada_ref[f // 2, f % 2].reshape(width, 2 * per)
+        cols = slice(f * per, (f + 1) * per)
+        total += dot(dg_ref[0, :, cols], block[:, :per], NT) + dot(dg_ref[1, :, cols], block[:, per:], NT)
+    time_ref[...] = total
+    traffic.drain()
+
+
+def skip_back(inputs, skip_in, d_low, w_skip, ada, d_gammas, g_qkv):
+    length, width = inputs.shape
+    vmem = pl.BlockSpec(memory_space=pltpu.VMEM)
+    pieces = 10
     return pl.pallas_call(
-        functools.partial(reduce_body, plan, len(grads)),
-        in_specs=[ANY] * len(grads),
-        out_shape=tuple(shaped(top, F32) for top in tops),
-        scratch_shapes=sems + room,
-        compiler_params=params(collective_id=1, has_side_effects=True),
-        name="reduce_all",
-    )(*[g.reshape((4, 2, 2, 2) + top) for g, top in zip(grads, tops)])
+        skip_back_body,
+        in_specs=[vmem] * 6 + [ANY],
+        out_shape=(
+            shaped((length, width), F32),
+            shaped((length, width), F32),
+            shaped((8, width), F32),
+            shaped((4 * UNIT, UNIT), F32),
+            shaped((2 * UNIT, 3 * UNIT), F32),
+        ),
+        scratch_shapes=[pltpu.VMEM(w_skip.shape, BF)]
+        + semaphores(pieces, Reduce.sems)
+        + ([pltpu.VMEM((4, 2, 2, UNIT, UNIT), BF)] + Reduce.room(UNIT, UNIT)) * pieces,
+        compiler_params=params(collective_id=4, has_side_effects=True),
+        name="skip_back",
+    )(inputs, skip_in, d_low, w_skip, ada, d_gammas, g_qkv)
+
+
+def rotary(positions):
+    half = HD // 2
+    lane = jnp.arange(128)
+    frequency = 10000.0 ** (-2.0 * (lane % half).astype(F32) / HD)
+    phase = positions.reshape(-1, 1).astype(F32) * frequency[None, :]
+    cosine, sine = jnp.cos(phase), jnp.sin(phase)
+    early = (lane % HD < half)[None, :]
+    return cosine, jnp.where(early, -sine, 0.0), jnp.where(early, 0.0, sine)
 
 
 def gathered(shard):
@@ -730,68 +1301,94 @@
     return lax.psum_scatter(part, "dp", scatter_dimension=0, tiled=True).astype(F32)
 
 
-def shards(
-    fast, inputs, skip_in, time_emb, seg_ids, positions, pad_mask,
+def ada_grads(flat_time, d_gammas, tall, thin):
+    every = lax.all_gather(flat_time, "fsdp", axis=0, tiled=True)
+    every = lax.all_gather(every, "dp", axis=0, tiled=True)
+    every = lax.dynamic_slice_in_dim(every, lax.axis_index("dp") * tall, tall, 1)
+    gammas = lax.all_gather(d_gammas, "fsdp", axis=1, tiled=True)
+    gammas = lax.all_gather(gammas, "dp", axis=1, tiled=True)
+    gammas = lax.dynamic_slice_in_dim(gammas, lax.axis_index("fsdp") * thin, thin, 2)
+    return [jnp.einsum("nd,ne->de", every, part, preferred_element_type=F32) for part in gammas]
+
+
+def fused(
+    inputs, skip_in, time_emb, seg_ids, positions, pad_mask,
     w_skip, w_ada1, w_qkv, w_out, w_ada2, w_up, w_down, cotangent,
 ):
     slots = time_emb.shape[1]
+    length, width = inputs.shape
     seg_col, seg_row = seg_ids.reshape(-1, 1), seg_ids.reshape(1, -1)
     pad_col = pad_mask.reshape(-1, 1)
     tables = rotary(positions)
     flat_time = time_emb.reshape(slots, -1)
     time8 = jnp.pad(flat_time, ((0, 8 - slots), (0, 0)))
-    if fast:
-        w_ada = jnp.concatenate([w_ada1, w_ada2], axis=1)
-        f_skip, ada, f_qkv, f_out, f_up, f_down = gather_all(w_skip, w_ada, w_qkv, w_out, w_up, w_down)
-    else:
-        f_skip, f_qkv, f_out = gathered(w_skip), gathered(w_qkv), gathered(w_out)
-        f_up, f_down = gathered(w_up), gathered(w_down)
-        ada = jnp.concatenate([gathered(w_ada1), gathered(w_ada2)], axis=2)
-    stream0, normed1, gamma1, gamma2 = front(inputs, skip_in, f_skip, time8, ada, seg_col)
-    q, k, v, ctx, lse = attend(normed1, f_qkv, tables, seg_col, pad_col, seg_row)
-    output, g_down, g_up, g_out, d_stream1, d_ctx, d_gamma2 = mlp(
+    w_ada = jnp.concatenate([w_ada1, w_ada2], axis=1)
+    stream0, normed1, gamma1, gamma2, f_skip, f_ada, f_qkv = front(
+        inputs, skip_in, time8, seg_col, w_skip, w_ada, w_qkv
+    )
+    f_qkv = f_qkv.reshape(NB, width, -1)
+    q, k, v, ctx, lse, f_out, fup0, fdn0, fup1 = attend(
+        normed1, f_qkv, tables, seg_col, pad_col, seg_row, w_out, w_up, w_down
+    )
+    output, g_out, d_stream1, d_ctx, d_gamma2, sup0, sdn0, sup1, sdn1, *rest = mlp(
+        stream0, ctx, f_out, gamma2, seg_col, seg_row, cotangent, w_up, w_down, fup0, fdn0, fup1
+    )
+    g_qkv, d_low, d_gamma1, sup2, sdn2, sup3, sdn3, s_out = attend_back(
+        normed1, f_qkv, tables, seg_col, pad_col, seg_row, q, k, v, d_ctx, ctx, lse, gamma1,
+        stream0, d_stream1, (*rest[:4], g_out),
+    )
+    d_gammas = jnp.stack([d_gamma1, d_gamma2]).astype(BF)
+    d_input, d_skip, d_time, s_skip, s_qkv = skip_back(
+        inputs, skip_in, d_low, f_skip, f_ada, d_gammas, g_qkv.reshape(4, 2, 3, 2, 2, -1, UNIT)
+    )
+    g_ada = ada_grads(flat_time, d_gammas[:, :slots], *w_ada1.shape)
+    s_up = jnp.concatenate([sup0, sup1, sup2, sup3], axis=1)
+    s_down = jnp.stack([sdn0, sdn1, sdn2, sdn3]).reshape(4, 2, UNIT, UNIT)
+    s_down = jnp.transpose(s_down, (1, 0, 2, 3)).reshape(w_down.shape)
+    return (
+        output, d_input, d_skip, d_time[:slots].reshape(time_emb.shape),
+        s_skip, g_ada[0], s_qkv, s_out, g_ada[1], s_up, s_down,
+    )
+
+
+def plain(
+    inputs, skip_in, time_emb, seg_ids, positions, pad_mask,
+    w_skip, w_ada1, w_qkv, w_out, w_ada2, w_up, w_down, cotangent,
+):
+    slots = time_emb.shape[1]
+    width = inputs.shape[1]
+    seg_col, seg_row = seg_ids.reshape(-1, 1), seg_ids.reshape(1, -1)
+    pad_col = pad_mask.reshape(-1, 1)
+    tables = rotary(positions)
+    flat_time = time_emb.reshape(slots, -1)
+    time8 = jnp.pad(flat_time, ((0, 8 - slots), (0, 0)))
+    f_skip, f_qkv, f_out, f_up, f_down, f_ada1, f_ada2 = [
+        gathered(w) for w in (w_skip, w_qkv, w_out, w_up, w_down, w_ada1, w_ada2)
+    ]
+    ada = jnp.concatenate([f_ada1, f_ada2], axis=2)
+    stream0, normed1, gamma1, gamma2 = plain_front(inputs, skip_in, f_skip, time8, ada, seg_col)
+    q, k, v, ctx, lse = plain_attend(normed1, f_qkv, tables, seg_col, pad_col, seg_row)
+    output, g_down, g_up, g_out, d_stream1, d_ctx, d_gamma2 = plain_mlp(
         stream0, ctx, f_out, gamma2, seg_col, seg_row, f_up, f_down, cotangent
     )
-    g_qkv, d_low, d_gamma1 = attend_back(
+    g_qkv, d_low, d_gamma1 = plain_attend_back(
         normed1, f_qkv, tables, seg_col, pad_col, seg_row, q, k, v, d_ctx, ctx, lse,
         stream0, gamma1, d_stream1,
     )
-    width = inputs.shape[1]
     g_qkv = jnp.transpose(
         g_qkv.reshape(NB, 3, width, 128), (0, 2, 1, 3)
     ).reshape(NB, width, 3 * width // NB)
-    g_skip, d_input, d_skip = skip_back(inputs, skip_in, d_low, f_skip)
-    d_gammas = [d[:slots].astype(BF) for d in (d_gamma1, d_gamma2)]
-    per = width // NB
+    g_skip, d_input, d_skip = plain_skip_back(inputs, skip_in, d_low, f_skip)
+    d_gammas = jnp.stack([d_gamma1, d_gamma2]).astype(BF)[:, :slots]
     d_time = 0.0
-    for d_gamma, part in zip(d_gammas, (ada[:, :, :per], ada[:, :, per:])):
+    for d_gamma, part in zip(d_gammas, (f_ada1, f_ada2)):
         flat = jnp.transpose(part, (1, 0, 2)).reshape(width, width)
         d_time = d_time + jnp.einsum("ne,de->nd", d_gamma, flat, preferred_element_type=F32)
-    axes = ("dp", "fsdp")
-    all_time = lax.all_gather(flat_time, axes, axis=0, tiled=True)
-    tall, thin = w_ada1.shape
-    all_time = lax.dynamic_slice_in_dim(all_time, lax.axis_index("dp") * tall, tall, 1)
-    all_gamma = lax.all_gather(jnp.concatenate(d_gammas, axis=1), axes, axis=0, tiled=True)
-    g_ada = []
-    for i in range(2):
-        mine = lax.dynamic_slice_in_dim(all_gamma, i * width + lax.axis_index("fsdp") * thin, thin, 1)
-        g_ada.append(jnp.einsum("nd,ne->de", all_time, mine, preferred_element_type=F32))
-    if fast:
-        s_down, s_up, s_out, s_qkv, s_skip = reduce_all(g_down, g_up, g_out, g_qkv, g_skip)
-    else:
-        s_down, s_up, s_out, s_qkv, s_skip = [scattered(g) for g in (g_down, g_up, g_out, g_qkv, g_skip)]
+    g_ada = ada_grads(flat_time, d_gammas, *w_ada1.shape)
     return (
-        output,
-        d_input,
-        d_skip,
-        d_time.reshape(time_emb.shape),
-        s_skip,
-        g_ada[0],
-        s_qkv,
-        s_out,
-        g_ada[1],
-        s_up,
-        s_down,
+        output, d_input, d_skip, d_time.reshape(time_emb.shape),
+        scattered(g_skip), g_ada[0], scattered(g_qkv), scattered(g_out), g_ada[1],
+        scattered(g_up), scattered(g_down),
     )
 
 
@@ -799,9 +1396,9 @@
     rows = P(("dp", "fsdp"), None)
     cube = P(("dp", "fsdp"), None, None)
     tile = P("dp", "fsdp")
-    fast = mesh.shape["dp"] == 4 and mesh.shape["fsdp"] == NB
+    fits = mesh.shape["dp"] == 4 and mesh.shape["fsdp"] == NB
     return jax.shard_map(
-        functools.partial(shards, fast),
+        fused if fits else plain,
         mesh=mesh,
         in_specs=(rows, rows, cube) + (rows,) * 3 + (tile,) * 7 + (rows,),
         out_specs=(rows, rows, rows, cube) + (tile,) * 7,

time: 683 us -> 531 us (0.78)
  Pallas kernels: 534 us -> 453 us
  local copies, waits for them, and re-layouts: 55.3 us -> 17.1 us
  blocking collectives: 79.5 us -> 46.3 us
    pallas_call x5 -> x3, Pallas kernels: 423 us -> 291 us  [the longest x1 134 us: mlp(): pl.pallas_call(mlp_body, grid=(8,), in_specs=[ANY, full, whole(w_out.shap...]
    all_gather x2 -> x4, blocking collectives: 79.5 us -> 46.3 us  [the longest x1 14 us: ada_grads(): gammas = lax.all_gather(d_gammas, 'fsdp', axis=1, tiled=True)]
    another operation x2 -> x0, local copies, waits for them, and re-layouts: 27.4 us -> none  [reduce_all(): g.reshape((4, 2, 2, 2) + top)]
    pallas_call x1, Pallas kernels: 38.1 us -> 64.4 us  [attend(): pl.pallas_call(attend_body, grid=(groups,), in_specs=[whole((length, widt...]
    pallas_call x1, Pallas kernels: 73 us -> 98.2 us  [attend_back(): pl.pallas_call(attend_back_body, grid=(groups,), in_specs=[full] + units...]
    transpose x3 -> x1, local copies, waits for them, and re-layouts: 10.3 us -> 0.83 us  [fused(): s_down = jnp.transpose(s_down, (1, 0, 2, 3)).reshape(w_down.shape)]
    reshape x3, local copies, waits for them, and re-layouts: 11.4 us -> 4.1 us  [the longest x1 1.71 us: fused(): seg_col, seg_row = (seg_ids.reshape(-1, 1), seg_ids.reshape(1, -1))]
    unnamed x27 -> x41, local copies, waits for them, and re-layouts: 3.87 us -> 10.8 us
where the time goes in v3:
time: 531 us; the launch traced here: 527 us
  Pallas kernels  453 us (85%)
  blocking collectives  46.3 us (9%)
  local copies, waits for them, and re-layouts  17.1 us (3%)
  other arithmetic  7.34 us (1%)
    pallas_call x1, Pallas kernels, mlp(): pl.pallas_call(mlp_body, grid=(8,), in_specs=[ANY, full, whole(w_out.shap...  134 us
    pallas_call x1, Pallas kernels, attend_back(): pl.pallas_call(attend_back_body, grid=(groups,), in_specs=[full] + units...  98.2 us
    pallas_call x1, Pallas kernels, front(): pl.pallas_call(front_body, in_specs=[vmem] * 4 + [ANY] * 3, out_specs=(vm...  86.3 us
    pallas_call x1, Pallas kernels, skip_back(): pl.pallas_call(skip_back_body, in_specs=[vmem] * 6 + [ANY], out_shape=(sh...  70.4 us
    pallas_call x1, Pallas kernels, attend(): pl.pallas_call(attend_body, grid=(groups,), in_specs=[whole((length, widt...  64.4 us
    all_gather x1, blocking collectives, ada_grads(): gammas = lax.all_gather(d_gammas, 'fsdp', axis=1, tiled=True)  14 us
    all_gather x1, blocking collectives, ada_grads(): every = lax.all_gather(flat_time, 'fsdp', axis=0, tiled=True)  14 us
    unnamed x41, local copies, waits for them, and re-layouts  10.8 us

profile of v3, /device:TPU:0, one launch (start us, length us, event | category | flops | bytes accessed | tf_op | source)
XLA Modules:
  0.0 527.1 jit_solution(908696789371066308)
XLA Ops:
  0.6 1.7 copy.42.seg_ref
  2.4 1.5 pad_maximum_fusion.1.ada_ref
  3.9 1.3 pad.4.time_ref
  5.2 86.3 %front.1 = (f32[1024,1024]{1,0:T(8,128)}, bf16[1024,1024]{1,0:T(8,128)(2,1)}, f32[8,1024]{1,0:T(8,128)}, f32[8,1024]{1,0:T(8,128)}, bf16[4,2,2,2,512,128]{5,4,3,...) custom-call(bf16[1024,1024]{1,0:T(8,128)(2,1)} %x_ref.3, ...), custom_call_target="tpu_custom_call" | custom-call | tf_op jit(solution)/shard_map/front/pallas_call | solution.py:736
  91.6 3.2 fusion
  94.8 1.0 copy.44.pad_ref
  95.8 64.4 %attend.1 = (bf16[1024,1024]{1,0:T(8,128)(2,1)}, bf16[1024,1024]{1,0:T(8,128)(2,1)}, bf16[1024,1024]{1,0:T(8,128)(2,1)}, bf16[1024,1024]{1,0:T(8,128)(2,1)}, f32...) custom-call(bf16[1024,1024]{1,0:T(8,128)(2,1)} %get-tuple-element.54, ...), custom_call_target="tpu_custom_call" | custom-call | tf_op jit(solution)/shard_map/attend/pallas_call | solution.py:808
  160.2 133.9 %mlp.1 = (bf16[1024,1024]{1,0:T(8,128)(2,1)}, bf16[4,2,2,2,256,128]{5,4,3,2,1,0:T(8,128)(2,1)}, f32[1024,1024]{1,0:T(8,128)}, bf16[1024,1024]{1,0:T(8,128)(2,1)}...) custom-call(f32[1024,1024]{1,0:T(8,128)} %get-tuple-element.53.strea, ...), custom_call_target="tpu_custom_call" | custom-call | tf_op jit(solution)/shard_map/mlp/pallas_call | solution.py:995
  294.1 98.2 %attend_back.1 = (bf16[3,8,1024,128]{3,2,1,0:T(8,128)(2,1)}, bf16[1024,1024]{1,0:T(8,128)(2,1)}, f32[8,1024]{1,0:T(8,128)}, f32[256,128]{1,0:T(8,128)}, f32[256,...) custom-call(bf16[1024,1024]{1,0:T(8,128)(2,1)} %get-tuple-element.54.n_ref, ...), custom_call_target="tpu_custom_call" | custom-call | tf_op jit(solution)/shard_map/attend_back/pallas_call | solution.py:1157
  392.5 0.0 copy-start.14
  392.5 1.1 maximum_bitcast_fusion
  393.6 0.8 copy.52
  394.4 0.0 copy-done.7
  394.5 0.0 copy-done.11
  394.5 0.8 pad_maximum_fusion
  395.3 14.0 %all_gather.14 = bf16[2,32,1024]{2,0,1:T(2,128)(2,1)S(1)} all-gather(bf16[2,4,1024]{2,0,1:T(2,128)(2,1)S(1)} %copy.50), channel_id=1, replica_groups=mesh['dp'=4,'fsdp'=8] {'fsdp'}, dimensions={1}, use_global_device_ids=true | all-gather | bytes 147456 | tf_op jit(solution)/shard_map/all_gather | solution.py:1308
  409.3 9.5 %all_gather.15 = bf16[2,128,1024]{2,1,0:T(8,128)(2,1)S(1)} all-gather(bf16[2,32,1024]{2,1,0:T(8,128)(2,1)S(1)} %copy.51), channel_id=1, replica_groups=mesh['dp'=4,'fsdp'=8] {'dp'}, dimensions={1}, use_global_device_ids=true | all-gather | bytes 655360 | tf_op jit(solution)/shard_map/all_gather | solution.py:1309
  418.9 14.0 %all-gather = bf16[1,32,1024]{2,0,1:T(2,128)(2,1)S(1)} all-gather(bf16[1,4,1024]{2,0,1:T(2,128)(2,1)S(1)} %copy.48), channel_id=2, replica_groups=mesh['dp'=4,'fsdp'=8] {'fsdp'}, dimensions={1}, use_global_device_ids=true | all-gather | bytes 73728 | tf_op jit(solution)/shard_map/all_gather | solution.py:1305
  432.9 8.8 %all-gather.1 = bf16[1,128,1024]{2,1,0:T(8,128)(2,1)S(1)} all-gather(bf16[1,32,1024]{2,1,0:T(8,128)(2,1)S(1)} %copy.49), channel_id=3, replica_groups=mesh['dp'=4,'fsdp'=8] {'dp'}, dimensions={1}, use_global_device_ids=true | all-gather | bytes 327680 | tf_op jit(solution)/shard_map/all_gather | solution.py:1306
  441.7 0.9 fusion.3
  442.6 0.8 fusion.5
  443.4 0.6 pad_maximum_fusion.2.dg_ref
  444.0 70.4 %skip_back.1 = (f32[1024,1024]{1,0:T(8,128)}, f32[1024,1024]{1,0:T(8,128)}, f32[8,1024]{1,0:T(8,128)}, f32[512,128]{1,0:T(8,128)}, f32[256,384]{1,0:T(8,128)}) custom-call(bf16[1024,1024]{1,0:T(8,128)(2,1)} %x_ref.3, bf16[1024,1024]{1,0:T(8,128)(2,1)} %s_ref.3, bf16[1024,1024]{1,0:T(8,128)(2,1)} %get-tuple-element.75.d_ref, ...), custom_call_target="tpu_custom_call" | custom-call | tf_op jit(solution)/shard_map/skip_back/pallas_call | solution.py:1259
  514.5 1.4 slice_bitcast_fusion
  515.8 1.3 copy.59
  517.2 1.6 copy-done.1
  518.8 2.1 copy.60
  520.9 1.6 copy-done
  522.5 2.0 copy.61
  524.5 0.7 copy.62
  525.2 0.7 copy.63
  526.0 0.7 copy.64
  (38 shorter events, 0.2 us)
Async XLA Ops:
  5.2 86.4 %copy-start.16 = (s32[1,1024]{1,0:T(1,128)S(1)}, s32[1,1024]{1,0:T(1,128)}, u32[]{:S(2)}) copy-start(s32[1,1024]{1,0:T(1,128)} %param.18) | copy-start | bytes 12292
  5.2 89.6 %copy-start.15 = (s32[1,1024]{1,0:T(1,128)S(1)}, s32[1,1024]{1,0:T(1,128)}, u32[]{:S(2)}) copy-start(s32[1,1024]{1,0:T(1,128)} %param.19) | copy-start | bytes 12292
  294.1 98.3 %copy-start.8 = (f32[256,128]{1,0:T(8,128)S(1)}, f32[256,128]{1,0:T(8,128)}, u32[]{:S(2)}) copy-start(f32[256,128]{1,0:T(8,128)} %get-tuple-element.91) | copy-start | bytes 393220
  294.1 98.3 %copy-start.9 = (f32[256,128]{1,0:T(8,128)S(1)}, f32[256,128]{1,0:T(8,128)}, u32[]{:S(2)}) copy-start(f32[256,128]{1,0:T(8,128)} %get-tuple-element.92) | copy-start | bytes 393220
  392.4 2.1 copy-start.6
  392.4 2.1 copy-start.7
  392.4 2.0 copy-start.10
  392.4 2.0 copy-start.11
  392.4 2.9 copy-start.12
  392.4 2.9 copy-start.13
  392.5 26.4 %copy-start.14 = (bf16[1,4,1024]{2,1,0:T(4,128)(2,1)S(1)}, bf16[1,4,1024]{2,1,0:T(4,128)(2,1)}, u32[]{:S(2)}) copy-start(bf16[1,4,1024]{2,1,0:T(4,128)(2,1)} %param.16) | copy-start | bytes 24580
  444.0 71.8 %copy-start.2 = (bf16[1024,1024]{1,0:T(8,128)(2,1)S(1)}, bf16[1024,1024]{1,0:T(8,128)(2,1)}, u32[]{:S(2)}) copy-start(bf16[1024,1024]{1,0:T(8,128)(2,1)} %get-tuple-element.111) | copy-start | bytes 6291460
  515.8 2.9 copy-start.1
  518.8 3.7 copy-start
  522.5 2.0 copy-start.4
  522.5 2.7 copy-start.3
  522.5 3.5 copy-start.5

commit v4 on v3

--- a/solution.py
+++ b/solution.py
@@ -74,10 +74,12 @@
 
 def fill_bias(bias_ref, seg_ref, pad_ref, row_ref):
     length = seg_ref.shape[0]
-    for t in range(length // 128):
-        rows = slice(t * 128, (t + 1) * 128)
-        keys = lax.broadcasted_iota(jnp.int32, (128, length), 0) + t * 128
-        queries = lax.broadcasted_iota(jnp.int32, (128, length), 1)
+
+    @pl.loop(0, length // UNIT)
+    def _(t):
+        rows = pl.ds(pl.multiple_of(t * UNIT, UNIT), UNIT)
+        keys = lax.broadcasted_iota(jnp.int32, (UNIT, length), 0) + t * UNIT
+        queries = lax.broadcasted_iota(jnp.int32, (UNIT, length), 1)
         allowed = (seg_ref[rows, :] == row_ref[0:1, :]) & (
             (pad_ref[rows, :] > 0) | (keys == queries)
         )
@@ -460,10 +462,20 @@
     def along_z(self, hop):
         return (self.dp, ((self.z + hop) % 4) * 2 + self.c)
 
-    def greet(self):
+    def on_dp(self, index):
+        return (index, self.fs)
+
+    def on_fsdp(self, index):
+        return (self.dp, index)
+
+    def greet(self, wide=False):
         barrier = pltpu.get_barrier_semaphore()
-        peers = [self.across_x(), self.across_y(), self.sibling()]
-        peers += [self.along_z(hop) for hop in (1, 2, 3)]
+        if wide:
+            peers = [self.on_dp((self.dp + hop) % 4) for hop in range(1, 4)]
+            peers += [self.on_fsdp((self.fs + hop) % NB) for hop in range(1, NB)]
+        else:
+            peers = [self.across_x(), self.across_y(), self.sibling()]
+            peers += [self.along_z(hop) for hop in (1, 2, 3)]
         for peer in peers:
             pl.semaphore_signal(barrier, inc=1, device_id=peer, device_id_type=pl.DeviceIdType.MESH)
         pl.semaphore_wait(barrier, len(peers))
@@ -595,21 +607,31 @@
             if self.load:
                 flow(*load).wait()
             made[0].wait_recv()
-            self.own[...] = self.own[...] + self.other[...]
+
+            @pl.loop(0, 4)
+            def _(z):
+                self.own[z] = self.own[z] + self.other[z]
+
             made[1].start()
         elif number == 2:
             made[1].wait_recv()
-            if self.flip:
-                self.half[...] = self.half[...] + self.own[:, :, me.x]
-            else:
-                self.half[...] = self.half[...] + self.own[:, me.y]
+
+            @pl.loop(0, 4)
+            def _(z):
+                kept = self.own[z, :, me.x] if self.flip else self.own[z, me.y]
+                self.half[z] = self.half[z] + kept
+
             made[2].start()
         elif number == 3:
             made[0].wait_send()
             made[1].wait_send()
             made[2].wait_recv()
             kept = me.y if self.flip else me.x
-            self.quarter[...] = self.quarter[...] + self.half[:, kept]
+
+            @pl.loop(0, 4)
+            def _(z):
+                self.quarter[z] = self.quarter[z] + self.half[z, kept]
+
             for copy in made[3:]:
                 copy.start()
         else:
@@ -623,15 +645,36 @@
                 copy.wait_send()
 
 
+class Swap:
+    def __init__(self, place, axis, what, into, send, recv):
+        count = 4 if axis == "dp" else NB
+        at = place.dp if axis == "dp" else place.fs
+        find = place.on_dp if axis == "dp" else place.on_fsdp
+        self.at, self.what, self.into = at, what, into
+        self.plan = []
+        for hop in range(1, count):
+            peer = (at + hop) % count
+            self.plan.append((what(peer), into(at), send.at[hop - 1], recv.at[hop - 1], find(peer)))
+
+    def start(self):
+        for copy in self.plan:
+            remote(*copy).start()
+
+    def wait(self):
+        for copy in self.plan:
+            remote(*copy).wait()
+
+
 class Traffic:
     def __init__(self):
         self.todo, self.pieces = {}, []
 
-    def add(self, first, *pieces, gap=1):
+    def add(self, first, *pieces, gap=2):
         self.pieces += pieces
+        hooks = first if isinstance(first, tuple) else [first + stage * gap for stage in range(5)]
         for piece in pieces:
-            for stage in range(5):
-                self.todo.setdefault(first + stage * gap, []).append((stage, piece))
+            for stage, hook in enumerate(hooks):
+                self.todo.setdefault(hook, []).append((stage, piece))
 
     def bind(self, send, recv, local):
         for i, piece in enumerate(self.pieces):
@@ -687,69 +730,106 @@
 
 
 def front_body(
-    x_ref, s_ref, time_ref, seg_ref, skip_ref, ada_ref, qkv_ref,
-    stream_ref, normed_ref, g1_ref, g2_ref, fskip_ref, fada_ref, fqkv_ref,
-    w_ref, a_ref, w_sem, send, recv, local,
+    x_ref, s_ref, time_ref, seg_ref, ada_ref, skip_ref, qkv_ref,
+    stream_ref, normed_ref, g1_ref, g2_ref, slots, fskip_ref, fqkv_ref,
+    w_ref, part, got, summed, gam, w_sem, sends, recvs, send, recv, local,
 ):
     length, width = x_ref.shape
     per = ada_ref.shape[1] // 2
     me = Place()
-    me.greet()
+    me.greet(True)
     traffic = Traffic()
-    plan = row_pairs(me, skip_ref, fskip_ref, 4) + row_pairs(me, ada_ref, fada_ref, 2)
-    need = len(plan) + 4
-    plan += row_pairs(me, qkv_ref, fqkv_ref, 4)
+    plan = row_pairs(me, skip_ref, fskip_ref, 8)
+    need = len(plan) + 8
+    plan += row_pairs(me, qkv_ref, fqkv_ref, 8)
     for i, pair in enumerate(plan):
         traffic.add(i, *pair)
     traffic.bind(send, recv, local)
-    for hook in range(need):
+    lay = functools.partial(pl.ds, 0)
+    swaps = [
+        Swap(me, "dp", lambda p: time_ref.at[p], lambda m: slots.at[m, me.fs], sends.at[0], recvs.at[0]),
+        Swap(me, "fsdp", lambda p: slots.at[:, me.fs], lambda m: slots.at[:, m], sends.at[1], recvs.at[1]),
+        Swap(me, "dp", lambda p: part.at[p, :, lay(8), :], lambda m: got.at[m], sends.at[2], recvs.at[2]),
+        Swap(me, "fsdp", lambda p: summed.at[p], lambda m: gam.at[m], sends.at[3], recvs.at[3]),
+    ]
+    slots[me.dp, me.fs] = time_ref[me.dp]
+    swaps[0].start()
+    traffic.at(0)
+    swaps[0].wait()
+    swaps[1].start()
+    traffic.at(1)
+    swaps[1].wait()
+    made = dot(slots[...].reshape(4 * NB * 16, -1), ada_ref[...])
+    part[...] = made.reshape(part.shape)
+    got[me.dp] = part[me.dp, :, :8, :]
+    swaps[2].start()
+    traffic.at(2)
+    swaps[2].wait()
+    summed[...] = got[0] + got[1] + got[2] + got[3]
+    gam[me.fs] = summed[me.fs]
+    swaps[3].start()
+    for hook in range(3, need):
         traffic.at(hook)
-    loads = [flow(fskip_ref, w_ref, w_sem.at[0]), flow(fada_ref, a_ref, w_sem.at[1])]
-    for load in loads:
-        load.start()
-    for load in loads:
-        load.wait()
-    for i in range(4):
+    load = flow(fskip_ref, w_ref, w_sem)
+    load.start()
+    swaps[3].wait()
+    for f in range(NB):
+        g1_ref[:, f * per : (f + 1) * per] = gam[f, :, :per]
+        g2_ref[:, f * per : (f + 1) * per] = gam[f, :, per:]
+    load.wait()
+
+    def stream(i):
         tile = jnp.concatenate([w_ref[i, c].reshape(2 * width, UNIT) for c in range(2)], axis=1)
-        part = dot(x_ref[...], tile[:width]) + dot(s_ref[...], tile[width:])
-        stream_ref[:, i * 2 * UNIT : (i + 1) * 2 * UNIT] = part
-        if i % 2 == 1:
-            traffic.at(need + i // 2)
-    for f in range(NB):
-        both = dot(time_ref[...], a_ref[f // 2, f % 2].reshape(width, 2 * per))
-        g1_ref[:, f * per : (f + 1) * per] = both[:, :per]
-        g2_ref[:, f * per : (f + 1) * per] = both[:, per:]
-
-    @pl.loop(0, length // UNIT)
-    def _(t):
+        lanes = pl.ds(pl.multiple_of(i * 2 * UNIT, 2 * UNIT), 2 * UNIT)
+        stream_ref[:, lanes] = dot(x_ref[...], tile[:width]) + dot(s_ref[...], tile[width:])
+
+    def normalise(t):
         rows = pl.ds(pl.multiple_of(t * UNIT, UNIT), UNIT)
         gain = token_gain(seg_ref[rows, :], g1_ref)
         normed_ref[rows, :] = norm(stream_ref[rows, :], gain)
 
+    pl.loop(0, 2)(stream)
+    traffic.at(need)
+    pl.loop(2, 4)(stream)
+    traffic.at(need + 1)
+    half = length // UNIT // 2
+    pl.loop(0, half)(normalise)
+    traffic.at(need + 2)
+    pl.loop(half, 2 * half)(normalise)
     traffic.drain()
 
 
-def front(inputs, skip_in, time8, seg_col, w_skip, w_ada, w_qkv):
+def front(inputs, skip_in, time_cut, seg_col, w_ada, w_skip, w_qkv):
     length, width = inputs.shape
-    fulls = [full_of(*w.shape) for w in (w_skip, w_ada, w_qkv)]
+    fulls = [full_of(*w.shape) for w in (w_skip, w_qkv)]
     vmem = pl.BlockSpec(memory_space=pltpu.VMEM)
+    per = w_ada.shape[1]
     return pl.pallas_call(
         front_body,
-        in_specs=[vmem] * 4 + [ANY] * 3,
-        out_specs=(vmem,) * 4 + (ANY,) * 3,
+        in_specs=[vmem] * 5 + [ANY] * 2,
+        out_specs=(vmem,) * 5 + (ANY,) * 2,
         out_shape=(
             shaped((length, width), F32),
             shaped((length, width), BF),
             shaped((8, width), F32),
             shaped((8, width), F32),
+            shaped((4, NB, 16, w_ada.shape[0]), BF),
             *fulls,
         ),
-        scratch_shapes=[pltpu.VMEM(f.shape, BF) for f in fulls[:2]]
-        + [pltpu.SemaphoreType.DMA((2,))]
-        + semaphores(10, Gather.sems),
+        scratch_shapes=[
+            pltpu.VMEM(fulls[0].shape, BF),
+            pltpu.VMEM((4, NB, 16, per), F32),
+            pltpu.VMEM((4, NB, 8, per), F32),
+            pltpu.VMEM((NB, 8, per), F32),
+            pltpu.VMEM((NB, 8, per), F32),
+            pltpu.SemaphoreType.DMA,
+            pltpu.SemaphoreType.DMA((4, NB - 1)),
+            pltpu.SemaphoreType.DMA((4, NB - 1)),
+        ]
+        + semaphores(16, Gather.sems),
         compiler_params=params(collective_id=0, has_side_effects=True),
         name="front",
-    )(inputs, skip_in, time8, seg_col, w_skip, w_ada, w_qkv)
+    )(inputs, skip_in, time_cut, seg_col, w_ada, w_skip, w_qkv)
 
 
 def attend_body(
@@ -767,7 +847,7 @@
         up_pair(me, up_ref, fup1_ref, 1),
     ]
     for i, pair in enumerate(pairs):
-        traffic.add(2 * i, *pair, gap=2)
+        traffic.add(2 * i, *pair, gap=3)
     traffic.bind(send, recv, local)
     fire = functools.partial(traffic.fire, step, 4, 4)
 
@@ -826,7 +906,7 @@
 def mlp_body(
     stream0_ref, ctx_ref, wout_ref, g2_ref, seg_ref, row_ref, cot_ref,
     up_ref, down_ref, fup0, fdn0, fup1,
-    out_ref, gout_ref, ds1_ref, dctx_ref, dg2_ref, sup0, sdn0, sup1, sdn1, gup2, gdn2, gup3, gdn3,
+    out_ref, gout_ref, ds1_ref, dctx_ref, dg2_ref, sup0, sdn0, gup1, gdn1, gup2, gdn2, gup3, gdn3,
     fdn1, fup2, fdn2, fup3, fdn3,
     s1_ref, n2_ref, acc_ref, dn_ref, up_tile, dn_tile, act_ref, pre_ref, stage_up, stage_dn,
     sem, gsend, grecv, glocal, rsend, rrecv, rlocal, *room,
@@ -837,14 +917,14 @@
     tiles = length // UNIT
     me = Place()
     gather, reduce = Traffic(), Traffic()
-    gather.add(0, *down_pair(me, down_ref, fdn1, 1))
+    gather.add((0, 1, 3, 5, 6), *down_pair(me, down_ref, fdn1, 1))
     gather.add(2, *up_pair(me, up_ref, fup2, 2))
     gather.add(4, *down_pair(me, down_ref, fdn2, 2))
-    gather.add(6, *up_pair(me, up_ref, fup3, 3))
-    gather.add(8, *down_pair(me, down_ref, fdn3, 3))
+    gather.add(7, *up_pair(me, up_ref, fup3, 3))
+    gather.add(10, *down_pair(me, down_ref, fdn3, 3))
     gather.bind(gsend, grecv, glocal)
     count = 0
-    for q, (sup, sdn) in enumerate(((sup0, sdn0), (sup1, sdn1))):
+    for q, (sup, sdn) in enumerate(((sup0, sdn0),)):
         made = []
         for rows, flip in halves(2 * UNIT):
             theirs = stage_up.at[q, 1 - me.c, :, :, :, rows, :]
@@ -857,11 +937,11 @@
             rows = pl.ds(e * UNIT, UNIT)
             made.append(Reduce(me, theirs, mine, mine, room[4 * count : 4 * count + 4], sdn.at[rows, :], e == 1, False))
             count += 1
-        reduce.add(4 + 4 * q, *made[2:])
-        reduce.add(5 + 4 * q, *made[:2])
+        reduce.add(6, *made[2:])
+        reduce.add(7, *made[:2])
     reduce.bind(rsend, rrecv, rlocal)
     ups, downs = (fup0, fup1, fup2, fup3), (fdn0, fdn1, fdn2, fdn3)
-    saves = {4: (gup2, gdn2), 6: (gup3, gdn3)}
+    saves = {2: (gup1, gdn1), 4: (gup2, gdn2), 6: (gup3, gdn3)}
 
     def tile_loads(s):
         q, e = s // 2, s % 2
@@ -874,13 +954,13 @@
         q, e = s // 2, s % 2
         gup, gdn = saves[2 * q]
         return (
-            flow(stage_up.at[q % 2, e], gup.at[e], sem.at[2, s - 4]),
-            flow(stage_dn.at[q % 2, e], gdn.at[e], sem.at[3, s - 4]),
+            flow(stage_up.at[q % 2, e], gup.at[e], sem.at[2, s - 2]),
+            flow(stage_dn.at[q % 2, e], gdn.at[e], sem.at[3, s - 2]),
         )
 
     def hook(which):
-        gather.fire(step, steps, 2, which)
-        reduce.fire(step, steps, 2, which)
+        gather.fire(step, steps, 3, which)
+        reduce.fire(step, steps, 3, which)
 
     @pl.when(step == 0)
     def _():
@@ -938,15 +1018,19 @@
     grad = dot(act_ref[...], cot_ref[...], TN).astype(BF)
     for f in range(NB):
         stage_dn[par, slot, f // 2, f % 2] = grad[:, f * UNIT : (f + 1) * UNIT].reshape(2, 2, UNIT, UNIT)
+    hook(2)
     grad = dot(n2_ref[...], pre_ref[...], TN).astype(BF)
     for z in range(4):
         stage_up[par, slot, z] = grad[:, z * UNIT : (z + 1) * UNIT].reshape(2, 2, 2 * UNIT, UNIT)
-    for s in range(4, steps):
+    for s in range(2, steps):
 
         @pl.when(step == s)
         def _(s=s):
             for save in grad_saves(s):
                 save.start()
+            if s == 5:
+                for save in grad_saves(2) + grad_saves(3):
+                    save.wait()
 
     @pl.when(step == steps - 1)
     def _():
@@ -991,7 +1075,7 @@
     part = pl.BlockSpec((2 * UNIT, UNIT), lambda j: (0, 0))
     quarter = full_of(2 * UNIT, UNIT)
     grads = (shaped((2, 4, 2, 2, 2 * UNIT, UNIT), BF), shaped((2, 4, 2, 2, 2, UNIT, UNIT), BF))
-    pieces = 8
+    pieces = 4
     return pl.pallas_call(
         mlp_body,
         grid=(8,),
@@ -1005,7 +1089,7 @@
             full,
         ]
         + [ANY] * 5,
-        out_specs=(full, whole(w_out.shape), ANY, full, whole((8, width))) + (part,) * 4 + (ANY,) * 9,
+        out_specs=(full, whole(w_out.shape), ANY, full, whole((8, width))) + (part,) * 2 + (ANY,) * 11,
         out_shape=(
             shaped((length, width), BF),
             shaped(w_out.shape, BF),
@@ -1013,8 +1097,8 @@
             shaped((length, width), BF),
             shaped((8, width), F32),
         )
-        + (shaped((2 * UNIT, UNIT), F32),) * 4
-        + grads * 2
+        + (shaped((2 * UNIT, UNIT), F32),) * 2
+        + grads * 3
         + (quarter,) * 5,
         scratch_shapes=[
             pltpu.VMEM((length, width), F32),
@@ -1027,7 +1111,7 @@
             pltpu.VMEM((length, 4 * UNIT), BF),
             pltpu.VMEM((2, 2, 4, 2, 2, 2 * UNIT, UNIT), BF),
             pltpu.VMEM((2, 2, 4, 2, 2, 2, UNIT, UNIT), BF),
-            pltpu.SemaphoreType.DMA((4, 4)),
+            pltpu.SemaphoreType.DMA((4, 6)),
         ]
         + semaphores(10, Gather.sems)
         + semaphores(pieces, Reduce.sems)
@@ -1039,8 +1123,8 @@
 
 def attend_back_body(
     n_ref, qa, qb, ka, kb, va, vb, cos_ref, lo_ref, hi_ref, seg_ref, pad_ref, row_ref,
-    q_ref, k_ref, v_ref, g_ref, c_ref, lse_ref, g1_ref, s0_ref, ds1_ref, gup2, gdn2, gup3, gdn3, gout,
-    gw_ref, dlow_ref, dg1_ref, sup2, sdn2, sup3, sdn3, sout,
+    q_ref, k_ref, v_ref, g_ref, c_ref, lse_ref, g1_ref, s0_ref, ds1_ref, gup1, gdn1, gup2, gdn2, gup3, gdn3, gout,
+    gw_ref, dlow_ref, dg1_ref, sup1, sdn1, sup2, sdn2, sup3, sdn3, sout,
     bias_ref, dn_ref, dq_ref, dk_ref, dv_ref, s0_buf, sem, send, recv, local, *room,
 ):
     step = pl.program_id(0)
@@ -1049,10 +1133,12 @@
     me = Place()
     traffic = Traffic()
     count = 0
-    for q, (gup, gdn, sup, sdn) in enumerate(((gup2, gdn2, sup2, sdn2), (gup3, gdn3, sup3, sdn3))):
+    for q, (gup, gdn, sup, sdn) in enumerate(
+        ((gup1, gdn1, sup1, sdn1), (gup2, gdn2, sup2, sdn2), (gup3, gdn3, sup3, sdn3))
+    ):
         ups, downs = [], []
         for e, (rows, flip) in enumerate(halves(2 * UNIT)):
-            own, *rest = room[5 * count : 5 * count + 5]
+            own, rest = room[count % 10], room[10 + 4 * count : 14 + 4 * count]
             ups.append(
                 Reduce(
                     me, gup.at[1 - me.c, :, :, :, rows, :], gup.at[me.c, :, :, :, rows, :], own, rest,
@@ -1060,7 +1146,7 @@
                 )
             )
             count += 1
-            own, *rest = room[5 * count : 5 * count + 5]
+            own, rest = room[count % 10], room[10 + 4 * count : 14 + 4 * count]
             downs.append(
                 Reduce(
                     me, gdn.at[e, :, 1 - me.c], gdn.at[e, :, me.c], own, rest,
@@ -1068,15 +1154,15 @@
                 )
             )
             count += 1
-        traffic.add(6 * q, *ups, gap=2)
-        traffic.add(6 * q + 3, *downs, gap=2)
+        traffic.add(4 * q, *ups)
+        traffic.add(4 * q + 2, *downs)
     outs = []
     for rows, flip in halves(2 * UNIT):
-        own, *rest = room[5 * count : 5 * count + 5]
+        own, rest = room[count % 10], room[10 + 4 * count : 14 + 4 * count]
         theirs, mine = gout.at[:, 1 - me.c, :, :, rows, :], gout.at[:, me.c, :, :, rows, :]
         outs.append(Reduce(me, theirs, mine, own, rest, sout.at[rows, :], flip, True))
         count += 1
-    traffic.add(11, *outs, gap=2)
+    traffic.add(12, *outs)
     traffic.bind(send, recv, local)
     fire = functools.partial(traffic.fire, step, 4, 5)
 
@@ -1153,7 +1239,7 @@
     column = pl.BlockSpec((length, 256), lambda j: (0, j))
     full = whole((length, width))
     part = whole((2 * UNIT, UNIT))
-    pieces = 10
+    pieces = 14
     return pl.pallas_call(
         attend_back_body,
         grid=(groups,),
@@ -1164,24 +1250,25 @@
         + [whole((1, length))]
         + [column] * 5
         + [pl.BlockSpec((8, length), lambda j: (j, 0)), whole((8, width))]
-        + [ANY] * 7,
+        + [ANY] * 9,
         out_specs=(
             pl.BlockSpec((3, 2, width, 128), lambda j: (0, j, 0, 0)),
             full,
             whole((8, width)),
         )
-        + (part,) * 5,
+        + (part,) * 7,
         out_shape=(
             shaped((3, width // 128, width, 128), BF),
             shaped((length, width), BF),
             shaped((8, width), F32),
         )
-        + (shaped((2 * UNIT, UNIT), F32),) * 5,
+        + (shaped((2 * UNIT, UNIT), F32),) * 7,
         scratch_shapes=[pltpu.VMEM((length, length), F32), pltpu.VMEM((length, width), F32)]
         + [pltpu.VMEM((length, 256), F32)] * 3
         + [pltpu.VMEM((length, width), F32), pltpu.SemaphoreType.DMA((2,))]
         + semaphores(pieces, Reduce.sems)
-        + ([pltpu.VMEM((4, 2, 2, UNIT, UNIT), BF)] + Reduce.room(UNIT, UNIT)) * pieces,
+        + [pltpu.VMEM((4, 2, 2, UNIT, UNIT), BF)] * 10
+        + Reduce.room(UNIT, UNIT) * pieces,
         compiler_params=params(collective_id=3, has_side_effects=True),
         name="attend_back",
     )(
@@ -1191,14 +1278,13 @@
 
 
 def skip_back_body(
-    x_ref, s_ref, d_ref, w_ref, ada_ref, dg_ref, gw_ref,
-    dx_ref, ds_ref, time_ref, sskip, sqkv, stage, send, recv, local, *room,
+    x_ref, s_ref, d_ref, w_ref, ada_ref, dg_ref, every_ref, gw_ref,
+    dx_ref, ds_ref, time_ref, gada_ref, sskip, sqkv,
+    stage, slots, part, got, summed, tim, sends, recvs, send, recv, local, *room,
 ):
-    low = d_ref[...]
     width = x_ref.shape[1]
-    per = ada_ref.shape[5] // 2
     me = Place()
-    me.greet()
+    me.greet(True)
     traffic = Traffic()
     count = 0
     pairs = []
@@ -1224,9 +1310,19 @@
     for i, made in enumerate(pairs):
         traffic.add(i if i < 3 else i + 1, *made)
     traffic.bind(send, recv, local)
+    lay = functools.partial(pl.ds, 0)
+    swaps = [
+        Swap(me, "fsdp", lambda p: dg_ref.at[p], lambda m: slots.at[me.dp, m], sends.at[0], recvs.at[0]),
+        Swap(me, "dp", lambda p: slots.at[me.dp], lambda m: slots.at[m], sends.at[1], recvs.at[1]),
+        Swap(me, "fsdp", lambda p: part.at[:, p, lay(8), :], lambda m: got.at[m], sends.at[2], recvs.at[2]),
+        Swap(me, "dp", lambda p: summed.at[p], lambda m: tim.at[m], sends.at[3], recvs.at[3]),
+    ]
+    slots[me.dp, me.fs] = dg_ref[me.fs]
+    swaps[0].start()
     traffic.at(0)
-    for i in range(4):
-        lanes = slice(i * 2 * UNIT, (i + 1) * 2 * UNIT)
+
+    def grads(i):
+        lanes = pl.ds(pl.multiple_of(i * 2 * UNIT, 2 * UNIT), 2 * UNIT)
         part = d_ref[:, lanes]
         top = dot(x_ref[...], part, TN).astype(BF)
         end = dot(s_ref[...], part, TN).astype(BF)
@@ -1234,44 +1330,78 @@
             cols = slice(c * UNIT, (c + 1) * UNIT)
             stage[i, c, 0] = top[:, cols].reshape(2, tall, UNIT)
             stage[i, c, 1] = end[:, cols].reshape(2, tall, UNIT)
-        if i < 3:
-            traffic.at(i + 1)
+
+    pl.loop(0, 1)(grads)
+    traffic.at(1)
+    swaps[0].wait()
+    swaps[1].start()
+    pl.loop(1, 2)(grads)
+    traffic.at(2)
+    pl.loop(2, 4)(grads)
+    traffic.at(3)
     traffic.at(4)
-    for i in range(4):
-        rows = slice((i % 2) * tall, (i % 2 + 1) * tall)
-        tile = jnp.concatenate([w_ref[f // 2, f % 2, i // 2, i % 2] for f in range(NB)], axis=1)
-        out = (dx_ref, ds_ref)[i // 2]
-        out[:, rows] = dot(low, tile, NT)
-        traffic.at(5 + i)
-    total = jnp.zeros((8, width), F32)
-    for f in range(NB):
-        block = ada_ref[f // 2, f % 2].reshape(width, 2 * per)
-        cols = slice(f * per, (f + 1) * per)
-        total += dot(dg_ref[0, :, cols], block[:, :per], NT) + dot(dg_ref[1, :, cols], block[:, per:], NT)
-    time_ref[...] = total
+    swaps[1].wait()
+    every = slots[...].reshape(4 * NB * 16, -1)
+    gada_ref[...] = dot(every_ref[...].reshape(4 * NB * 16, -1), every, TN)
+    part[...] = dot(every, ada_ref[...], NT).reshape(part.shape)
+    got[me.fs] = part[:, me.fs, :8, :]
+    swaps[2].start()
+
+    def back(which, out):
+        @pl.loop(0, 2)
+        def _(i):
+            rows = pl.ds(pl.multiple_of(i * tall, tall), tall)
+            tile = jnp.concatenate([w_ref[f // 2, f % 2, which, i] for f in range(NB)], axis=1)
+            out[:, rows] = dot(d_ref[...], tile, NT)
+
+    back(0, dx_ref)
+    traffic.at(5)
+    swaps[2].wait()
+    total = got[0]
+    for f in range(1, NB):
+        total = total + got[f]
+    summed[...] = total
+    tim[me.dp] = summed[me.dp]
+    swaps[3].start()
+    traffic.at(6)
+    back(1, ds_ref)
+    swaps[3].wait()
+    for d in range(4):
+        time_ref[:, d * 2 * UNIT : (d + 1) * 2 * UNIT] = tim[d]
     traffic.drain()
 
 
-def skip_back(inputs, skip_in, d_low, w_skip, ada, d_gammas, g_qkv):
+def skip_back(inputs, skip_in, d_low, w_skip, w_ada, dg_cut, every, g_qkv):
     length, width = inputs.shape
     vmem = pl.BlockSpec(memory_space=pltpu.VMEM)
+    tall, per = w_ada.shape
     pieces = 10
     return pl.pallas_call(
         skip_back_body,
-        in_specs=[vmem] * 6 + [ANY],
+        in_specs=[vmem] * 7 + [ANY],
         out_shape=(
             shaped((length, width), F32),
             shaped((length, width), F32),
             shaped((8, width), F32),
+            shaped((tall, per), F32),
             shaped((4 * UNIT, UNIT), F32),
             shaped((2 * UNIT, 3 * UNIT), F32),
         ),
-        scratch_shapes=[pltpu.VMEM(w_skip.shape, BF)]
+        scratch_shapes=[
+            pltpu.VMEM(w_skip.shape, BF),
+            pltpu.VMEM((4, NB, 16, per), BF),
+            pltpu.VMEM((4, NB, 16, tall), F32),
+            pltpu.VMEM((NB, 4, 8, tall), F32),
+            pltpu.VMEM((4, 8, tall), F32),
+            pltpu.VMEM((4, 8, tall), F32),
+            pltpu.SemaphoreType.DMA((4, NB - 1)),
+            pltpu.SemaphoreType.DMA((4, NB - 1)),
+        ]
         + semaphores(pieces, Reduce.sems)
         + ([pltpu.VMEM((4, 2, 2, UNIT, UNIT), BF)] + Reduce.room(UNIT, UNIT)) * pieces,
         compiler_params=params(collective_id=4, has_side_effects=True),
         name="skip_back",
-    )(inputs, skip_in, d_low, w_skip, ada, d_gammas, g_qkv)
+    )(inputs, skip_in, d_low, w_skip, w_ada, dg_cut, every, g_qkv)
 
 
 def rotary(positions):
@@ -1321,33 +1451,34 @@
     pad_col = pad_mask.reshape(-1, 1)
     tables = rotary(positions)
     flat_time = time_emb.reshape(slots, -1)
-    time8 = jnp.pad(flat_time, ((0, 8 - slots), (0, 0)))
+    time_cut = jnp.pad(flat_time, ((0, 16 - slots), (0, 0)))
+    time_cut = jnp.transpose(time_cut.reshape(16, 4, -1), (1, 0, 2))
     w_ada = jnp.concatenate([w_ada1, w_ada2], axis=1)
-    stream0, normed1, gamma1, gamma2, f_skip, f_ada, f_qkv = front(
-        inputs, skip_in, time8, seg_col, w_skip, w_ada, w_qkv
+    stream0, normed1, gamma1, gamma2, every, f_skip, f_qkv = front(
+        inputs, skip_in, time_cut, seg_col, w_ada, w_skip, w_qkv
     )
     f_qkv = f_qkv.reshape(NB, width, -1)
     q, k, v, ctx, lse, f_out, fup0, fdn0, fup1 = attend(
         normed1, f_qkv, tables, seg_col, pad_col, seg_row, w_out, w_up, w_down
     )
-    output, g_out, d_stream1, d_ctx, d_gamma2, sup0, sdn0, sup1, sdn1, *rest = mlp(
+    output, g_out, d_stream1, d_ctx, d_gamma2, sup0, sdn0, *rest = mlp(
         stream0, ctx, f_out, gamma2, seg_col, seg_row, cotangent, w_up, w_down, fup0, fdn0, fup1
     )
-    g_qkv, d_low, d_gamma1, sup2, sdn2, sup3, sdn3, s_out = attend_back(
+    g_qkv, d_low, d_gamma1, sup1, sdn1, sup2, sdn2, sup3, sdn3, s_out = attend_back(
         normed1, f_qkv, tables, seg_col, pad_col, seg_row, q, k, v, d_ctx, ctx, lse, gamma1,
-        stream0, d_stream1, (*rest[:4], g_out),
+        stream0, d_stream1, (*rest[:6], g_out),
     )
-    d_gammas = jnp.stack([d_gamma1, d_gamma2]).astype(BF)
-    d_input, d_skip, d_time, s_skip, s_qkv = skip_back(
-        inputs, skip_in, d_low, f_skip, f_ada, d_gammas, g_qkv.reshape(4, 2, 3, 2, 2, -1, UNIT)
+    dg_cut = jnp.concatenate([d.reshape(8, NB, -1) for d in (d_gamma1, d_gamma2)], axis=2)
+    dg_cut = jnp.pad(jnp.transpose(dg_cut, (1, 0, 2)).astype(BF), ((0, 0), (0, 8), (0, 0)))
+    d_input, d_skip, d_time, g_ada, s_skip, s_qkv = skip_back(
+        inputs, skip_in, d_low, f_skip, w_ada, dg_cut, every, g_qkv.reshape(4, 2, 3, 2, 2, -1, UNIT)
     )
-    g_ada = ada_grads(flat_time, d_gammas[:, :slots], *w_ada1.shape)
     s_up = jnp.concatenate([sup0, sup1, sup2, sup3], axis=1)
     s_down = jnp.stack([sdn0, sdn1, sdn2, sdn3]).reshape(4, 2, UNIT, UNIT)
     s_down = jnp.transpose(s_down, (1, 0, 2, 3)).reshape(w_down.shape)
     return (
         output, d_input, d_skip, d_time[:slots].reshape(time_emb.shape),
-        s_skip, g_ada[0], s_qkv, s_out, g_ada[1], s_up, s_down,
+        s_skip, g_ada[:, :UNIT], s_qkv, s_out, g_ada[:, UNIT:], s_up, s_down,
     )
 
 

time: 531 us -> 460 us (0.87)
  blocking collectives: 46.3 us -> 0 us
  Pallas kernels: 453 us -> 426 us
    all_gather x4 -> x0, blocking collectives: 46.3 us -> none  [the longest x1 14 us: ada_grads(): gammas = lax.all_gather(d_gammas, 'fsdp', axis=1, tiled=True)]
    pallas_call x1, Pallas kernels: 134 us -> 121 us  [mlp(): pl.pallas_call(mlp_body, grid=(8,), in_specs=[ANY, full, whole(w_out.shap...]
    pallas_call x2, Pallas kernels: 157 us -> 148 us  [the longest x1 74.1 us: front(): pl.pallas_call(front_body, in_specs=[vmem] * 5 + [ANY] * 2, out_specs=(vm...]
    unnamed x41 -> x39, local copies, waits for them, and re-layouts: 10.8 us -> 11.7 us
where the time goes in v4:
time: 460 us; the launch traced here: 455 us
  Pallas kernels  426 us (93%)
  local copies, waits for them, and re-layouts  22 us (5%)
  other arithmetic  5.5 us (1%)
    pallas_call x1, Pallas kernels, mlp(): pl.pallas_call(mlp_body, grid=(8,), in_specs=[ANY, full, whole(w_out.shap...  121 us
    pallas_call x1, Pallas kernels, attend_back(): pl.pallas_call(attend_back_body, grid=(groups,), in_specs=[full] + units...  95.4 us
    pallas_call x1, Pallas kernels, front(): pl.pallas_call(front_body, in_specs=[vmem] * 5 + [ANY] * 2, out_specs=(vm...  74.1 us
    pallas_call x1, Pallas kernels, skip_back(): pl.pallas_call(skip_back_body, in_specs=[vmem] * 7 + [ANY], out_shape=(sh...  73.5 us
    pallas_call x1, Pallas kernels, attend(): pl.pallas_call(attend_body, grid=(groups,), in_specs=[whole((length, widt...  61.6 us
    unnamed x39, local copies, waits for them, and re-layouts  11.7 us

profile of v4, /device:TPU:0, one launch (start us, length us, event | category | flops | bytes accessed | tf_op | source)
XLA Modules:
  0.0 454.5 jit_solution(14649582142704848246)
XLA Ops:
  0.7 0.7 convert_element_type.26
  1.4 0.7 pad.8
  2.1 0.6 copy.36
  2.7 0.9 constant_dynamic-update-slice_fusion.1
  3.5 0.9 constant_dynamic-update-slice_fusion.ada_ref
  4.4 0.0 copy-start.3
  4.4 1.7 copy.27.seg_ref
  6.1 1.7 copy.29.pad_ref
  7.9 3.2 fusion
  11.0 74.1 %front.1 = (f32[1024,1024]{1,0:T(8,128)}, bf16[1024,1024]{1,0:T(8,128)(2,1)}, f32[8,1024]{1,0:T(8,128)}, f32[8,1024]{1,0:T(8,128)}, bf16[4,8,16,256]{3,2,1,0:T(8...) custom-call(bf16[1024,1024]{1,0:T(8,128)(2,1)} %x_ref.3, ...), custom_call_target="tpu_custom_call" | custom-call | tf_op jit(solution)/shard_map/front/pallas_call | solution.py:807
  85.1 61.6 %attend.1 = (bf16[1024,1024]{1,0:T(8,128)(2,1)}, bf16[1024,1024]{1,0:T(8,128)(2,1)}, bf16[1024,1024]{1,0:T(8,128)(2,1)}, bf16[1024,1024]{1,0:T(8,128)(2,1)}, f32...) custom-call(bf16[1024,1024]{1,0:T(8,128)(2,1)} %get-tuple-element.57, ...), custom_call_target="tpu_custom_call" | custom-call | tf_op jit(solution)/shard_map/attend/pallas_call | solution.py:888
  146.7 121.4 %mlp.1 = (bf16[1024,1024]{1,0:T(8,128)(2,1)}, bf16[4,2,2,2,256,128]{5,4,3,2,1,0:T(8,128)(2,1)}, f32[1024,1024]{1,0:T(8,128)}, bf16[1024,1024]{1,0:T(8,128)(2,1)}...) custom-call(f32[1024,1024]{1,0:T(8,128)} %get-tuple-element.56.strea, ...), custom_call_target="tpu_custom_call" | custom-call | tf_op jit(solution)/shard_map/mlp/pallas_call | solution.py:1079
  268.1 95.4 %attend_back.1 = (bf16[3,8,1024,128]{3,2,1,0:T(8,128)(2,1)}, bf16[1024,1024]{1,0:T(8,128)(2,1)}, f32[8,1024]{1,0:T(8,128)}, f32[256,128]{1,0:T(8,128)}, f32[256,...) custom-call(bf16[1024,1024]{1,0:T(8,128)(2,1)} %get-tuple-element.57, ...), custom_call_target="tpu_custom_call" | custom-call | tf_op jit(solution)/shard_map/attend_back/pallas_call | solution.py:1243
  363.6 0.8 convert_bitcast_fusion
  364.3 0.6 pad.9.dg_ref
  365.0 73.5 %skip_back.1 = (f32[1024,1024]{1,0:T(8,128)}, f32[1024,1024]{1,0:T(8,128)}, f32[8,1024]{1,0:T(8,128)}, f32[256,256]{1,0:T(8,128)}, f32[512,128]{1,0:T(8,128)}, /*index=5*/f32[256,384]{1,0:T(8,128)}) custom-call(bf16[1024,1024]{1,0:T(8,128)(2,1)} %x_ref.3, bf16[1024,1024]{1,0:T(8,128)(2,1)} %s_ref.3, bf16[1024,1024]{1,0:T(8,128)(2,1)} %get-tuple-element.80.d_ref, ...), custom_call_target="tpu_custom_call" | custom-call | tf_op jit(solution)/shard_map/skip_back/pallas_call | solution.py:1379
  438.6 0.0 copy-start.2
  438.6 1.5 slice_bitcast_fusion
  440.1 1.7 fusion.7
  441.8 0.0 copy-done.13
  441.8 0.0 copy-done.14
  441.8 0.8 pad_maximum_fusion
  442.6 0.0 copy-done.7
  442.7 0.8 copy.33
  443.5 1.3 copy.44
  444.9 1.6 copy-done.1
  446.5 2.1 copy.45
  448.6 1.6 copy-done
  450.2 2.0 copy.46
  452.2 0.7 copy.47
  452.9 0.7 copy.48
  453.7 0.7 copy.49
  (29 shorter events, 0.1 us)
Async XLA Ops:
  4.4 6.6 %copy-start.3 = (bf16[256,256]{1,0:T(8,128)(2,1)}, bf16[256,256]{1,0:T(8,128)(2,1)S(1)}, u32[]{:S(2)}) copy-start(bf16[256,256]{1,0:T(8,128)(2,1)S(1)} %constant_dynamic-update-slice_fusion.ada_ref) | copy-start | bytes 393220
  268.1 95.4 %copy-start.15 = (f32[8,1024]{1,0:T(8,128)S(1)}, f32[8,1024]{1,0:T(8,128)}, u32[]{:S(2)}) copy-start(f32[8,1024]{1,0:T(8,128)} %get-tuple-element.83) | copy-start | bytes 98308
  365.0 76.8 %copy-start.8 = (f32[256,128]{1,0:T(8,128)S(1)}, f32[256,128]{1,0:T(8,128)}, u32[]{:S(2)}) copy-start(f32[256,128]{1,0:T(8,128)} %get-tuple-element.93) | copy-start | bytes 393220
  365.0 76.8 %copy-start.12 = (f32[256,128]{1,0:T(8,128)S(1)}, f32[256,128]{1,0:T(8,128)}, u32[]{:S(2)}) copy-start(f32[256,128]{1,0:T(8,128)} %get-tuple-element.94) | copy-start | bytes 393220
  365.0 76.8 %copy-start.13 = (f32[256,128]{1,0:T(8,128)S(1)}, f32[256,128]{1,0:T(8,128)}, u32[]{:S(2)}) copy-start(f32[256,128]{1,0:T(8,128)} %get-tuple-element.95) | copy-start | bytes 393220
  365.0 76.8 %copy-start.14 = (f32[256,128]{1,0:T(8,128)S(1)}, f32[256,128]{1,0:T(8,128)}, u32[]{:S(2)}) copy-start(f32[256,128]{1,0:T(8,128)} %get-tuple-element.96) | copy-start | bytes 393220
  365.0 77.7 %copy-start.7 = (f32[256,128]{1,0:T(8,128)S(1)}, f32[256,128]{1,0:T(8,128)}, u32[]{:S(2)}) copy-start(f32[256,128]{1,0:T(8,128)} %get-tuple-element.97) | copy-start | bytes 393220
  365.0 77.6 %copy-start.9 = (f32[256,128]{1,0:T(8,128)S(1)}, f32[256,128]{1,0:T(8,128)}, u32[]{:S(2)}) copy-start(f32[256,128]{1,0:T(8,128)} %get-tuple-element.98) | copy-start | bytes 393220
  365.0 77.6 %copy-start.10 = (f32[256,128]{1,0:T(8,128)S(1)}, f32[256,128]{1,0:T(8,128)}, u32[]{:S(2)}) copy-start(f32[256,128]{1,0:T(8,128)} %get-tuple-element.99) | copy-start | bytes 393220
  365.0 77.6 %copy-start.11 = (f32[256,128]{1,0:T(8,128)S(1)}, f32[256,128]{1,0:T(8,128)}, u32[]{:S(2)}) copy-start(f32[256,128]{1,0:T(8,128)} %get-tuple-element.100) | copy-start | bytes 393220
  438.6 4.9 %copy-start.2 = (bf16[1024,1024]{1,0:T(8,128)(2,1)S(1)}, bf16[1024,1024]{1,0:T(8,128)(2,1)}, u32[]{:S(2)}) copy-start(bf16[1024,1024]{1,0:T(8,128)(2,1)} %get-tuple-element.119) | copy-start | bytes 6291460
  443.5 2.9 copy-start.1
  446.5 3.7 copy-start
  450.2 2.0 copy-start.5
  450.2 2.7 copy-start.4
  450.2 3.5 copy-start.6

commit v5 on v4

--- a/solution.py
+++ b/solution.py
@@ -669,11 +669,10 @@
     def __init__(self):
         self.todo, self.pieces = {}, []
 
-    def add(self, first, *pieces, gap=2):
+    def add(self, hooks, pieces):
         self.pieces += pieces
-        hooks = first if isinstance(first, tuple) else [first + stage * gap for stage in range(5)]
-        for piece in pieces:
-            for stage, hook in enumerate(hooks):
+        for piece, places in zip(pieces, hooks, strict=True):
+            for stage, hook in enumerate(places):
                 self.todo.setdefault(hook, []).append((stage, piece))
 
     def bind(self, send, recv, local):
@@ -688,6 +687,11 @@
         for s in range(steps):
             if s * per + hook in self.todo:
                 pl.when(step == s)(functools.partial(self.at, s * per + hook))
+
+    def inside(self, index, first, count):
+        for s in range(count):
+            if first + s in self.todo:
+                pl.when(index == s)(functools.partial(self.at, first + s))
 
     def drain(self):
         for hook in sorted(self.todo):
@@ -720,13 +724,61 @@
     ]
 
 
-def row_pairs(me, shard, full, count):
+def row_pieces(me, shard, full, count):
     tall = shard.shape[0] // count
-    made = [
+    return [
         Gather(me, shard.at[pl.ds(i * tall, tall), :], full, pl.ds(i * tall, tall), i % 2 == 1)
         for i in range(count)
     ]
-    return [made[i : i + 2] for i in range(0, count, 2)]
+
+
+FRONT_HOOKS = (
+    (1, 4, 7, 13, 14), (1, 4, 7, 13, 14),
+    (4, 7, 10, 18, 19), (4, 7, 10, 18, 19),
+    (0, 1, 3, 7, 8), (0, 1, 3, 7, 8),
+    (3, 6, 9, 16, 18), (3, 6, 9, 16, 18),
+    (9, 13, 18, 25, 28), (9, 13, 18, 25, 28),
+    (6, 9, 15, 22, 25), (6, 9, 15, 22, 25),
+    (0, 2, 5, 11, 13), (0, 2, 5, 10, 12),
+    (13, 17, 21, 28, 31), (13, 17, 21, 28, 31),
+)
+FRONT_READY = 19
+ATTEND_HOOKS = (
+    (7, 10, 12, 15, 16), (7, 10, 12, 15, 16),
+    (1, 4, 6, 9, 10), (1, 4, 6, 9, 10),
+    (0, 1, 3, 5, 6), (0, 1, 3, 5, 6),
+    (6, 9, 11, 14, 15), (6, 9, 11, 14, 15),
+    (2, 5, 7, 10, 11), (2, 5, 7, 10, 11),
+)
+MLP_HOOKS = (
+    (0, 1, 4, 7, 9), (0, 1, 4, 7, 9),
+    (0, 1, 5, 9, 10), (0, 2, 5, 9, 10),
+    (11, 14, 18, 22, 24), (11, 16, 18, 22, 24),
+    (10, 13, 17, 21, 22), (10, 13, 17, 21, 22),
+    (9, 10, 14, 17, 20), (9, 11, 14, 17, 21),
+    (8, 9, 13, 16, 17), (8, 9, 13, 16, 18),
+)
+ATTEND_BACK_HOOKS = (
+    (0, 1, 4, 8, 10), (0, 1, 4, 8, 10),
+    (1, 2, 8, 11, 14), (1, 2, 8, 11, 14),
+    (7, 8, 13, 16, 19), (7, 8, 13, 16, 19),
+    (2, 3, 9, 12, 16), (2, 3, 9, 12, 16),
+    (3, 4, 10, 13, 17), (3, 4, 10, 13, 17),
+    (11, 12, 16, 18, 20), (11, 12, 16, 18, 20),
+    (12, 13, 17, 19, 20), (12, 13, 17, 19, 20),
+)
+SKIP_BACK_HOOKS = (
+    (5, 6, 11, 13, 16), (5, 6, 9, 12, 13),
+    (7, 9, 13, 16, 19), (7, 9, 12, 14, 16),
+    (2, 4, 7, 10, 12), (2, 4, 6, 9, 10),
+    (5, 6, 11, 13, 16), (6, 7, 11, 13, 16),
+    (0, 2, 5, 6, 8), (0, 2, 5, 7, 9),
+    (2, 4, 7, 10, 12), (4, 5, 7, 10, 12),
+    (11, 12, 16, 19, 20), (11, 12, 14, 17, 19),
+    (12, 13, 18, 20, 22), (12, 13, 17, 19, 21),
+    (13, 15, 19, 20, 23), (13, 15, 19, 20, 23),
+    (7, 9, 13, 16, 19), (9, 10, 13, 16, 19),
+)
 
 
 def front_body(
@@ -739,11 +791,8 @@
     me = Place()
     me.greet(True)
     traffic = Traffic()
-    plan = row_pairs(me, skip_ref, fskip_ref, 8)
-    need = len(plan) + 8
-    plan += row_pairs(me, qkv_ref, fqkv_ref, 8)
-    for i, pair in enumerate(plan):
-        traffic.add(i, *pair)
+    plan = row_pieces(me, skip_ref, fskip_ref, 8) + row_pieces(me, qkv_ref, fqkv_ref, 8)
+    traffic.add(FRONT_HOOKS, plan)
     traffic.bind(send, recv, local)
     lay = functools.partial(pl.ds, 0)
     swaps = [
@@ -754,22 +803,22 @@
     ]
     slots[me.dp, me.fs] = time_ref[me.dp]
     swaps[0].start()
-    traffic.at(0)
-    swaps[0].wait()
-    swaps[1].start()
-    traffic.at(1)
-    swaps[1].wait()
-    made = dot(slots[...].reshape(4 * NB * 16, -1), ada_ref[...])
-    part[...] = made.reshape(part.shape)
-    got[me.dp] = part[me.dp, :, :8, :]
-    swaps[2].start()
-    traffic.at(2)
-    swaps[2].wait()
-    summed[...] = got[0] + got[1] + got[2] + got[3]
-    gam[me.fs] = summed[me.fs]
-    swaps[3].start()
-    for hook in range(3, need):
+    for hook in range(FRONT_READY + 1):
         traffic.at(hook)
+        if hook == 4:
+            swaps[0].wait()
+            swaps[1].start()
+        elif hook == 8:
+            swaps[1].wait()
+            made = dot(slots[...].reshape(4 * NB * 16, -1), ada_ref[...])
+            part[...] = made.reshape(part.shape)
+            got[me.dp] = part[me.dp, :, :8, :]
+            swaps[2].start()
+        elif hook == 12:
+            swaps[2].wait()
+            summed[...] = got[0] + got[1] + got[2] + got[3]
+            gam[me.fs] = summed[me.fs]
+            swaps[3].start()
     load = flow(fskip_ref, w_ref, w_sem)
     load.start()
     swaps[3].wait()
@@ -788,14 +837,16 @@
         gain = token_gain(seg_ref[rows, :], g1_ref)
         normed_ref[rows, :] = norm(stream_ref[rows, :], gain)
 
-    pl.loop(0, 2)(stream)
-    traffic.at(need)
-    pl.loop(2, 4)(stream)
-    traffic.at(need + 1)
-    half = length // UNIT // 2
-    pl.loop(0, half)(normalise)
-    traffic.at(need + 2)
-    pl.loop(half, 2 * half)(normalise)
+    @pl.loop(0, 4)
+    def _(i):
+        stream(i)
+        traffic.inside(i, FRONT_READY + 1, 4)
+
+    @pl.loop(0, length // UNIT)
+    def _(t):
+        normalise(t)
+        traffic.inside(t, FRONT_READY + 5, 8)
+
     traffic.drain()
 
 
@@ -834,20 +885,21 @@
 
 def attend_body(
     n_ref, qa, qb, ka, kb, va, vb, cos_ref, lo_ref, hi_ref, seg_ref, pad_ref, row_ref, out_ref, up_ref, down_ref,
-    q_ref, k_ref, v_ref, c_ref, lse_ref, fout_ref, fup0_ref, fdn0_ref, fup1_ref,
+    q_ref, k_ref, v_ref, c_ref, lse_ref, fout_ref, fup0_ref, fdn0_ref, fup1_ref, fdn1_ref,
     bias_ref, send, recv, local,
 ):
     step = pl.program_id(0)
     last = pl.num_programs(0) - 1
     me = Place()
     traffic = Traffic()
-    pairs = row_pairs(me, out_ref, fout_ref, 2) + [
-        up_pair(me, up_ref, fup0_ref, 0),
-        down_pair(me, down_ref, fdn0_ref, 0),
-        up_pair(me, up_ref, fup1_ref, 1),
-    ]
-    for i, pair in enumerate(pairs):
-        traffic.add(2 * i, *pair, gap=3)
+    pieces = (
+        up_pair(me, up_ref, fup0_ref, 0)
+        + down_pair(me, down_ref, fdn0_ref, 0)
+        + up_pair(me, up_ref, fup1_ref, 1)
+        + down_pair(me, down_ref, fdn1_ref, 1)
+        + row_pieces(me, out_ref, fout_ref, 2)
+    )
+    traffic.add(ATTEND_HOOKS, pieces)
     traffic.bind(send, recv, local)
     fire = functools.partial(traffic.fire, step, 4, 4)
 
@@ -894,10 +946,10 @@
         + [whole((length, 1))] * 2
         + [whole((1, length))]
         + [ANY] * 3,
-        out_specs=(column,) * 4 + (pl.BlockSpec((8, length), lambda j: (j, 0)),) + (ANY,) * 4,
+        out_specs=(column,) * 4 + (pl.BlockSpec((8, length), lambda j: (j, 0)),) + (ANY,) * 5,
         out_shape=(wide,) * 4
-        + (shaped((8 * groups, length), F32), full_of(*w_out.shape), quarter, quarter, quarter),
-        scratch_shapes=[pltpu.VMEM((length, length), F32)] + semaphores(8, Gather.sems),
+        + (shaped((8 * groups, length), F32), full_of(*w_out.shape)) + (quarter,) * 4,
+        scratch_shapes=[pltpu.VMEM((length, length), F32)] + semaphores(10, Gather.sems),
         compiler_params=params(collective_id=1, has_side_effects=True),
         name="attend",
     )(normed, *([w_qkv] * 6), *tables, seg_col, pad_col, seg_row, w_out, w_up, w_down)
@@ -905,9 +957,9 @@
 
 def mlp_body(
     stream0_ref, ctx_ref, wout_ref, g2_ref, seg_ref, row_ref, cot_ref,
-    up_ref, down_ref, fup0, fdn0, fup1,
+    up_ref, down_ref, fup0, fdn0, fup1, fdn1,
     out_ref, gout_ref, ds1_ref, dctx_ref, dg2_ref, sup0, sdn0, gup1, gdn1, gup2, gdn2, gup3, gdn3,
-    fdn1, fup2, fdn2, fup3, fdn3,
+    fup2, fdn2, fup3, fdn3,
     s1_ref, n2_ref, acc_ref, dn_ref, up_tile, dn_tile, act_ref, pre_ref, stage_up, stage_dn,
     sem, gsend, grecv, glocal, rsend, rrecv, rlocal, *room,
 ):
@@ -917,11 +969,13 @@
     tiles = length // UNIT
     me = Place()
     gather, reduce = Traffic(), Traffic()
-    gather.add((0, 1, 3, 5, 6), *down_pair(me, down_ref, fdn1, 1))
-    gather.add(2, *up_pair(me, up_ref, fup2, 2))
-    gather.add(4, *down_pair(me, down_ref, fdn2, 2))
-    gather.add(7, *up_pair(me, up_ref, fup3, 3))
-    gather.add(10, *down_pair(me, down_ref, fdn3, 3))
+    pieces = (
+        up_pair(me, up_ref, fup2, 2)
+        + down_pair(me, down_ref, fdn2, 2)
+        + up_pair(me, up_ref, fup3, 3)
+        + down_pair(me, down_ref, fdn3, 3)
+    )
+    gather.add(MLP_HOOKS[:8], pieces)
     gather.bind(gsend, grecv, glocal)
     count = 0
     for q, (sup, sdn) in enumerate(((sup0, sdn0),)):
@@ -937,8 +991,7 @@
             rows = pl.ds(e * UNIT, UNIT)
             made.append(Reduce(me, theirs, mine, mine, room[4 * count : 4 * count + 4], sdn.at[rows, :], e == 1, False))
             count += 1
-        reduce.add(6, *made[2:])
-        reduce.add(7, *made[:2])
+        reduce.add(MLP_HOOKS[8:], made)
     reduce.bind(rsend, rrecv, rlocal)
     ups, downs = (fup0, fup1, fup2, fup3), (fdn0, fdn1, fdn2, fdn3)
     saves = {2: (gup1, gdn1), 4: (gup2, gdn2), 6: (gup3, gdn3)}
@@ -959,8 +1012,8 @@
         )
 
     def hook(which):
-        gather.fire(step, steps, 3, which)
-        reduce.fire(step, steps, 3, which)
+        gather.fire(step, steps, 4, which)
+        reduce.fire(step, steps, 4, which)
 
     @pl.when(step == 0)
     def _():
@@ -1003,22 +1056,20 @@
     down = jnp.concatenate([dn_tile[slot, f // 2, f % 2].reshape(4 * UNIT, UNIT) for f in range(NB)], axis=1)
     hidden = dot(n2_ref[...], up)
     square = hidden * hidden
-    tanh = jnp.tanh(ROOT * hidden * (1.0 + CUBE * square))
-    active = (0.5 * hidden * (1.0 + tanh)).astype(BF)
-    act_ref[...] = active
-    slope = 0.5 * (1.0 + tanh) + 0.5 * hidden * (1.0 - tanh * tanh) * (
-        ROOT * (1.0 + 3.0 * CUBE * square)
-    )
-    d_pre = (dot(cot_ref[...], down, NT) * slope).astype(BF)
-    pre_ref[...] = d_pre
-    acc_ref[...] += dot(active, down)
-    dn_ref[...] += dot(d_pre, up, NT)
+    half = 0.5 + 0.5 * jnp.tanh(hidden * (ROOT + ROOT * CUBE * square))
+    act_ref[...] = (hidden * half).astype(BF)
+    bend = hidden * (2.0 * ROOT + 6.0 * ROOT * CUBE * square)
+    slope = half + half * (1.0 - half) * bend
+    pre_ref[...] = (dot(cot_ref[...], down, NT) * slope).astype(BF)
     hook(1)
+    acc_ref[...] += dot(act_ref[...], down)
+    dn_ref[...] += dot(pre_ref[...], up, NT)
+    hook(2)
     par = (step // 2) % 2
     grad = dot(act_ref[...], cot_ref[...], TN).astype(BF)
     for f in range(NB):
         stage_dn[par, slot, f // 2, f % 2] = grad[:, f * UNIT : (f + 1) * UNIT].reshape(2, 2, UNIT, UNIT)
-    hook(2)
+    hook(3)
     grad = dot(n2_ref[...], pre_ref[...], TN).astype(BF)
     for z in range(4):
         stage_up[par, slot, z] = grad[:, z * UNIT : (z + 1) * UNIT].reshape(2, 2, 2 * UNIT, UNIT)
@@ -1069,7 +1120,7 @@
         keep.wait()
 
 
-def mlp(stream0, ctx, w_out, gamma2, seg_col, seg_row, cotangent, s_up, s_down, fup0, fdn0, fup1):
+def mlp(stream0, ctx, w_out, gamma2, seg_col, seg_row, cotangent, s_up, s_down, fup0, fdn0, fup1, fdn1):
     length, width = ctx.shape
     full = whole((length, width))
     part = pl.BlockSpec((2 * UNIT, UNIT), lambda j: (0, 0))
@@ -1088,8 +1139,8 @@
             whole((1, length)),
             full,
         ]
-        + [ANY] * 5,
-        out_specs=(full, whole(w_out.shape), ANY, full, whole((8, width))) + (part,) * 2 + (ANY,) * 11,
+        + [ANY] * 6,
+        out_specs=(full, whole(w_out.shape), ANY, full, whole((8, width))) + (part,) * 2 + (ANY,) * 10,
         out_shape=(
             shaped((length, width), BF),
             shaped(w_out.shape, BF),
@@ -1099,7 +1150,7 @@
         )
         + (shaped((2 * UNIT, UNIT), F32),) * 2
         + grads * 3
-        + (quarter,) * 5,
+        + (quarter,) * 4,
         scratch_shapes=[
             pltpu.VMEM((length, width), F32),
             pltpu.VMEM((length, width), BF),
@@ -1113,12 +1164,12 @@
             pltpu.VMEM((2, 2, 4, 2, 2, 2, UNIT, UNIT), BF),
             pltpu.SemaphoreType.DMA((4, 6)),
         ]
-        + semaphores(10, Gather.sems)
+        + semaphores(8, Gather.sems)
         + semaphores(pieces, Reduce.sems)
         + Reduce.room(UNIT, UNIT) * pieces,
         compiler_params=params(collective_id=2, has_side_effects=True),
         name="mlp",
-    )(stream0, ctx, w_out, gamma2, seg_col, seg_row, cotangent, s_up, s_down, fup0, fdn0, fup1)
+    )(stream0, ctx, w_out, gamma2, seg_col, seg_row, cotangent, s_up, s_down, fup0, fdn0, fup1, fdn1)
 
 
 def attend_back_body(
@@ -1132,37 +1183,24 @@
     length, width = n_ref.shape
     me = Place()
     traffic = Traffic()
-    count = 0
+    made = []
+
+    def add(theirs, mine, out, e, own):
+        count = len(made)
+        rest = room[10 + 4 * count : 14 + 4 * count]
+        made.append(Reduce(me, theirs, mine, room[own + e], rest, out, e == 1, True))
+
     for q, (gup, gdn, sup, sdn) in enumerate(
         ((gup1, gdn1, sup1, sdn1), (gup2, gdn2, sup2, sdn2), (gup3, gdn3, sup3, sdn3))
     ):
-        ups, downs = [], []
-        for e, (rows, flip) in enumerate(halves(2 * UNIT)):
-            own, rest = room[count % 10], room[10 + 4 * count : 14 + 4 * count]
-            ups.append(
-                Reduce(
-                    me, gup.at[1 - me.c, :, :, :, rows, :], gup.at[me.c, :, :, :, rows, :], own, rest,
-                    sup.at[rows, :], flip, True,
-                )
-            )
-            count += 1
-            own, rest = room[count % 10], room[10 + 4 * count : 14 + 4 * count]
-            downs.append(
-                Reduce(
-                    me, gdn.at[e, :, 1 - me.c], gdn.at[e, :, me.c], own, rest,
-                    sdn.at[pl.ds(e * UNIT, UNIT), :], flip, True,
-                )
-            )
-            count += 1
-        traffic.add(4 * q, *ups)
-        traffic.add(4 * q + 2, *downs)
-    outs = []
-    for rows, flip in halves(2 * UNIT):
-        own, rest = room[count % 10], room[10 + 4 * count : 14 + 4 * count]
+        for e, (rows, _) in enumerate(halves(2 * UNIT)):
+            add(gup.at[1 - me.c, :, :, :, rows, :], gup.at[me.c, :, :, :, rows, :], sup.at[rows, :], e, (0, 4, 8)[q])
+        for e in range(2):
+            add(gdn.at[e, :, 1 - me.c], gdn.at[e, :, me.c], sdn.at[pl.ds(e * UNIT, UNIT), :], e, (2, 6, 0)[q])
+    for e, (rows, _) in enumerate(halves(2 * UNIT)):
         theirs, mine = gout.at[:, 1 - me.c, :, :, rows, :], gout.at[:, me.c, :, :, rows, :]
-        outs.append(Reduce(me, theirs, mine, own, rest, sout.at[rows, :], flip, True))
-        count += 1
-    traffic.add(12, *outs)
+        add(theirs, mine, sout.at[rows, :], e, 2)
+    traffic.add(ATTEND_BACK_HOOKS, made)
     traffic.bind(send, recv, local)
     fire = functools.partial(traffic.fire, step, 4, 5)
 
@@ -1286,29 +1324,23 @@
     me = Place()
     me.greet(True)
     traffic = Traffic()
-    count = 0
-    pairs = []
+    made = []
+    tall = 512
+
+    def add(theirs, mine, out):
+        own, *rest = room[5 * len(made) : 5 * len(made) + 5]
+        made.append(Reduce(me, theirs, mine, own, rest, out, len(made) % 2 == 1, True))
+
     for sub in range(3):
-        made = []
-        for rows, flip in halves(2 * UNIT):
-            own, *rest = room[5 * count : 5 * count + 5]
+        for i in range(4):
+            rows = pl.ds(i * UNIT // 2, UNIT // 2)
             theirs, mine = gw_ref.at[:, 1 - me.c, sub, :, :, rows, :], gw_ref.at[:, me.c, sub, :, :, rows, :]
-            out = sqkv.at[rows, pl.ds(sub * UNIT, UNIT)]
-            made.append(Reduce(me, theirs, mine, own, rest, out, flip, True))
-            count += 1
-        pairs.append(made)
-    tall = 512
-    for i in range(2):
-        made = []
-        for e in range(2):
-            rows = pl.ds((2 * i + e) * UNIT, UNIT)
-            own, *rest = room[5 * count : 5 * count + 5]
-            theirs, mine = stage.at[:, 1 - me.c, :, :, rows, :], stage.at[:, me.c, :, :, rows, :]
-            made.append(Reduce(me, theirs, mine, own, rest, sskip.at[rows, :], e == 1, True))
-            count += 1
-        pairs.append(made)
-    for i, made in enumerate(pairs):
-        traffic.add(i if i < 3 else i + 1, *made)
+            add(theirs, mine, sqkv.at[rows, pl.ds(sub * UNIT, UNIT)])
+    for i in range(8):
+        rows = pl.ds(i * UNIT // 2, UNIT // 2)
+        theirs, mine = stage.at[:, 1 - me.c, :, :, rows, :], stage.at[:, me.c, :, :, rows, :]
+        add(theirs, mine, sskip.at[rows, :])
+    traffic.add(SKIP_BACK_HOOKS, made)
     traffic.bind(send, recv, local)
     lay = functools.partial(pl.ds, 0)
     swaps = [
@@ -1331,15 +1363,17 @@
             stage[i, c, 0] = top[:, cols].reshape(2, tall, UNIT)
             stage[i, c, 1] = end[:, cols].reshape(2, tall, UNIT)
 
-    pl.loop(0, 1)(grads)
-    traffic.at(1)
-    swaps[0].wait()
-    swaps[1].start()
-    pl.loop(1, 2)(grads)
-    traffic.at(2)
-    pl.loop(2, 4)(grads)
-    traffic.at(3)
-    traffic.at(4)
+    def second():
+        swaps[0].wait()
+        swaps[1].start()
+
+    @pl.loop(0, 4)
+    def _(i):
+        grads(i)
+        traffic.inside(i, 1, 4)
+        pl.when(i == 1)(second)
+
+    traffic.at(5)
     swaps[1].wait()
     every = slots[...].reshape(4 * NB * 16, -1)
     gada_ref[...] = dot(every_ref[...].reshape(4 * NB * 16, -1), every, TN)
@@ -1347,15 +1381,15 @@
     got[me.fs] = part[:, me.fs, :8, :]
     swaps[2].start()
 
-    def back(which, out):
+    def back(which, out, first):
         @pl.loop(0, 2)
         def _(i):
+            traffic.inside(i, first, 2)
             rows = pl.ds(pl.multiple_of(i * tall, tall), tall)
             tile = jnp.concatenate([w_ref[f // 2, f % 2, which, i] for f in range(NB)], axis=1)
             out[:, rows] = dot(d_ref[...], tile, NT)
 
-    back(0, dx_ref)
-    traffic.at(5)
+    back(0, dx_ref, 6)
     swaps[2].wait()
     total = got[0]
     for f in range(1, NB):
@@ -1363,8 +1397,7 @@
     summed[...] = total
     tim[me.dp] = summed[me.dp]
     swaps[3].start()
-    traffic.at(6)
-    back(1, ds_ref)
+    back(1, ds_ref, 8)
     swaps[3].wait()
     for d in range(4):
         time_ref[:, d * 2 * UNIT : (d + 1) * 2 * UNIT] = tim[d]
@@ -1375,7 +1408,7 @@
     length, width = inputs.shape
     vmem = pl.BlockSpec(memory_space=pltpu.VMEM)
     tall, per = w_ada.shape
-    pieces = 10
+    pieces = 20
     return pl.pallas_call(
         skip_back_body,
         in_specs=[vmem] * 7 + [ANY],
@@ -1398,7 +1431,7 @@
             pltpu.SemaphoreType.DMA((4, NB - 1)),
         ]
         + semaphores(pieces, Reduce.sems)
-        + ([pltpu.VMEM((4, 2, 2, UNIT, UNIT), BF)] + Reduce.room(UNIT, UNIT)) * pieces,
+        + ([pltpu.VMEM((4, 2, 2, UNIT // 2, UNIT), BF)] + Reduce.room(UNIT // 2, UNIT)) * pieces,
         compiler_params=params(collective_id=4, has_side_effects=True),
         name="skip_back",
     )(inputs, skip_in, d_low, w_skip, w_ada, dg_cut, every, g_qkv)
@@ -1458,11 +1491,11 @@
         inputs, skip_in, time_cut, seg_col, w_ada, w_skip, w_qkv
     )
     f_qkv = f_qkv.reshape(NB, width, -1)
-    q, k, v, ctx, lse, f_out, fup0, fdn0, fup1 = attend(
+    q, k, v, ctx, lse, f_out, fup0, fdn0, fup1, fdn1 = attend(
         normed1, f_qkv, tables, seg_col, pad_col, seg_row, w_out, w_up, w_down
     )
     output, g_out, d_stream1, d_ctx, d_gamma2, sup0, sdn0, *rest = mlp(
-        stream0, ctx, f_out, gamma2, seg_col, seg_row, cotangent, w_up, w_down, fup0, fdn0, fup1
+        stream0, ctx, f_out, gamma2, seg_col, seg_row, cotangent, w_up, w_down, fup0, fdn0, fup1, fdn1
     )
     g_qkv, d_low, d_gamma1, sup1, sdn1, sup2, sdn2, sup3, sdn3, s_out = attend_back(
         normed1, f_qkv, tables, seg_col, pad_col, seg_row, q, k, v, d_ctx, ctx, lse, gamma1,

time: 460 us -> 432 us (0.939)
  Pallas kernels: 426 us -> 399 us
    pallas_call x1, Pallas kernels: 121 us -> 106 us  [mlp(): pl.pallas_call(mlp_body, grid=(8,), in_specs=[ANY, full, whole(w_out.shap...]
    pallas_call x1, Pallas kernels: 95.4 us -> 88.6 us  [attend_back(): pl.pallas_call(attend_back_body, grid=(groups,), in_specs=[full] + units...]
    pallas_call x1, Pallas kernels: 74.1 us -> 68.6 us  [front(): pl.pallas_call(front_body, in_specs=[vmem] * 5 + [ANY] * 2, out_specs=(vm...]
where the time goes in v5:
time: 432 us; the launch traced here: 428 us
  Pallas kernels  399 us (92%)
  local copies, waits for them, and re-layouts  22 us (5%)
  other arithmetic  5.5 us (1%)
    pallas_call x1, Pallas kernels, mlp(): pl.pallas_call(mlp_body, grid=(8,), in_specs=[ANY, full, whole(w_out.shap...  106 us
    pallas_call x1, Pallas kernels, attend_back(): pl.pallas_call(attend_back_body, grid=(groups,), in_specs=[full] + units...  88.6 us
    pallas_call x1, Pallas kernels, skip_back(): pl.pallas_call(skip_back_body, in_specs=[vmem] * 7 + [ANY], out_shape=(sh...  71.7 us
    pallas_call x1, Pallas kernels, front(): pl.pallas_call(front_body, in_specs=[vmem] * 5 + [ANY] * 2, out_specs=(vm...  68.6 us
    pallas_call x1, Pallas kernels, attend(): pl.pallas_call(attend_body, grid=(groups,), in_specs=[whole((length, widt...  64.9 us
    unnamed x39, local copies, waits for them, and re-layouts  11.7 us

profile of v5, /device:TPU:0, one launch (start us, length us, event | category | flops | bytes accessed | tf_op | source)
XLA Modules:
  0.0 428.0 jit_solution(10251590850255869482)
XLA Ops:
  0.7 0.7 convert_element_type.26
  1.4 0.7 pad.8
  2.1 0.6 copy.36
  2.7 0.9 constant_dynamic-update-slice_fusion.1
  3.5 0.9 constant_dynamic-update-slice_fusion.ada_ref
  4.4 0.0 copy-start.3
  4.4 1.7 copy.27.seg_ref
  6.1 1.7 copy.29.pad_ref
  7.9 3.2 fusion
  11.0 68.6 %front.1 = (f32[1024,1024]{1,0:T(8,128)}, bf16[1024,1024]{1,0:T(8,128)(2,1)}, f32[8,1024]{1,0:T(8,128)}, f32[8,1024]{1,0:T(8,128)}, bf16[4,8,16,256]{3,2,1,0:T(8...) custom-call(bf16[1024,1024]{1,0:T(8,128)(2,1)} %x_ref.3, ...), custom_call_target="tpu_custom_call" | custom-call | tf_op jit(solution)/shard_map/front/pallas_call | solution.py:858
  79.7 64.9 %attend.1 = (bf16[1024,1024]{1,0:T(8,128)(2,1)}, bf16[1024,1024]{1,0:T(8,128)(2,1)}, bf16[1024,1024]{1,0:T(8,128)(2,1)}, bf16[1024,1024]{1,0:T(8,128)(2,1)}, f32...) custom-call(bf16[1024,1024]{1,0:T(8,128)(2,1)} %get-tuple-element.58, ...), custom_call_target="tpu_custom_call" | custom-call | tf_op jit(solution)/shard_map/attend/pallas_call | solution.py:940
  144.5 105.6 %mlp.1 = (bf16[1024,1024]{1,0:T(8,128)(2,1)}, bf16[4,2,2,2,256,128]{5,4,3,2,1,0:T(8,128)(2,1)}, f32[1024,1024]{1,0:T(8,128)}, bf16[1024,1024]{1,0:T(8,128)(2,1)}...) custom-call(f32[1024,1024]{1,0:T(8,128)} %get-tuple-element.57.strea, ...), custom_call_target="tpu_custom_call" | custom-call | tf_op jit(solution)/shard_map/mlp/pallas_call | solution.py:1130
  250.2 88.6 %attend_back.1 = (bf16[3,8,1024,128]{3,2,1,0:T(8,128)(2,1)}, bf16[1024,1024]{1,0:T(8,128)(2,1)}, f32[8,1024]{1,0:T(8,128)}, f32[256,128]{1,0:T(8,128)}, f32[256,...) custom-call(bf16[1024,1024]{1,0:T(8,128)(2,1)} %get-tuple-element.58, ...), custom_call_target="tpu_custom_call" | custom-call | tf_op jit(solution)/shard_map/attend_back/pallas_call | solution.py:1281
  338.9 0.0 copy-done.15
  338.9 0.8 convert_bitcast_fusion
  339.6 0.6 pad.9.dg_ref
  340.3 71.7 %skip_back.1 = (f32[1024,1024]{1,0:T(8,128)}, f32[1024,1024]{1,0:T(8,128)}, f32[8,1024]{1,0:T(8,128)}, f32[256,256]{1,0:T(8,128)}, f32[512,128]{1,0:T(8,128)}, /*index=5*/f32[256,384]{1,0:T(8,128)}) custom-call(bf16[1024,1024]{1,0:T(8,128)(2,1)} %x_ref.3, bf16[1024,1024]{1,0:T(8,128)(2,1)} %s_ref.3, bf16[1024,1024]{1,0:T(8,128)(2,1)} %get-tuple-element.82.d_ref, ...), custom_call_target="tpu_custom_call" | custom-call | tf_op jit(solution)/shard_map/skip_back/pallas_call | solution.py:1412
  412.0 0.0 copy-start.2
  412.0 1.5 slice_bitcast_fusion
  413.5 1.7 fusion.7
  415.2 0.0 copy-done.13
  415.2 0.0 copy-done.14
  415.2 0.8 pad_maximum_fusion
  416.1 0.8 copy.33
  417.0 1.3 copy.44
  418.3 1.6 copy-done.1
  419.9 2.1 copy.45
  422.0 1.6 copy-done
  423.6 2.0 copy.46
  425.6 0.7 copy.47
  426.3 0.7 copy.48
  427.1 0.7 copy.49
  (29 shorter events, 0.1 us)
Async XLA Ops:
  4.4 6.6 %copy-start.3 = (bf16[256,256]{1,0:T(8,128)(2,1)}, bf16[256,256]{1,0:T(8,128)(2,1)S(1)}, u32[]{:S(2)}) copy-start(bf16[256,256]{1,0:T(8,128)(2,1)S(1)} %constant_dynamic-update-slice_fusion.ada_ref) | copy-start | bytes 393220
  250.2 88.7 %copy-start.15 = (f32[8,1024]{1,0:T(8,128)S(1)}, f32[8,1024]{1,0:T(8,128)}, u32[]{:S(2)}) copy-start(f32[8,1024]{1,0:T(8,128)} %get-tuple-element.85) | copy-start | bytes 98308
  340.3 74.9 %copy-start.8 = (f32[256,128]{1,0:T(8,128)S(1)}, f32[256,128]{1,0:T(8,128)}, u32[]{:S(2)}) copy-start(f32[256,128]{1,0:T(8,128)} %get-tuple-element.95) | copy-start | bytes 393220
  340.3 74.9 %copy-start.12 = (f32[256,128]{1,0:T(8,128)S(1)}, f32[256,128]{1,0:T(8,128)}, u32[]{:S(2)}) copy-start(f32[256,128]{1,0:T(8,128)} %get-tuple-element.96) | copy-start | bytes 393220
  340.3 74.9 %copy-start.13 = (f32[256,128]{1,0:T(8,128)S(1)}, f32[256,128]{1,0:T(8,128)}, u32[]{:S(2)}) copy-start(f32[256,128]{1,0:T(8,128)} %get-tuple-element.97) | copy-start | bytes 393220
  340.3 74.9 %copy-start.14 = (f32[256,128]{1,0:T(8,128)S(1)}, f32[256,128]{1,0:T(8,128)}, u32[]{:S(2)}) copy-start(f32[256,128]{1,0:T(8,128)} %get-tuple-element.98) | copy-start | bytes 393220
  340.3 75.8 %copy-start.7 = (f32[256,128]{1,0:T(8,128)S(1)}, f32[256,128]{1,0:T(8,128)}, u32[]{:S(2)}) copy-start(f32[256,128]{1,0:T(8,128)} %get-tuple-element.99) | copy-start | bytes 393220
  340.3 75.8 %copy-start.9 = (f32[256,128]{1,0:T(8,128)S(1)}, f32[256,128]{1,0:T(8,128)}, u32[]{:S(2)}) copy-start(f32[256,128]{1,0:T(8,128)} %get-tuple-element.100) | copy-start | bytes 393220
  340.3 75.8 %copy-start.10 = (f32[256,128]{1,0:T(8,128)S(1)}, f32[256,128]{1,0:T(8,128)}, u32[]{:S(2)}) copy-start(f32[256,128]{1,0:T(8,128)} %get-tuple-element.101) | copy-start | bytes 393220
  340.3 75.8 %copy-start.11 = (f32[256,128]{1,0:T(8,128)S(1)}, f32[256,128]{1,0:T(8,128)}, u32[]{:S(2)}) copy-start(f32[256,128]{1,0:T(8,128)} %get-tuple-element.102) | copy-start | bytes 393220
  412.0 4.9 %copy-start.2 = (bf16[1024,1024]{1,0:T(8,128)(2,1)S(1)}, bf16[1024,1024]{1,0:T(8,128)(2,1)}, u32[]{:S(2)}) copy-start(bf16[1024,1024]{1,0:T(8,128)(2,1)} %get-tuple-element.121) | copy-start | bytes 6291460
  417.0 2.9 copy-start.1
  419.9 3.7 copy-start
  423.6 2.0 copy-start.5
  423.6 2.7 copy-start.4
  423.6 3.5 copy-start.6

commit v6 on v5

--- a/solution.py
+++ b/solution.py
@@ -751,12 +751,12 @@
     (2, 5, 7, 10, 11), (2, 5, 7, 10, 11),
 )
 MLP_HOOKS = (
-    (0, 1, 4, 7, 9), (0, 1, 4, 7, 9),
-    (0, 1, 5, 9, 10), (0, 2, 5, 9, 10),
-    (11, 14, 18, 22, 24), (11, 16, 18, 22, 24),
-    (10, 13, 17, 21, 22), (10, 13, 17, 21, 22),
-    (9, 10, 14, 17, 20), (9, 11, 14, 17, 21),
-    (8, 9, 13, 16, 17), (8, 9, 13, 16, 18),
+    (0, 2, 5, 12, 13), (0, 2, 5, 12, 13),
+    (0, 2, 5, 12, 13), (0, 2, 5, 12, 13),
+    (14, 17, 20, 23, 24), (14, 17, 20, 23, 24),
+    (12, 15, 17, 21, 23), (12, 15, 17, 21, 23),
+    (8, 10, 16, 18, 23), (8, 10, 16, 18, 23),
+    (8, 10, 16, 18, 23), (8, 10, 16, 18, 23),
 )
 ATTEND_BACK_HOOKS = (
     (0, 1, 4, 8, 10), (0, 1, 4, 8, 10),
@@ -768,22 +768,22 @@
     (12, 13, 17, 19, 20), (12, 13, 17, 19, 20),
 )
 SKIP_BACK_HOOKS = (
-    (5, 6, 11, 13, 16), (5, 6, 9, 12, 13),
-    (7, 9, 13, 16, 19), (7, 9, 12, 14, 16),
-    (2, 4, 7, 10, 12), (2, 4, 6, 9, 10),
-    (5, 6, 11, 13, 16), (6, 7, 11, 13, 16),
-    (0, 2, 5, 6, 8), (0, 2, 5, 7, 9),
-    (2, 4, 7, 10, 12), (4, 5, 7, 10, 12),
-    (11, 12, 16, 19, 20), (11, 12, 14, 17, 19),
-    (12, 13, 18, 20, 22), (12, 13, 17, 19, 21),
-    (13, 15, 19, 20, 23), (13, 15, 19, 20, 23),
-    (7, 9, 13, 16, 19), (9, 10, 13, 16, 19),
+    (5, 6, 8, 10, 11), (5, 6, 8, 10, 11),
+    (4, 5, 7, 8, 9), (4, 5, 7, 8, 9),
+    (6, 7, 9, 11, 13), (6, 7, 9, 11, 13),
+    (0, 2, 4, 6, 7), (0, 2, 4, 6, 7),
+    (2, 4, 6, 7, 8), (2, 4, 6, 7, 8),
+    (8, 9, 11, 13, 14), (8, 9, 11, 13, 14),
+    (11, 12, 14, 15, 18), (11, 12, 14, 15, 18),
+    (7, 8, 10, 12, 14), (7, 8, 10, 12, 14),
+    (8, 9, 12, 14, 15), (8, 9, 12, 14, 15),
+    (10, 11, 14, 15, 18), (10, 11, 14, 15, 18),
 )
 
 
 def front_body(
-    x_ref, s_ref, time_ref, seg_ref, ada_ref, skip_ref, qkv_ref,
-    stream_ref, normed_ref, g1_ref, g2_ref, slots, fskip_ref, fqkv_ref,
+    x_ref, s_ref, time_ref, row_ref, freq_ref, ada_ref, skip_ref, qkv_ref,
+    stream_ref, normed_ref, g1_ref, g2_ref, slots, seg_ref, pad_ref, cos_ref, lo_ref, hi_ref, fskip_ref, fqkv_ref,
     w_ref, part, got, summed, gam, w_sem, sends, recvs, send, recv, local,
 ):
     length, width = x_ref.shape
@@ -801,11 +801,26 @@
         Swap(me, "dp", lambda p: part.at[p, :, lay(8), :], lambda m: got.at[m], sends.at[2], recvs.at[2]),
         Swap(me, "fsdp", lambda p: summed.at[p], lambda m: gam.at[m], sends.at[3], recvs.at[3]),
     ]
+
+    def prepare(t):
+        rows = pl.ds(pl.multiple_of(t * UNIT, UNIT), UNIT)
+        turned = row_ref[:, rows].T
+        seg_ref[rows, :] = turned[:, 0:1]
+        pad_ref[rows, :] = turned[:, 1:2]
+        phase = turned[:, 2:3].astype(F32) * freq_ref[0:1, :]
+        cosine, sine = jnp.cos(phase), jnp.sin(phase)
+        early = lax.broadcasted_iota(jnp.int32, phase.shape, 1) % HD < HD // 2
+        cos_ref[rows, :] = cosine
+        lo_ref[rows, :] = jnp.where(early, -sine, 0.0)
+        hi_ref[rows, :] = jnp.where(early, 0.0, sine)
+
     slots[me.dp, me.fs] = time_ref[me.dp]
     swaps[0].start()
     for hook in range(FRONT_READY + 1):
         traffic.at(hook)
-        if hook == 4:
+        if hook == 2:
+            pl.loop(0, length // UNIT)(prepare)
+        elif hook == 4:
             swaps[0].wait()
             swaps[1].start()
         elif hook == 8:
@@ -850,21 +865,26 @@
     traffic.drain()
 
 
-def front(inputs, skip_in, time_cut, seg_col, w_ada, w_skip, w_qkv):
+def front(inputs, skip_in, time_cut, rows, freq, w_ada, w_skip, w_qkv):
     length, width = inputs.shape
     fulls = [full_of(*w.shape) for w in (w_skip, w_qkv)]
     vmem = pl.BlockSpec(memory_space=pltpu.VMEM)
     per = w_ada.shape[1]
     return pl.pallas_call(
         front_body,
-        in_specs=[vmem] * 5 + [ANY] * 2,
-        out_specs=(vmem,) * 5 + (ANY,) * 2,
+        in_specs=[vmem] * 6 + [ANY] * 2,
+        out_specs=(vmem,) * 10 + (ANY,) * 2,
         out_shape=(
             shaped((length, width), F32),
             shaped((length, width), BF),
             shaped((8, width), F32),
             shaped((8, width), F32),
             shaped((4, NB, 16, w_ada.shape[0]), BF),
+            shaped((length, 1), jnp.int32),
+            shaped((length, 1), jnp.int32),
+            shaped((length, UNIT), F32),
+            shaped((length, UNIT), F32),
+            shaped((length, UNIT), F32),
             *fulls,
         ),
         scratch_shapes=[
@@ -880,7 +900,7 @@
         + semaphores(16, Gather.sems),
         compiler_params=params(collective_id=0, has_side_effects=True),
         name="front",
-    )(inputs, skip_in, time_cut, seg_col, w_ada, w_skip, w_qkv)
+    )(inputs, skip_in, time_cut, rows, freq, w_ada, w_skip, w_qkv)
 
 
 def attend_body(
@@ -958,9 +978,9 @@
 def mlp_body(
     stream0_ref, ctx_ref, wout_ref, g2_ref, seg_ref, row_ref, cot_ref,
     up_ref, down_ref, fup0, fdn0, fup1, fdn1,
-    out_ref, gout_ref, ds1_ref, dctx_ref, dg2_ref, sup0, sdn0, gup1, gdn1, gup2, gdn2, gup3, gdn3,
+    acts_ref, keep1_ref, gout_ref, ds1_ref, dctx_ref, dg2_ref, sup0, sdn0, gup1, gdn1, gup2, gdn2, gup3, gdn3,
     fup2, fdn2, fup3, fdn3,
-    s1_ref, n2_ref, acc_ref, dn_ref, up_tile, dn_tile, act_ref, pre_ref, stage_up, stage_dn,
+    s1_ref, n2_ref, dn_ref, up_tile, dn_tile, act_ref, pre_ref, stage_up, stage_dn,
     sem, gsend, grecv, glocal, rsend, rrecv, rlocal, *room,
 ):
     step = pl.program_id(0)
@@ -1011,6 +1031,9 @@
             flow(stage_dn.at[q % 2, e], gdn.at[e], sem.at[3, s - 2]),
         )
 
+    def act_save(s):
+        return flow(act_ref.at[s % 2], acts_ref.at[s], sem.at[1, 2 + s % 2])
+
     def hook(which):
         gather.fire(step, steps, 4, which)
         reduce.fire(step, steps, 4, which)
@@ -1034,8 +1057,8 @@
             rows = pl.ds(pl.multiple_of(t * UNIT, UNIT), UNIT)
             n2_ref[rows, :] = norm(s1_ref[rows, :], token_gain(seg_ref[rows, :], g2_ref))
 
-        acc_ref[...] = jnp.zeros_like(acc_ref)
         dn_ref[...] = jnp.zeros_like(dn_ref)
+        flow(s1_ref, keep1_ref, sem.at[0, 2]).start()
 
     hook(0)
     for s in range(steps):
@@ -1050,6 +1073,8 @@
             if s % 2 == 0:
                 for load in tile_loads(s + 1):
                     load.start()
+            if s >= 2:
+                act_save(s - 2).wait()
 
     slot = step % 2
     up = jnp.concatenate([up_tile[slot, z].reshape(width, UNIT) for z in range(4)], axis=1)
@@ -1057,16 +1082,21 @@
     hidden = dot(n2_ref[...], up)
     square = hidden * hidden
     half = 0.5 + 0.5 * jnp.tanh(hidden * (ROOT + ROOT * CUBE * square))
-    act_ref[...] = (hidden * half).astype(BF)
+    act_ref[slot] = (hidden * half).astype(BF)
     bend = hidden * (2.0 * ROOT + 6.0 * ROOT * CUBE * square)
     slope = half + half * (1.0 - half) * bend
     pre_ref[...] = (dot(cot_ref[...], down, NT) * slope).astype(BF)
+    for s in range(steps):
+
+        @pl.when(step == s)
+        def _(s=s):
+            act_save(s).start()
+
     hook(1)
-    acc_ref[...] += dot(act_ref[...], down)
     dn_ref[...] += dot(pre_ref[...], up, NT)
     hook(2)
     par = (step // 2) % 2
-    grad = dot(act_ref[...], cot_ref[...], TN).astype(BF)
+    grad = dot(act_ref[slot], cot_ref[...], TN).astype(BF)
     for f in range(NB):
         stage_dn[par, slot, f // 2, f % 2] = grad[:, f * UNIT : (f + 1) * UNIT].reshape(2, 2, UNIT, UNIT)
     hook(3)
@@ -1086,12 +1116,12 @@
     @pl.when(step == steps - 1)
     def _():
         dg2_ref[...] = jnp.zeros_like(dg2_ref)
+        flow(s1_ref, keep1_ref, sem.at[0, 2]).wait()
 
         @pl.loop(0, tiles)
         def _(t):
             rows = pl.ds(pl.multiple_of(t * UNIT, UNIT), UNIT)
             stream = s1_ref[rows, :]
-            out_ref[rows, :] = (stream + acc_ref[rows, :]).astype(BF)
             gain = token_gain(seg_ref[rows, :], g2_ref)
             term, d_gain = norm_back(dn_ref[rows, :], stream, gain)
             d_stream = cot_ref[rows, :].astype(F32) + term
@@ -1110,14 +1140,16 @@
             lanes = slice(i * 2 * UNIT, (i + 1) * 2 * UNIT)
             tile = jnp.concatenate([wout_ref[i, c].reshape(width, UNIT) for c in range(2)], axis=1)
             part = dot(n2_ref[:, lanes], tile, NT)
-            acc_ref[...] = part if i == 0 else acc_ref[...] + part
-        dctx_ref[...] = acc_ref[...].astype(BF)
+            dn_ref[...] = part if i == 0 else dn_ref[...] + part
+        dctx_ref[...] = dn_ref[...].astype(BF)
         gather.drain()
         reduce.drain()
         for s in range(4, steps):
             for save in grad_saves(s):
                 save.wait()
         keep.wait()
+        for s in (steps - 2, steps - 1):
+            act_save(s).wait()
 
 
 def mlp(stream0, ctx, w_out, gamma2, seg_col, seg_row, cotangent, s_up, s_down, fup0, fdn0, fup1, fdn1):
@@ -1140,9 +1172,10 @@
             full,
         ]
         + [ANY] * 6,
-        out_specs=(full, whole(w_out.shape), ANY, full, whole((8, width))) + (part,) * 2 + (ANY,) * 10,
+        out_specs=(ANY, ANY, whole(w_out.shape), ANY, full, whole((8, width))) + (part,) * 2 + (ANY,) * 10,
         out_shape=(
-            shaped((length, width), BF),
+            shaped((8, length, 4 * UNIT), BF),
+            shaped((length, width), F32),
             shaped(w_out.shape, BF),
             shaped((length, width), F32),
             shaped((length, width), BF),
@@ -1155,10 +1188,9 @@
             pltpu.VMEM((length, width), F32),
             pltpu.VMEM((length, width), BF),
             pltpu.VMEM((length, width), F32),
-            pltpu.VMEM((length, width), F32),
             pltpu.VMEM((2, 4, 2, 2, 2 * UNIT, UNIT), BF),
             pltpu.VMEM((2, 4, 2, 2, 2, UNIT, UNIT), BF),
-            pltpu.VMEM((length, 4 * UNIT), BF),
+            pltpu.VMEM((2, length, 4 * UNIT), BF),
             pltpu.VMEM((length, 4 * UNIT), BF),
             pltpu.VMEM((2, 2, 4, 2, 2, 2 * UNIT, UNIT), BF),
             pltpu.VMEM((2, 2, 4, 2, 2, 2, UNIT, UNIT), BF),
@@ -1316,9 +1348,9 @@
 
 
 def skip_back_body(
-    x_ref, s_ref, d_ref, w_ref, ada_ref, dg_ref, every_ref, gw_ref,
-    dx_ref, ds_ref, time_ref, gada_ref, sskip, sqkv,
-    stage, slots, part, got, summed, tim, sends, recvs, send, recv, local, *room,
+    x_ref, s_ref, d_ref, w_ref, ada_ref, dg_ref, every_ref, gw_ref, acts_ref, keep1_ref, fdn0, fdn1, fdn2, fdn3,
+    out_ref, dx_ref, ds_ref, time_ref, gada_ref, sskip, sqkv,
+    stage, acc_ref, act_tile, dn_tile, sem, slots, part, got, summed, tim, sends, recvs, send, recv, local, *room,
 ):
     width = x_ref.shape[1]
     me = Place()
@@ -1349,9 +1381,30 @@
         Swap(me, "fsdp", lambda p: part.at[:, p, lay(8), :], lambda m: got.at[m], sends.at[2], recvs.at[2]),
         Swap(me, "dp", lambda p: summed.at[p], lambda m: tim.at[m], sends.at[3], recvs.at[3]),
     ]
+    downs = (fdn0, fdn1, fdn2, fdn3)
+
+    def tiles(s):
+        return (
+            flow(acts_ref.at[s], act_tile.at[s % 2], sem.at[0, s % 2]),
+            flow(downs[s // 2].at[:, :, :, :, pl.ds(s % 2 * UNIT, UNIT), :], dn_tile.at[s % 2], sem.at[1, s % 2]),
+        )
+
+    start1 = flow(keep1_ref, acc_ref, sem.at[0, 2])
     slots[me.dp, me.fs] = dg_ref[me.fs]
     swaps[0].start()
     traffic.at(0)
+    start1.start()
+    for load in tiles(0):
+        load.start()
+
+    def add_down(slot):
+        @pl.loop(0, 2)
+        def _(half):
+            tile = jnp.concatenate(
+                [dn_tile[slot, 2 * half + i // 2, i % 2].reshape(4 * UNIT, UNIT) for i in range(4)], axis=1
+            )
+            lanes = pl.ds(pl.multiple_of(half * 4 * UNIT, 4 * UNIT), 4 * UNIT)
+            acc_ref[:, lanes] += dot(act_tile[slot], tile)
 
     def grads(i):
         lanes = pl.ds(pl.multiple_of(i * 2 * UNIT, 2 * UNIT), 2 * UNIT)
@@ -1401,18 +1454,29 @@
     swaps[3].wait()
     for d in range(4):
         time_ref[:, d * 2 * UNIT : (d + 1) * 2 * UNIT] = tim[d]
+    start1.wait()
+    for s in range(8):
+        if s < 7:
+            for load in tiles(s + 1):
+                load.start()
+        for load in tiles(s):
+            load.wait()
+        add_down(s % 2)
+        traffic.at(10 + s)
+    out_ref[...] = acc_ref[...].astype(BF)
     traffic.drain()
 
 
-def skip_back(inputs, skip_in, d_low, w_skip, w_ada, dg_cut, every, g_qkv):
+def skip_back(inputs, skip_in, d_low, w_skip, w_ada, dg_cut, every, g_qkv, acts, stream1, fdowns):
     length, width = inputs.shape
     vmem = pl.BlockSpec(memory_space=pltpu.VMEM)
     tall, per = w_ada.shape
     pieces = 20
     return pl.pallas_call(
         skip_back_body,
-        in_specs=[vmem] * 7 + [ANY],
+        in_specs=[vmem] * 7 + [ANY] * 7,
         out_shape=(
+            shaped((length, width), BF),
             shaped((length, width), F32),
             shaped((length, width), F32),
             shaped((8, width), F32),
@@ -1422,6 +1486,10 @@
         ),
         scratch_shapes=[
             pltpu.VMEM(w_skip.shape, BF),
+            pltpu.VMEM((length, width), F32),
+            pltpu.VMEM((2, *acts.shape[1:]), BF),
+            pltpu.VMEM((2, 4, 2, 2, 2, UNIT, UNIT), BF),
+            pltpu.SemaphoreType.DMA((2, 3)),
             pltpu.VMEM((4, NB, 16, per), BF),
             pltpu.VMEM((4, NB, 16, tall), F32),
             pltpu.VMEM((NB, 4, 8, tall), F32),
@@ -1434,14 +1502,18 @@
         + ([pltpu.VMEM((4, 2, 2, UNIT // 2, UNIT), BF)] + Reduce.room(UNIT // 2, UNIT)) * pieces,
         compiler_params=params(collective_id=4, has_side_effects=True),
         name="skip_back",
-    )(inputs, skip_in, d_low, w_skip, w_ada, dg_cut, every, g_qkv)
+    )(inputs, skip_in, d_low, w_skip, w_ada, dg_cut, every, g_qkv, acts, stream1, *fdowns)
+
+
+def frequencies():
+    lane = jnp.arange(128) % (HD // 2)
+    return 10000.0 ** (-2.0 * lane.astype(F32) / HD)
 
 
 def rotary(positions):
     half = HD // 2
     lane = jnp.arange(128)
-    frequency = 10000.0 ** (-2.0 * (lane % half).astype(F32) / HD)
-    phase = positions.reshape(-1, 1).astype(F32) * frequency[None, :]
+    phase = positions.reshape(-1, 1).astype(F32) * frequencies()[None, :]
     cosine, sine = jnp.cos(phase), jnp.sin(phase)
     early = (lane % HD < half)[None, :]
     return cosine, jnp.where(early, -sine, 0.0), jnp.where(early, 0.0, sine)
@@ -1480,21 +1552,22 @@
 ):
     slots = time_emb.shape[1]
     length, width = inputs.shape
-    seg_col, seg_row = seg_ids.reshape(-1, 1), seg_ids.reshape(1, -1)
-    pad_col = pad_mask.reshape(-1, 1)
-    tables = rotary(positions)
+    seg_row = seg_ids.reshape(1, -1)
+    rows = jnp.concatenate([seg_row, pad_mask.reshape(1, -1), positions.reshape(1, -1)])
+    rows = jnp.pad(rows, ((0, 5), (0, 0)))
+    freq = jnp.broadcast_to(frequencies(), (8, UNIT))
     flat_time = time_emb.reshape(slots, -1)
     time_cut = jnp.pad(flat_time, ((0, 16 - slots), (0, 0)))
     time_cut = jnp.transpose(time_cut.reshape(16, 4, -1), (1, 0, 2))
     w_ada = jnp.concatenate([w_ada1, w_ada2], axis=1)
-    stream0, normed1, gamma1, gamma2, every, f_skip, f_qkv = front(
-        inputs, skip_in, time_cut, seg_col, w_ada, w_skip, w_qkv
+    stream0, normed1, gamma1, gamma2, every, seg_col, pad_col, *tables, f_skip, f_qkv = front(
+        inputs, skip_in, time_cut, rows, freq, w_ada, w_skip, w_qkv
     )
     f_qkv = f_qkv.reshape(NB, width, -1)
     q, k, v, ctx, lse, f_out, fup0, fdn0, fup1, fdn1 = attend(
         normed1, f_qkv, tables, seg_col, pad_col, seg_row, w_out, w_up, w_down
     )
-    output, g_out, d_stream1, d_ctx, d_gamma2, sup0, sdn0, *rest = mlp(
+    acts, stream1, g_out, d_stream1, d_ctx, d_gamma2, sup0, sdn0, *rest = mlp(
         stream0, ctx, f_out, gamma2, seg_col, seg_row, cotangent, w_up, w_down, fup0, fdn0, fup1, fdn1
     )
     g_qkv, d_low, d_gamma1, sup1, sdn1, sup2, sdn2, sup3, sdn3, s_out = attend_back(
@@ -1503,8 +1576,9 @@
     )
     dg_cut = jnp.concatenate([d.reshape(8, NB, -1) for d in (d_gamma1, d_gamma2)], axis=2)
     dg_cut = jnp.pad(jnp.transpose(dg_cut, (1, 0, 2)).astype(BF), ((0, 0), (0, 8), (0, 0)))
-    d_input, d_skip, d_time, g_ada, s_skip, s_qkv = skip_back(
-        inputs, skip_in, d_low, f_skip, w_ada, dg_cut, every, g_qkv.reshape(4, 2, 3, 2, 2, -1, UNIT)
+    output, d_input, d_skip, d_time, g_ada, s_skip, s_qkv = skip_back(
+        inputs, skip_in, d_low, f_skip, w_ada, dg_cut, every, g_qkv.reshape(4, 2, 3, 2, 2, -1, UNIT),
+        acts, stream1, (fdn0, fdn1, rest[7], rest[9]),
     )
     s_up = jnp.concatenate([sup0, sup1, sup2, sup3], axis=1)
     s_down = jnp.stack([sdn0, sdn1, sdn2, sdn3]).reshape(4, 2, UNIT, UNIT)

time: 432 us -> 426 us (0.986)
  no operation moved by 1% of the time
where the time goes in v6:
time: 426 us; the launch traced here: 422 us
  Pallas kernels  398 us (93%)
  local copies, waits for them, and re-layouts  20.4 us (5%)
    pallas_call x1, Pallas kernels, mlp(): pl.pallas_call(mlp_body, grid=(8,), in_specs=[ANY, full, whole(w_out.shap...  102 us
    pallas_call x1, Pallas kernels, attend_back(): pl.pallas_call(attend_back_body, grid=(groups,), in_specs=[full] + units...  87.8 us
    pallas_call x1, Pallas kernels, skip_back(): pl.pallas_call(skip_back_body, in_specs=[vmem] * 7 + [ANY] * 7, out_shape...  72.5 us
    pallas_call x1, Pallas kernels, front(): pl.pallas_call(front_body, in_specs=[vmem] * 6 + [ANY] * 2, out_specs=(vm...  71.5 us
    pallas_call x1, Pallas kernels, attend(): pl.pallas_call(attend_body, grid=(groups,), in_specs=[whole((length, widt...  64.7 us
    unnamed x39, local copies, waits for them, and re-layouts  12.3 us

profile of v6, /device:TPU:0, one launch (start us, length us, event | category | flops | bytes accessed | tf_op | source)
XLA Modules:
  0.0 422.2 jit_solution(1132553541458843358)
XLA Ops:
  0.7 0.6 broadcast_in_dim.3.freq_ref
  1.3 0.7 pad_add_fusion
  2.0 0.6 pad.13.row_ref
  2.6 0.7 pad.12
  3.3 0.6 copy.30
  3.9 0.9 constant_dynamic-update-slice_fusion.1
  4.8 0.9 constant_dynamic-update-slice_fusion.ada_ref
  5.7 0.0 copy-start.3
  5.7 0.6 copy-done.3
  6.3 71.5 %front.1 = (f32[1024,1024]{1,0:T(8,128)}, bf16[1024,1024]{1,0:T(8,128)(2,1)}, f32[8,1024]{1,0:T(8,128)}, f32[8,1024]{1,0:T(8,128)}, bf16[4,8,16,256]{3,2,1,0:T(8...) custom-call(bf16[1024,1024]{1,0:T(8,128)(2,1)} %x_ref.3, ...), custom_call_target="tpu_custom_call" | custom-call | tf_op jit(solution)/shard_map/front/pallas_call | solution.py:873
  77.8 64.7 %attend.1 = (bf16[1024,1024]{1,0:T(8,128)(2,1)}, bf16[1024,1024]{1,0:T(8,128)(2,1)}, bf16[1024,1024]{1,0:T(8,128)(2,1)}, bf16[1024,1024]{1,0:T(8,128)(2,1)}, f32...) custom-call(bf16[1024,1024]{1,0:T(8,128)(2,1)} %get-tuple-element.66, ...), custom_call_target="tpu_custom_call" | custom-call | tf_op jit(solution)/shard_map/attend/pallas_call | solution.py:960
  142.5 101.9 %mlp.1 = (bf16[8,1024,512]{2,1,0:T(8,128)(2,1)}, f32[1024,1024]{1,0:T(8,128)}, bf16[4,2,2,2,256,128]{5,4,3,2,1,0:T(8,128)(2,1)}, f32[1024,1024]{1,0:T(8,128)}, b...) custom-call(f32[1024,1024]{1,0:T(8,128)} %get-tuple-element.76.strea, ...), custom_call_target="tpu_custom_call" | custom-call | tf_op jit(solution)/shard_map/mlp/pallas_call | solution.py:1162
  244.4 87.8 %attend_back.1 = (bf16[3,8,1024,128]{3,2,1,0:T(8,128)(2,1)}, bf16[1024,1024]{1,0:T(8,128)(2,1)}, f32[8,1024]{1,0:T(8,128)}, f32[256,128]{1,0:T(8,128)}, f32[256,...) custom-call(bf16[1024,1024]{1,0:T(8,128)(2,1)} %get-tuple-element.66, ...), custom_call_target="tpu_custom_call" | custom-call | tf_op jit(solution)/shard_map/attend_back/pallas_call | solution.py:1313
  332.2 0.0 copy-done.15
  332.2 0.8 convert_bitcast_fusion
  333.0 0.6 pad.14.dg_ref
  333.7 72.5 %skip_back.1 = (bf16[1024,1024]{1,0:T(8,128)(2,1)}, f32[1024,1024]{1,0:T(8,128)}, f32[1024,1024]{1,0:T(8,128)}, f32[8,1024]{1,0:T(8,128)}, f32[256,256]{1,0:T(8,...) custom-call(bf16[1024,1024]{1,0:T(8,128)(2,1)} %x_ref.3, bf16[1024,1024]{1,0:T(8,128)(2,1)} %s_ref.3, ...), custom_call_target="tpu_custom_call" | custom-call | tf_op jit(solution)/shard_map/skip_back/pallas_call | solution.py:1475
  406.2 1.5 slice_bitcast_fusion
  407.8 1.7 fusion.3
  409.4 0.0 copy-done.12
  409.5 0.8 pad_maximum_fusion
  410.3 0.0 copy-done.10
  410.3 0.8 copy.27
  411.2 1.3 copy.38
  412.5 1.6 copy-done.1
  414.1 2.1 copy.39
  416.3 1.6 copy-done
  417.8 2.0 copy.40
  419.8 0.7 copy.41
  420.6 0.0 copy-done.4
  420.6 0.7 copy.42
  421.3 0.7 copy.43
  (27 shorter events, 0.1 us)
Async XLA Ops:
  5.7 0.7 copy-start.3
  244.4 87.8 %copy-start.15 = (f32[8,1024]{1,0:T(8,128)S(1)}, f32[8,1024]{1,0:T(8,128)}, u32[]{:S(2)}) copy-start(f32[8,1024]{1,0:T(8,128)} %get-tuple-element.98) | copy-start | bytes 98308
  333.6 75.8 %copy-start.8 = (f32[256,128]{1,0:T(8,128)S(1)}, f32[256,128]{1,0:T(8,128)}, u32[]{:S(2)}) copy-start(f32[256,128]{1,0:T(8,128)} %get-tuple-element.113) | copy-start | bytes 393220
  333.6 75.8 %copy-start.12 = (f32[256,128]{1,0:T(8,128)S(1)}, f32[256,128]{1,0:T(8,128)}, u32[]{:S(2)}) copy-start(f32[256,128]{1,0:T(8,128)} %get-tuple-element.114) | copy-start | bytes 393220
  333.6 75.8 %copy-start.13 = (f32[256,128]{1,0:T(8,128)S(1)}, f32[256,128]{1,0:T(8,128)}, u32[]{:S(2)}) copy-start(f32[256,128]{1,0:T(8,128)} %get-tuple-element.115) | copy-start | bytes 393220
  333.6 75.8 %copy-start.14 = (f32[256,128]{1,0:T(8,128)S(1)}, f32[256,128]{1,0:T(8,128)}, u32[]{:S(2)}) copy-start(f32[256,128]{1,0:T(8,128)} %get-tuple-element.116) | copy-start | bytes 393220
  333.7 76.6 %copy-start.7 = (f32[256,128]{1,0:T(8,128)S(1)}, f32[256,128]{1,0:T(8,128)}, u32[]{:S(2)}) copy-start(f32[256,128]{1,0:T(8,128)} %get-tuple-element.117) | copy-start | bytes 393220
  333.7 76.6 %copy-start.9 = (f32[256,128]{1,0:T(8,128)S(1)}, f32[256,128]{1,0:T(8,128)}, u32[]{:S(2)}) copy-start(f32[256,128]{1,0:T(8,128)} %get-tuple-element.118) | copy-start | bytes 393220
  333.7 76.6 %copy-start.10 = (f32[256,128]{1,0:T(8,128)S(1)}, f32[256,128]{1,0:T(8,128)}, u32[]{:S(2)}) copy-start(f32[256,128]{1,0:T(8,128)} %get-tuple-element.119) | copy-start | bytes 393220
  333.7 76.6 %copy-start.11 = (f32[256,128]{1,0:T(8,128)S(1)}, f32[256,128]{1,0:T(8,128)}, u32[]{:S(2)}) copy-start(f32[256,128]{1,0:T(8,128)} %get-tuple-element.120) | copy-start | bytes 393220
  406.2 4.9 %copy-start.2 = (bf16[1024,1024]{1,0:T(8,128)(2,1)S(1)}, bf16[1024,1024]{1,0:T(8,128)(2,1)}, u32[]{:S(2)}) copy-start(bf16[1024,1024]{1,0:T(8,128)(2,1)} %get-tuple-element.136) | copy-start | bytes 6291460
  411.2 2.9 copy-start.1
  414.1 3.7 copy-start
  417.8 2.0 copy-start.5
  417.8 2.7 copy-start.4
  417.8 3.5 copy-start.6

commit v7 on v6

--- a/solution.py
+++ b/solution.py
@@ -782,11 +782,14 @@
 
 
 def front_body(
-    x_ref, s_ref, time_ref, row_ref, freq_ref, ada_ref, skip_ref, qkv_ref,
-    stream_ref, normed_ref, g1_ref, g2_ref, slots, seg_ref, pad_ref, cos_ref, lo_ref, hi_ref, fskip_ref, fqkv_ref,
-    w_ref, part, got, summed, gam, w_sem, sends, recvs, send, recv, local,
+    x_hbm, s_hbm, time_ref, row_ref, freq_ref, ada_ref, skip_ref, qkv_ref,
+    stream_hbm, normed_ref, g1_ref, g2_ref, slots, seg_ref, pad_ref, cos_ref, lo_ref, hi_ref, fskip_ref, fqkv_ref,
+    x_ref, s_ref, stream_ref, near_sem, w_ref, part, got, summed, gam, w_sem, sends, recvs, send, recv, local,
 ):
     length, width = x_ref.shape
+    ahead = [flow(x_hbm, x_ref, near_sem.at[0]), flow(s_hbm, s_ref, near_sem.at[1])]
+    for load in ahead:
+        load.start()
     per = ada_ref.shape[1] // 2
     me = Place()
     me.greet(True)
@@ -841,6 +844,8 @@
         g1_ref[:, f * per : (f + 1) * per] = gam[f, :, :per]
         g2_ref[:, f * per : (f + 1) * per] = gam[f, :, per:]
     load.wait()
+    for load in ahead:
+        load.wait()
 
     def stream(i):
         tile = jnp.concatenate([w_ref[i, c].reshape(2 * width, UNIT) for c in range(2)], axis=1)
@@ -857,12 +862,16 @@
         stream(i)
         traffic.inside(i, FRONT_READY + 1, 4)
 
+    away = flow(stream_ref, stream_hbm, near_sem.at[2])
+    away.start()
+
     @pl.loop(0, length // UNIT)
     def _(t):
         normalise(t)
         traffic.inside(t, FRONT_READY + 5, 8)
 
     traffic.drain()
+    away.wait()
 
 
 def front(inputs, skip_in, time_cut, rows, freq, w_ada, w_skip, w_qkv):
@@ -872,8 +881,8 @@
     per = w_ada.shape[1]
     return pl.pallas_call(
         front_body,
-        in_specs=[vmem] * 6 + [ANY] * 2,
-        out_specs=(vmem,) * 10 + (ANY,) * 2,
+        in_specs=[ANY] * 2 + [vmem] * 4 + [ANY] * 2,
+        out_specs=(ANY,) + (vmem,) * 9 + (ANY,) * 2,
         out_shape=(
             shaped((length, width), F32),
             shaped((length, width), BF),
@@ -888,6 +897,10 @@
             *fulls,
         ),
         scratch_shapes=[
+            pltpu.VMEM((length, width), BF),
+            pltpu.VMEM((length, width), BF),
+            pltpu.VMEM((length, width), F32),
+            pltpu.SemaphoreType.DMA((3,)),
             pltpu.VMEM(fulls[0].shape, BF),
             pltpu.VMEM((4, NB, 16, per), F32),
             pltpu.VMEM((4, NB, 8, per), F32),
@@ -1348,11 +1361,18 @@
 
 
 def skip_back_body(
-    x_ref, s_ref, d_ref, w_ref, ada_ref, dg_ref, every_ref, gw_ref, acts_ref, keep1_ref, fdn0, fdn1, fdn2, fdn3,
-    out_ref, dx_ref, ds_ref, time_ref, gada_ref, sskip, sqkv,
-    stage, acc_ref, act_tile, dn_tile, sem, slots, part, got, summed, tim, sends, recvs, send, recv, local, *room,
+    x_hbm, s_hbm, d_ref, w_hbm, ada_ref, dg_ref, every_ref, gw_ref, acts_ref, keep1_ref, fdn0, fdn1, fdn2, fdn3,
+    out_ref, dx_hbm, ds_hbm, time_ref, gada_ref, sskip, sqkv,
+    x_ref, s_ref, w_ref, dx_ref, ds_ref, near_sem, stage, acc_ref, act_tile, dn_tile, sem, slots, part, got, summed, tim, sends, recvs, send, recv, local, *room,
 ):
     width = x_ref.shape[1]
+    ahead = [
+        flow(x_hbm, x_ref, near_sem.at[0]),
+        flow(s_hbm, s_ref, near_sem.at[1]),
+        flow(w_hbm, w_ref, near_sem.at[2]),
+    ]
+    for load in ahead:
+        load.start()
     me = Place()
     me.greet(True)
     traffic = Traffic()
@@ -1396,6 +1416,8 @@
     start1.start()
     for load in tiles(0):
         load.start()
+    ahead[0].wait()
+    ahead[1].wait()
 
     def add_down(slot):
         @pl.loop(0, 2)
@@ -1442,7 +1464,10 @@
             tile = jnp.concatenate([w_ref[f // 2, f % 2, which, i] for f in range(NB)], axis=1)
             out[:, rows] = dot(d_ref[...], tile, NT)
 
+    ahead[2].wait()
     back(0, dx_ref, 6)
+    away = [flow(dx_ref, dx_hbm, near_sem.at[3]), flow(ds_ref, ds_hbm, near_sem.at[4])]
+    away[0].start()
     swaps[2].wait()
     total = got[0]
     for f in range(1, NB):
@@ -1451,6 +1476,7 @@
     tim[me.dp] = summed[me.dp]
     swaps[3].start()
     back(1, ds_ref, 8)
+    away[1].start()
     swaps[3].wait()
     for d in range(4):
         time_ref[:, d * 2 * UNIT : (d + 1) * 2 * UNIT] = tim[d]
@@ -1465,6 +1491,8 @@
         traffic.at(10 + s)
     out_ref[...] = acc_ref[...].astype(BF)
     traffic.drain()
+    for copy in away:
+        copy.wait()
 
 
 def skip_back(inputs, skip_in, d_low, w_skip, w_ada, dg_cut, every, g_qkv, acts, stream1, fdowns):
@@ -1474,7 +1502,8 @@
     pieces = 20
     return pl.pallas_call(
         skip_back_body,
-        in_specs=[vmem] * 7 + [ANY] * 7,
+        in_specs=[ANY] * 2 + [vmem, ANY] + [vmem] * 3 + [ANY] * 7,
+        out_specs=(vmem, ANY, ANY) + (vmem,) * 4,
         out_shape=(
             shaped((length, width), BF),
             shaped((length, width), F32),
@@ -1485,6 +1514,12 @@
             shaped((2 * UNIT, 3 * UNIT), F32),
         ),
         scratch_shapes=[
+            pltpu.VMEM((length, width), BF),
+            pltpu.VMEM((length, width), BF),
+            pltpu.VMEM(w_skip.shape, BF),
+            pltpu.VMEM((length, width), F32),
+            pltpu.VMEM((length, width), F32),
+            pltpu.SemaphoreType.DMA((5,)),
             pltpu.VMEM(w_skip.shape, BF),
             pltpu.VMEM((length, width), F32),
             pltpu.VMEM((2, *acts.shape[1:]), BF),

time: 426 us -> 419 us (0.984)
  Pallas kernels: 398 us -> 391 us
    pallas_call x2, Pallas kernels: 144 us -> 137 us  [the longest x1 68.8 us: front(): pl.pallas_call(front_body, in_specs=[ANY] * 2 + [vmem] * 4 + [ANY] * 2, o...]
where the time goes in v7:
time: 419 us; the launch traced here: 415 us
  Pallas kernels  391 us (93%)
  local copies, waits for them, and re-layouts  20.4 us (5%)
    pallas_call x1, Pallas kernels, mlp(): pl.pallas_call(mlp_body, grid=(8,), in_specs=[ANY, full, whole(w_out.shap...  102 us
    pallas_call x1, Pallas kernels, attend_back(): pl.pallas_call(attend_back_body, grid=(groups,), in_specs=[full] + units...  87.7 us
    pallas_call x1, Pallas kernels, front(): pl.pallas_call(front_body, in_specs=[ANY] * 2 + [vmem] * 4 + [ANY] * 2, o...  68.8 us
    pallas_call x1, Pallas kernels, skip_back(): pl.pallas_call(skip_back_body, in_specs=[ANY] * 2 + [vmem, ANY] + [vmem]...  68 us
    pallas_call x1, Pallas kernels, attend(): pl.pallas_call(attend_body, grid=(groups,), in_specs=[whole((length, widt...  64.7 us
    unnamed x39, local copies, waits for them, and re-layouts  12.3 us

profile of v7, /device:TPU:0, one launch (start us, length us, event | category | flops | bytes accessed | tf_op | source)
XLA Modules:
  0.0 414.9 jit_solution(7799483033618351729)
XLA Ops:
  0.7 0.6 broadcast_in_dim.3.freq_ref
  1.3 0.7 pad_add_fusion
  2.0 0.6 pad.13.row_ref
  2.6 0.7 pad.12
  3.3 0.6 copy.30
  3.9 0.9 constant_dynamic-update-slice_fusion.1
  4.8 0.9 constant_dynamic-update-slice_fusion.ada_ref
  5.7 0.0 copy-start.3
  5.7 0.6 copy-done.3
  6.3 68.8 %front.1 = (f32[1024,1024]{1,0:T(8,128)}, bf16[1024,1024]{1,0:T(8,128)(2,1)}, f32[8,1024]{1,0:T(8,128)}, f32[8,1024]{1,0:T(8,128)}, bf16[4,8,16,256]{3,2,1,0:T(8...) custom-call(bf16[1024,1024]{1,0:T(8,128)(2,1)} %x_hbm.3, ...), custom_call_target="tpu_custom_call" | custom-call | tf_op jit(solution)/shard_map/front/pallas_call | solution.py:882
  75.1 64.7 %attend.1 = (bf16[1024,1024]{1,0:T(8,128)(2,1)}, bf16[1024,1024]{1,0:T(8,128)(2,1)}, bf16[1024,1024]{1,0:T(8,128)(2,1)}, bf16[1024,1024]{1,0:T(8,128)(2,1)}, f32...) custom-call(bf16[1024,1024]{1,0:T(8,128)(2,1)} %get-tuple-element.66, ...), custom_call_target="tpu_custom_call" | custom-call | tf_op jit(solution)/shard_map/attend/pallas_call | solution.py:973
  139.9 101.9 %mlp.1 = (bf16[8,1024,512]{2,1,0:T(8,128)(2,1)}, f32[1024,1024]{1,0:T(8,128)}, bf16[4,2,2,2,256,128]{5,4,3,2,1,0:T(8,128)(2,1)}, f32[1024,1024]{1,0:T(8,128)}, b...) custom-call(f32[1024,1024]{1,0:T(8,128)} %get-tuple-element.76.strea, ...), custom_call_target="tpu_custom_call" | custom-call | tf_op jit(solution)/shard_map/mlp/pallas_call | solution.py:1175
  241.8 87.7 %attend_back.1 = (bf16[3,8,1024,128]{3,2,1,0:T(8,128)(2,1)}, bf16[1024,1024]{1,0:T(8,128)(2,1)}, f32[8,1024]{1,0:T(8,128)}, f32[256,128]{1,0:T(8,128)}, f32[256,...) custom-call(bf16[1024,1024]{1,0:T(8,128)(2,1)} %get-tuple-element.66, ...), custom_call_target="tpu_custom_call" | custom-call | tf_op jit(solution)/shard_map/attend_back/pallas_call | solution.py:1326
  329.5 0.8 convert_bitcast_fusion
  330.3 0.6 pad.14.dg_ref
  331.0 68.0 %skip_back.1 = (bf16[1024,1024]{1,0:T(8,128)(2,1)}, f32[1024,1024]{1,0:T(8,128)}, f32[1024,1024]{1,0:T(8,128)}, f32[8,1024]{1,0:T(8,128)}, f32[256,256]{1,0:T(8,...) custom-call(bf16[1024,1024]{1,0:T(8,128)(2,1)} %x_hbm.3, bf16[1024,1024]{1,0:T(8,128)(2,1)} %s_hbm.3, ...), custom_call_target="tpu_custom_call" | custom-call | tf_op jit(solution)/shard_map/skip_back/pallas_call | solution.py:1503
  399.0 1.5 slice_bitcast_fusion
  400.5 1.7 fusion.3
  402.2 0.0 copy-done.8
  402.2 0.0 copy-done.13
  402.2 0.8 pad_maximum_fusion
  403.1 0.0 copy-done.11
  403.1 0.8 copy.27
  403.9 1.3 copy.38
  405.3 1.6 copy-done.1
  406.9 2.1 copy.39
  409.0 1.6 copy-done
  410.6 2.0 copy.40
  412.6 0.0 copy-done.5
  412.6 0.7 copy.41
  413.3 0.7 copy.42
  414.1 0.7 copy.43
  (27 shorter events, 0.1 us)
Async XLA Ops:
  5.7 0.7 copy-start.3
  241.8 87.8 %copy-start.15 = (f32[8,1024]{1,0:T(8,128)S(1)}, f32[8,1024]{1,0:T(8,128)}, u32[]{:S(2)}) copy-start(f32[8,1024]{1,0:T(8,128)} %get-tuple-element.98) | copy-start | bytes 98308
  330.9 71.2 %copy-start.8 = (f32[256,128]{1,0:T(8,128)S(1)}, f32[256,128]{1,0:T(8,128)}, u32[]{:S(2)}) copy-start(f32[256,128]{1,0:T(8,128)} %get-tuple-element.113) | copy-start | bytes 393220
  330.9 71.2 %copy-start.12 = (f32[256,128]{1,0:T(8,128)S(1)}, f32[256,128]{1,0:T(8,128)}, u32[]{:S(2)}) copy-start(f32[256,128]{1,0:T(8,128)} %get-tuple-element.114) | copy-start | bytes 393220
  331.0 71.2 %copy-start.13 = (f32[256,128]{1,0:T(8,128)S(1)}, f32[256,128]{1,0:T(8,128)}, u32[]{:S(2)}) copy-start(f32[256,128]{1,0:T(8,128)} %get-tuple-element.115) | copy-start | bytes 393220
  331.0 71.3 %copy-start.14 = (f32[256,128]{1,0:T(8,128)S(1)}, f32[256,128]{1,0:T(8,128)}, u32[]{:S(2)}) copy-start(f32[256,128]{1,0:T(8,128)} %get-tuple-element.116) | copy-start | bytes 393220
  331.0 72.1 %copy-start.7 = (f32[256,128]{1,0:T(8,128)S(1)}, f32[256,128]{1,0:T(8,128)}, u32[]{:S(2)}) copy-start(f32[256,128]{1,0:T(8,128)} %get-tuple-element.117) | copy-start | bytes 393220
  331.0 72.1 %copy-start.9 = (f32[256,128]{1,0:T(8,128)S(1)}, f32[256,128]{1,0:T(8,128)}, u32[]{:S(2)}) copy-start(f32[256,128]{1,0:T(8,128)} %get-tuple-element.118) | copy-start | bytes 393220
  331.0 72.1 %copy-start.10 = (f32[256,128]{1,0:T(8,128)S(1)}, f32[256,128]{1,0:T(8,128)}, u32[]{:S(2)}) copy-start(f32[256,128]{1,0:T(8,128)} %get-tuple-element.119) | copy-start | bytes 393220
  331.0 72.1 %copy-start.11 = (f32[256,128]{1,0:T(8,128)S(1)}, f32[256,128]{1,0:T(8,128)}, u32[]{:S(2)}) copy-start(f32[256,128]{1,0:T(8,128)} %get-tuple-element.120) | copy-start | bytes 393220
  399.0 4.9 %copy-start.2 = (bf16[1024,1024]{1,0:T(8,128)(2,1)S(1)}, bf16[1024,1024]{1,0:T(8,128)(2,1)}, u32[]{:S(2)}) copy-start(bf16[1024,1024]{1,0:T(8,128)(2,1)} %get-tuple-element.136) | copy-start | bytes 6291460
  403.9 2.9 copy-start.1
  406.9 3.7 copy-start
  410.6 2.0 copy-start.5
  410.6 2.7 copy-start.4
  410.6 3.5 copy-start.6
